TPU v7x, 32 devices: a whole 2x2x4 slice. The times are simulated.
32 devices in a mesh: query: 4 (over y, x), corpus: 8 (over z, core).
Axes of the slice: x: 2, y: 2, z: 4, core: 2. Of those that a mesh axis runs over, the one named last changes fastest.
Arguments:
- queries: float32 [32, 32, 128], P(('query', 'corpus')), may hold values from -6 to 6
- passages: float32 [128, 180, 128], P(('query', 'corpus')), may hold values from -0.5 to 0.5
- clusters: int32 [128, 180], P(('query', 'corpus')), may hold values from 0 to 23
- lengths: int32 [128], P(('query', 'corpus')), may hold values from 45 to 180, as said below
- feedback: int32 [32, 3], replicated, may hold values from 0 to 127, as said below
- ranks: int32 [32, 24], replicated, may hold values from 0 to 23, each once within a row
- cand_local: int32 [32, 64], P(None, ('query', 'corpus')), may hold values from 0 to 3
- cand_count: int32 [32, 32], P(None, ('query', 'corpus')), may hold values from 1 to 2, as said below
Outputs:
- scores: float32 [32, 64], P(('query', 'corpus'))
Inputs may be any that keep to these rules, and one draw needn't show every extreme that they name: `lengths`: some passages fill all 180 slots of their tile. `cand_count`: each query fills all 2 slots on at least one device. The passages of exactly 3 of the (query, feedback) pairs lie on each device. `ranks`: each row is a permutation of 0 to 23.
All inputs are finite; a program needn't handle non-finite values.
Results may differ from a plain program's by a relative error of at most 0.0003.
Values sent between devices are 32-bit elements; how exact they have to be, the bound alone decides.
No kernel may reach another device: no remote copies, remote signals or barrier semaphores. Data moves between devices by JAX's collectives and lax.ppermute only.
A program may use at most 64 MiB of HBM per device.

v0:
```python
import jax
import jax.numpy as jnp
from jax import lax
from jax.sharding import PartitionSpec as P

DIM = 128
QL = 32
PL = 180
NCENT = 24
EXP = 10
CAP = 2


beta_prf = 0.5
highest = lax.Precision.HIGHEST


def idf_weights():
    order = jnp.arange(EXP).astype(jnp.float32)
    return beta_prf * jnp.log((NCENT + 1.0) / (order + 1.0))


def expand_tokens(tokens, sums, ranking):
    scale = lax.rsqrt(jnp.mean(sums * sums, axis=-1, keepdims=True) + 1e-05)
    centroid = sums * scale
    select = (ranking[:, None, :] == jnp.arange(EXP, dtype=jnp.int32)[None, :, None]).astype(
        jnp.float32
    )
    extra = jnp.einsum("njk,nkd->njd", select, centroid, precision=highest)
    extra = extra * idf_weights()[None, :, None]
    return jnp.concatenate([tokens, extra], axis=1)


def body(queries, passages, clusters, lengths, feedback, ranks, cand_local, cand_count):
    position = lax.axis_index(("query", "corpus"))
    shard_count = passages.shape[0]
    query_count = queries.shape[0]
    token_axis = jnp.arange(PL, dtype=jnp.int32)
    alive = token_axis[None, :] < lengths[:, None]
    member = (
        (clusters[:, None, :] == jnp.arange(NCENT, dtype=jnp.int32)[None, :, None])
        & alive[:, None, :]
    ).astype(jnp.float32)
    local_sums = jnp.einsum("pkt,ptd->pkd", member, passages, precision=highest)
    flat_tiles = passages.reshape(shard_count * PL, DIM)
    flat_alive = alive.reshape(shard_count * PL)
    passage_axis = jnp.arange(shard_count, dtype=jnp.int32)
    slot_axis = jnp.arange(CAP, dtype=jnp.int32)

    def score_one(items):
        row_expanded, row_local, row_count = items
        similar = jnp.einsum("ed,md->em", row_expanded, flat_tiles, precision=highest)
        similar = jnp.where(flat_alive[None, :], similar, -1e30)
        largest = jnp.max(similar.reshape(-1, shard_count, PL), axis=2)
        per_passage = jnp.sum(largest, axis=0) / QL
        chooser = (row_local[:, None] == passage_axis[None, :]).astype(jnp.float32)
        values = jnp.dot(chooser, per_passage, precision=highest)
        return jnp.where(slot_axis < row_count[0], values, jnp.zeros_like(values))

    global_ids = position * shard_count + jnp.arange(shard_count, dtype=jnp.int32)
    requests = jnp.sum(
        (feedback[:, :, None] == global_ids[None, None, :]).astype(jnp.float32), axis=1
    )
    total_sums = lax.psum(
        jnp.dot(requests, local_sums.reshape(shard_count, NCENT * DIM), precision=highest).reshape(
            -1, NCENT, DIM
        ),
        ("query", "corpus"),
    )
    piece = lax.all_gather(queries, ("query", "corpus"), axis=0, tiled=True)
    expanded = expand_tokens(piece, total_sums, ranks)
    rows = expanded.shape[0]
    scores = lax.map(score_one, (expanded, cand_local, cand_count), batch_size=min(rows, 32))
    blocks = scores.reshape(lax.axis_size("query"), lax.axis_size("corpus"), query_count, CAP)
    moved = lax.all_to_all(
        lax.all_to_all(blocks, "query", split_axis=0, concat_axis=0, tiled=True),
        "corpus",
        split_axis=1,
        concat_axis=1,
        tiled=True,
    )
    return jnp.transpose(moved, (2, 0, 1, 3)).reshape(query_count, -1)


def solution(mesh):
    in_specs = (
        P(("query", "corpus"), None, None),
        P(("query", "corpus"), None, None),
        P(("query", "corpus"), None),
        P(("query", "corpus")),
        P(),
        P(),
        P(None, ("query", "corpus")),
        P(None, ("query", "corpus")),
    )
    out_specs = P(("query", "corpus"), None)
    return jax.shard_map(body, mesh=mesh, in_specs=in_specs, out_specs=out_specs, check_vma=False)
```

profile of v0, /device:TPU:0, one launch (start us, length us, event | category | flops | bytes accessed | tf_op | source)
XLA Modules:
  0.0 190.8 jit_solution(14468064179825250075)
XLA Ops:
  6.5 0.0 all-reduce.2.cloned.1.call-start
  6.5 0.7 iota_compare_fusion.3
  7.3 0.8 convert_reduce_fusion
  8.0 1.3 convolution_bitcast_fusion
  9.3 1.3 fusion.9
  10.6 0.0 all-reduce.2.cloned.1.call-update
  10.7 0.1 lt.52
  10.8 1.0 copy.33
  11.8 0.8 copy.32
  12.6 0.8 copy.31
  13.4 45.7 %all_gather.3 = f32[32,32,128]{2,1,0:T(8,128)S(1)} all-gather(f32[1,32,128]{2,1,0:T(8,128)} %param.8), channel_id=1, replica_groups=mesh['query'=4,'corpus'=8] {'query','corpus'}, dimensions={0}, use_global_device_ids=true | all-gather | bytes 540672 | tf_op jit(solution)/shard_map/all_gather | solution.py:70
  59.1 84.2 %all-reduce.2.cloned.1.call-done = f32[32,24,128]{2,0,1:T(8,128)} async-done(((f32[32,24,128]{2,0,1:T(8,128)}), f32[32,24,128]{2,0,1:T(8,128)}) %all-reduce.2.cloned.1.call-update) | async-done | bytes 393232 | tf_op jit(solution)/shard_map/psum | solution.py:64
  143.3 1.2 multiply_reduce_fusion
  144.5 1.2 broadcast_multiply_fusion
  145.7 0.5 convolution_multiply_fusion
  146.2 3.9 %broadcast_select_fusion = f32[32,42,720]{2,1,0:T(8,128)S(1)} fusion(pred[720]{0:T(1024)(128)(4,1)S(1)} %lt.52, f32[720,128,1]{1,0,2:T(8,128)S(1)} %reshape.73, f32[32,10,128]{2,1,0:T(8,128)S(1)} %convolution_multiply_fusion, f32[32,32,128]{2,1,0:T(8,128)S(1)} %all_gather.3), kind=kOutput, calls=%fused_computation | convolution fusion | flops 1487496192 | bytes 4928208 | tf_op jit(solution)/shard_map/while/body/eval_jaxpr/vmap(ed,md->em)/dot_general | solution.py:52
  150.1 4.4 %copy.36 = f32[32,42,720]{2,0,1:T(8,128)} copy(f32[32,42,720]{2,1,0:T(8,128)S(1)} %broadcast_select_fusion) | data formatting | bytes 7741440 | tf_op jit(solution)/shard_map/while/body/eval_jaxpr/vmap(jit(_where))/select_n | solution.py:53
  154.5 7.7 %reshape.71 = f32[32,42,4,180]{3,2,0,1:T(4,128)} reshape(f32[32,42,720]{2,0,1:T(8,128)} %copy.36) | data formatting | bytes 7741440 | tf_op jit(solution)/shard_map/while/body/eval_jaxpr/vmap()/reshape | solution.py:54
  162.2 0.0 copy-start
  162.2 4.1 %reduce_max.10 = f32[32,42,4]{2,0,1:T(8,128)S(1)} reduce(f32[32,42,4,180]{3,2,0,1:T(4,128)} %reshape.71, f32[]{:T(128)} %constant.50.clone.1), dimensions={3}, to_apply=%region_3.4 | reduce | flops 962304 | bytes 3892228 | tf_op jit(solution)/shard_map/while/body/eval_jaxpr/vmap()/reduce_max | solution.py:54
  166.3 0.1 reduce_sum.30
  166.4 0.3 fusion.7
  166.8 0.1 copy.41
  166.8 0.0 copy-done
  166.8 0.1 reshape_reshape.3
  166.9 8.1 %all_to_all.10 = f32[4,8,1,2]{1,3,2,0:T(2,128)S(1)} all-to-all(f32[4,8,1,2]{1,3,2,0:T(2,128)S(1)} %copy.37), channel_id=1, replica_groups=mesh['query'=4,'corpus'=8] {'query'}, dimensions={0} | all-to-all | bytes 512 | tf_op jit(solution)/shard_map/all_to_all | solution.py:76
  175.0 0.1 copy.38
  175.1 8.1 %all_to_all.11 = f32[4,8,1,2]{0,3,2,1:T(2,128)S(1)} all-to-all(f32[4,8,1,2]{0,3,2,1:T(2,128)S(1)} %copy.38), channel_id=1, replica_groups=mesh['query'=4,'corpus'=8] {'corpus'}, dimensions={1} | all-to-all | bytes 512 | tf_op jit(solution)/shard_map/all_to_all | solution.py:75
  183.2 0.1 copy.39
  183.4 0.6 reshape_transpose.3
  (7 shorter events, 0.1 us)
Async XLA Ops:
  6.5 136.8 %all-reduce.2.cloned.1.call-start = ((), (), s32[]{:S(2)}) async-start(), calls=%async_computation.2 | async-start | bytes 786432 | tf_op jit(solution)/shard_map/psum | solution.py:64
  162.2 4.6 %copy-start = (s32[32,1]{0,1:T(1,128)S(1)}, s32[32,1]{0,1:T(1,128)}, u32[]{:S(2)}) copy-start(s32[32,1]{0,1:T(1,128)} %param.15) | copy-start | bytes 388
Sparse Core Ops, SparseCore 0:
  12.7 130.6 all-reduce.1
where the time goes:
time: 191 us
  waiting for transfers between devices  84.2 us (44%)
  blocking collectives  61.9 us (32%)
  local copies, waits for them, and re-layouts  15.8 us (8%)
  between operations  13.5 us (7%)
  other arithmetic  8.03 us (4%)
  matrix products  7.34 us (4%)
    psum x1, waiting for transfers between devices, body(): lax.psum(jnp.dot(requests, local_sums.reshape(shard_count, NCENT * DIM),...  84.2 us
    all_gather x1, blocking collectives, body(): piece = lax.all_gather(queries, ('query', 'corpus'), axis=0, tiled=True)  45.7 us
    all_to_all x1, blocking collectives, body(): lax.all_to_all(lax.all_to_all(blocks, 'query', split_axis=0, concat_axis=...  8.13 us
    all_to_all x1, blocking collectives, body(): lax.all_to_all(blocks, 'query', split_axis=0, concat_axis=0, tiled=True)  8.08 us
    reshape x1, local copies, waits for them, and re-layouts, score_one(): largest = jnp.max(similar.reshape(-1, shard_count, PL), axis=2)  7.73 us
    select_n x1, local copies, waits for them, and re-layouts, score_one(): similar = jnp.where(flat_alive[None, :], similar, -1e+30)  4.4 us
    reduce_max x1, other arithmetic, score_one(): largest = jnp.max(similar.reshape(-1, shard_count, PL), axis=2)  4.09 us
    dot_general x1, matrix products, score_one(): jnp.einsum('ed,md->em', row_expanded, flat_tiles, precision=highest)  3.9 us
  transfers between devices with their start and end apart: 1, of which 1 were waited for; matrix products, arithmetic and copies ran while one was open for 1% of the time, Pallas kernels for 0%

commit v1 on v0

v1 whole, which is shorter than its diff:
```python
import functools

import jax
import jax.numpy as jnp
from jax import lax
from jax.experimental import pallas as pl
from jax.experimental.pallas import tpu as pltpu
from jax.sharding import PartitionSpec as P

DIM = 128
QL = 32
NCENT = 24
EXP = 10
CAP = 2
FB = 3
BETA = 0.5
AXES = ("query", "corpus")
ID_ROW = 31
CAND_ROW = 32
HIGHEST = lax.Precision.HIGHEST


def iota(shape, axis):
    return lax.broadcasted_iota(jnp.int32, shape, axis)


def spread(index, masks):
    total = 0
    for k, mask in enumerate(masks):
        total = total | (((index >> k) & 1) * mask)
    return total


def gather_bits(device, masks):
    total = 0
    for k, mask in enumerate(masks):
        total = total | (jnp.where((device & mask) != 0, 1, 0) << k)
    return total


def pairs_kernel(queries_n, held, tokens, pos_ref, len_ref, tiles_ref, clusters_ref, feedback_ref, ranks_ref,
                 local_ref, count_ref, masked_ref, pay_ref):
    pos = pos_ref[0]
    per_tile = 8 // held
    row = iota((8, DIM), 0)
    limit = jnp.zeros((8, DIM), jnp.int32)
    for p in range(held):
        limit = jnp.where(row % held == p, len_ref[p], limit)
    first = tiles_ref[0:held, :]
    first = jnp.concatenate([first] * per_tile, axis=0)
    groups = tokens * held // 8
    token = iota((groups, 8, DIM), 0) * per_tile + (iota((groups, 8, DIM), 1) // held)
    tiles = tiles_ref[...].reshape(groups, 8, DIM)
    masked_ref[...] = jnp.where(token < limit[None], tiles, first[None]).reshape(groups * 8, DIM)

    nearby = feedback_ref[...] - pos * held
    number = (iota(nearby.shape, 0) * queries_n + iota(nearby.shape, 1)) * held + nearby
    far = 1e9
    key = jnp.where((nearby >= 0) & (nearby < held), number.astype(jnp.float32), far)
    ranks = ranks_ref[...].astype(jnp.float32)
    lane = iota(ranks.shape, 1)
    pay_ref[...] = jnp.zeros(pay_ref.shape, jnp.float32)
    ids = jnp.zeros((1, DIM), jnp.float32)
    slot = iota((1, DIM), 1) // EXP
    kinds = iota((NCENT, tokens), 0)
    times = iota((EXP, tokens), 1)
    wanted = iota((EXP, tokens), 0).astype(jnp.float32)
    for s in range(FB):
        best = jnp.min(key)
        key = jnp.where(key > best, key, far)
        whole = best.astype(jnp.int32)
        p = whole % held
        q = (whole // held) % queries_n
        ids = jnp.where(slot == s, q.astype(jnp.float32), ids)
        rank = jnp.sum(jnp.where(lane == q, ranks, 0.0), axis=1, keepdims=True)
        kind = clusters_ref[pl.ds(p, 1), :]
        of_token = jnp.sum(jnp.where(kind == kinds, rank, 0.0), axis=0, keepdims=True)
        chosen = jnp.where((of_token == wanted) & (times < len_ref[p]), 1.0, 0.0)
        passage = tiles_ref[pl.ds(p, tokens, stride=held), :]
        pay_ref[s * EXP:(s + 1) * EXP, :] = jnp.dot(
            chosen, passage, precision=HIGHEST, preferred_element_type=jnp.float32)
    pay_ref[ID_ROW:ID_ROW + 1, :] = ids
    for c, at in enumerate(range(0, queries_n, DIM)):
        width = min(DIM, queries_n - at)
        top = CAND_ROW + (CAP + 1) * c
        pay_ref[top:top + CAP, 0:width] = local_ref[:, at:at + width].astype(jnp.float32)
        pay_ref[top + CAP:top + CAP + 1, 0:width] = count_ref[:, at:at + width].astype(jnp.float32)


def combine_kernel(inner, outer, pos_ref, *refs):
    *pays, tokens_ref, out_ref = refs
    pos = pos_ref[0]
    inside = sum(inner)
    rows = (1 << len(outer)) * EXP
    row = iota((rows, DIM), 0)
    owner = (pos & inside) | spread(row // EXP, outer)
    col = iota((rows, DIM), 1)
    fits = (col % EXP == row % EXP) & (col < FB * EXP)
    total = jnp.zeros((rows, DIM), jnp.float32)
    for pay in pays:
        for at in range(0, pay.shape[0], pay_rows_of(pays)):
            ids = pay[at + ID_ROW:at + ID_ROW + 1, :]
            pick = jnp.where(fits & (ids == owner.astype(jnp.float32)), 1.0, 0.0)[:, :32]
            block = pay[at:at + 32, :]
            block = jnp.where(iota((32, DIM), 0) < FB * EXP, block, 0.0)
            total += jnp.dot(pick, block, precision=HIGHEST, preferred_element_type=jnp.float32)
    out_ref[0:rows, :] = total
    out_ref[rows:rows + QL, :] = tokens_ref[...]


def pay_rows_of(pays):
    return pays[0].shape[0]


def nt_dot(a, b, precision=None):
    return lax.dot_general(a, b, (((1,), (1,)), ((), ())), precision=precision, preferred_element_type=jnp.float32)


def split(x):
    high = x.astype(jnp.bfloat16)
    return high, (x - high.astype(jnp.float32)).astype(jnp.bfloat16)


def score_kernel(inner, outer, queries_n, held, tokens, n_tiles, n_pays, pos_ref, *refs):
    tile_refs = refs[:n_tiles]
    pay_refs = refs[n_tiles:n_tiles + n_pays]
    mine_ref, theirs_ref, out_ref = refs[n_tiles + n_pays:]
    pos = pos_ref[0]
    inside, outside = sum(inner), sum(outer)
    n_in, n_out = 1 << len(inner), 1 << len(outer)
    me_in = gather_bits(pos, inner)
    me_out = gather_bits(pos, outer)
    rows = n_out * EXP
    sums = mine_ref[0:rows, :] + theirs_ref[0:rows, :]
    scale = lax.rsqrt(jnp.mean(sums * sums, axis=1, keepdims=True) + 1e-05)
    order = (iota((rows, 1), 0) % EXP).astype(jnp.float32)
    weight = BETA * jnp.log((NCENT + 1.0) / (order + 1.0))
    extra = sums * (scale * weight)
    expanded = jnp.concatenate([mine_ref[rows:, :], theirs_ref[rows:, :], extra], axis=0)
    total = expanded.shape[0]
    lefts = []
    for ref in tile_refs:
        high, low = split(ref[...])
        lefts.append((high, jnp.concatenate([high, low], axis=1)))
    parts = [[] for _ in lefts]
    for at in range(0, total, 256):
        high, low = split(expanded[at:at + 256])
        twice = jnp.concatenate([high, high], axis=1)
        for i, (left, wide) in enumerate(lefts):
            similar = nt_dot(wide, twice) + nt_dot(left, low)
            groups = similar.shape[0] // 8
            parts[i].append(jnp.max(similar.reshape(groups, 8, similar.shape[1]), axis=0))
    largest = []
    for part in parts:
        top = jnp.concatenate(part, axis=1)
        step = held
        while step < 8:
            top = jnp.maximum(top, pltpu.roll(top, step, 0))
            step *= 2
        largest.append(top)
    largest = jnp.concatenate(largest, axis=0)
    col = iota((n_out, total), 1)
    of_col = jnp.where(col < n_out * QL, (col // QL) ^ me_out, (col - n_out * QL) // EXP)
    member = jnp.where(of_col == iota((n_out, total), 0), 1.0 / QL, 0.0)
    values = nt_dot(member, largest, HIGHEST)

    cands = jnp.concatenate([
        pay[at + CAND_ROW:at + CAND_ROW + 8, :]
        for pay in pay_refs for at in range(0, pay.shape[0], pay_refs[0].shape[0])
    ], axis=0)
    shape = (n_out, DIM)
    own = (pos & inside) | spread(iota(shape, 0), outer)
    slots = out_ref.shape[1]
    slot = iota((n_in * 8, slots), 1)
    entry = iota((n_in * 8, slots), 0)
    device = slot // CAP
    block = gather_bits(device, inner) ^ me_in
    same = block == entry // 8
    local = jnp.zeros((n_out, slots), jnp.float32)
    count = jnp.zeros((n_out, slots), jnp.float32)
    for c, at in enumerate(range(0, queries_n, DIM)):
        found = nt_dot(jnp.where(own - at == iota(shape, 1), 1.0, 0.0), cands, HIGHEST)
        top = (CAP + 1) * c
        pick = jnp.where(same & (entry % 8 == top + slot % CAP), 1.0, 0.0)
        local += jnp.dot(found, pick, precision=HIGHEST, preferred_element_type=jnp.float32)
        pick = jnp.where(same & (entry % 8 == top + CAP), 1.0, 0.0)
        count += jnp.dot(found, pick, precision=HIGHEST, preferred_element_type=jnp.float32)
    result = jnp.zeros((n_out, slots), jnp.float32)
    for p in range(held):
        pick = jnp.where(same & (entry % 8 == p), 1.0, 0.0)
        value = jnp.dot(values, pick, precision=HIGHEST, preferred_element_type=jnp.float32)
        result = jnp.where(local == float(p), value, result)
    slot = iota((n_out, slots), 1)
    live = ((slot % CAP).astype(jnp.float32) < count) & (((slot // CAP) & outside) == (pos & outside))
    out_ref[...] = jnp.where(live, result, 0.0)


def call(kernel, outs, *args, flops=0):
    smem = pl.BlockSpec(memory_space=pltpu.SMEM)
    vmem = pl.BlockSpec(memory_space=pltpu.VMEM)
    specs = [smem if a.ndim == 1 else vmem for a in args]
    moved = sum(a.size * 4 for a in args) + sum(o.size * 4 for o in outs)
    return pl.pallas_call(
        kernel,
        out_shape=outs if len(outs) > 1 else outs[0],
        in_specs=specs,
        out_specs=[vmem] * len(outs) if len(outs) > 1 else vmem,
        compiler_params=pltpu.CompilerParams(vmem_limit_bytes=40 * 1024 * 1024),
        cost_estimate=pl.CostEstimate(flops=flops, bytes_accessed=moved, transcendentals=0),
    )(*args)


def body(queries, passages, clusters, lengths, feedback, ranks, cand_local, cand_count):
    held, tokens, _ = passages.shape
    queries_n = feedback.shape[0]
    n_corpus = lax.axis_size("corpus")
    devices = lax.axis_size("query") * n_corpus
    masks = [1 << k for k in range(devices.bit_length() - 1)]
    inner = [1, n_corpus]
    outer = [2 * n_corpus] + [m for m in masks if m not in inner and m != 2 * n_corpus]
    n_out = 1 << len(outer)
    pos = lax.axis_index(AXES).astype(jnp.int32).reshape(1)

    def swap(x, mask):
        return lax.ppermute(x, AXES, [(i, i ^ mask) for i in range(devices)])

    def struct(rows, cols=DIM):
        return jax.ShapeDtypeStruct((rows, cols), jnp.float32)

    chunks = -(-queries_n // DIM)
    pay_rows = CAND_ROW + 8
    assert (CAP + 1) * chunks <= 8 and queries.shape[0] == 1 and 8 % held == 0
    tiles = jnp.transpose(passages, (1, 0, 2)).reshape(tokens * held, DIM)
    masked, pay = call(
        functools.partial(pairs_kernel, queries_n, held, tokens),
        [struct(tokens * held), struct(pay_rows)],
        pos, lengths, tiles, clusters, feedback.T, ranks.T, cand_local.T, cand_count.T,
    )
    blocks, pays = [masked], [pay]
    for mask in inner:
        blocks = blocks + [swap(b, mask) for b in blocks]
        joined = pays[0] if len(pays) == 1 else jnp.concatenate(pays, axis=0)
        pays = pays + [swap(joined, mask)]
    send = call(functools.partial(combine_kernel, inner, outer), [struct(n_out * EXP + QL)], pos, *pays, queries[0])
    rows = n_out * EXP
    for mask in outer[:-1]:
        came = swap(send, mask)
        send = jnp.concatenate([send[:rows] + came[:rows], send[rows:], came[rows:]], axis=0)
    came = swap(send, outer[-1])
    table = call(
        functools.partial(score_kernel, inner, outer, queries_n, held, tokens, len(blocks), len(pays)),
        [struct(n_out, devices * CAP)],
        pos, *blocks, *pays, send, came,
        flops=2 * 3 * n_out * (QL + EXP) * len(blocks) * held * tokens * DIM,
    )
    for mask in reversed(outer):
        table = table + swap(table, mask)
    mine = sum(jnp.where((pos[0] & mask) != 0, 1 << k, 0) for k, mask in enumerate(outer))
    return lax.dynamic_slice(table, (mine, 0), (1, devices * CAP))


def solution(mesh):
    in_specs = (
        P(AXES, None, None),
        P(AXES, None, None),
        P(AXES, None),
        P(AXES),
        P(),
        P(),
        P(None, AXES),
        P(None, AXES),
    )
    return jax.shard_map(body, mesh=mesh, in_specs=in_specs, out_specs=P(AXES, None), check_vma=False)
```

time: 191 us -> 46.4 us (0.24)
  waiting for transfers between devices: 84.2 us -> 21.6 us
  blocking collectives: 61.9 us -> 0 us
  starting transfers between devices: 0.01 us -> 18.6 us
  local copies, waits for them, and re-layouts: 15.8 us -> 2.25 us
  between operations: 13.5 us -> 0.06 us
  other arithmetic: 8.03 us -> 0.04 us
  matrix products: 7.34 us -> 0 us
  Pallas kernels: 0 us -> 3.63 us
    psum x1 -> x0, waiting for transfers between devices: 84.2 us -> none  [body(): lax.psum(jnp.dot(requests, local_sums.reshape(shard_count, NCENT * DIM),...]
    all_gather x1 -> x0, blocking collectives: 45.7 us -> none  [body(): piece = lax.all_gather(queries, ('query', 'corpus'), axis=0, tiled=True)]
    ppermute x0 -> x11, waiting for transfers between devices: none -> 21.6 us  [swap(): return lax.ppermute(x, AXES, [(i, i ^ mask) for i in range(devices)])]
    ppermute x0 -> x11, starting transfers between devices: none -> 18.6 us  [swap(): return lax.ppermute(x, AXES, [(i, i ^ mask) for i in range(devices)])]
    all_to_all x2 -> x0, blocking collectives: 16.2 us -> none  [the longest x1 8.13 us: body(): lax.all_to_all(lax.all_to_all(blocks, 'query', split_axis=0, concat_axis=...]
    reshape x2 -> x0, local copies, waits for them, and re-layouts: 7.76 us -> none  [the longest x1 7.73 us: score_one(): largest = jnp.max(similar.reshape(-1, shard_count, PL), axis=2)]
    dot_general x5 -> x0, matrix products: 7.34 us -> none  [the longest x1 3.9 us: score_one(): jnp.einsum('ed,md->em', row_expanded, flat_tiles, precision=highest)]
    select_n x1 -> x0, local copies, waits for them, and re-layouts: 4.4 us -> none  [score_one(): similar = jnp.where(flat_alive[None, :], similar, -1e+30)]
  transfers between devices with their start and end apart: 1 -> 11, of which waited for: 1 -> 10; matrix products, arithmetic and copies ran while one was open for 1% -> 0% of each run, Pallas kernels for 0% -> 0%
where the time goes in v1:
time: 46.4 us; the launch traced here: 46.2 us
  waiting for transfers between devices  21.6 us (47%)
  starting transfers between devices  18.6 us (40%)
  Pallas kernels  3.63 us (8%)
  local copies, waits for them, and re-layouts  2.25 us (5%)
    ppermute x11, waiting for transfers between devices, swap(): return lax.ppermute(x, AXES, [(i, i ^ mask) for i in range(devices)])  21.6 us
    ppermute x11, starting transfers between devices, swap(): return lax.ppermute(x, AXES, [(i, i ^ mask) for i in range(devices)])  18.6 us
    pallas_call x3, Pallas kernels, call(): pl.pallas_call(kernel, out_shape=outs if len(outs) > 1 else outs[0], in_s...  3.63 us
    unnamed x16, local copies, waits for them, and re-layouts  1.72 us
  transfers between devices with their start and end apart: 11, of which 10 were waited for; matrix products, arithmetic and copies ran while one was open for 0% of the time, Pallas kernels for 0%

profile of v1, /device:TPU:0, one launch (start us, length us, event | category | flops | bytes accessed | tf_op | source)
XLA Modules:
  0.0 46.2 jit_solution(10809147100398902771)
XLA Ops:
  0.0 0.0 copy-start.2
  0.0 0.0 copy-start.7
  0.0 0.0 copy-start.3
  0.0 0.0 copy-start.4
  0.0 0.0 copy-start.5
  0.0 0.0 copy-start.6
  0.0 0.7 %copy-done.2 = s32[32,24]{0,1:T(8,128)S(1)} copy-done((s32[32,24]{0,1:T(8,128)S(1)}, s32[32,24]{0,1:T(8,128)}, u32[]{:S(2)}) %copy-start.2) | copy-done | bytes 3096
  0.7 0.0 copy-done.7
  0.7 0.0 copy-done.3
  0.7 0.0 copy-done.4
  0.7 0.0 copy-done.5
  0.7 0.0 copy-done.6
  0.7 0.0 copy-start
  0.7 1.0 %copy-done = f32[4,180,128]{2,0,1:T(4,128)S(1)} copy-done((f32[4,180,128]{2,0,1:T(4,128)S(1)}, f32[4,180,128]{2,0,1:T(4,128)}, u32[]{:S(2)}) %copy-start) | copy-done | bytes 368664
  1.7 1.3 %shard_map.82 = (f32[720,128]{1,0:T(8,128)S(1)}, f32[40,128]{1,0:T(8,128)S(1)}) custom-call(s32[1]{0:T(128)} %bitcast.pos_ref, s32[4]{0:T(128)S(1)} %copy-done.6, f32[720,128]{1,0:T(8,128)S(1)} %bitcast.9, s32[4,180]{1,0:T(4,128)S(1)} %copy-done.3, s32[3,32]{1,0:T(4,128)S(1)} %bitcast.12, s32[24,32]{1,0:T(8,128)S(1)} %bitcast.11, s32[2,32]{1,0:T(2,128)S(1)} %bitcast.13, ...), custom_call_target="tpu_custom_call" | custom-call | bytes 764500 | tf_op jit(solution)/shard_map/pallas_call | solution.py:203
  3.0 0.0 copy-start.1
  3.0 0.5 collective-permute-start.3
  3.5 0.8 %collective-permute-done.3.refs_1_.refs_5_ = f32[40,128]{1,0:T(8,128)S(1)} collective-permute-done((f32[40,128]{1,0:T(8,128)S(1)}, f32[40,128]{1,0:T(8,128)S(1)}, u32[]{:S(2)}, u32[]{:S(2)}) %collective-permute-start.3) | collective-permute-done | bytes 20512 | tf_op jit(solution)/shard_map/ppermute | solution.py:225
  4.3 2.8 %collective-permute-start.4 = (f32[80,128]{1,0:T(8,128)S(1)}, f32[80,128]{1,0:T(8,128)S(1)}, u32[]{:S(2)}, u32[]{:S(2)}) collective-permute-start(f32[80,128]{1,0:T(8,128)S(1)} %pad_maximum_fusion.2), channel_id=1, source_target_pairs={{0,8},{1,9},{2,10},{3,11},{4,12},{5,13},{6,14},{7,15},{8,0},{9,1},... | collective-permute-start | bytes 122888 | tf_op jit(solution)/shard_map/ppermute | solution.py:225
  7.1 2.0 %collective-permute-done.4.refs_2_.refs_6_ = f32[80,128]{1,0:T(8,128)S(1)} collective-permute-done((f32[80,128]{1,0:T(8,128)S(1)}, f32[80,128]{1,0:T(8,128)S(1)}, u32[]{:S(2)}, u32[]{:S(2)}) %collective-permute-start.4) | collective-permute-done | bytes 40992 | tf_op jit(solution)/shard_map/ppermute | solution.py:225
  9.1 0.0 copy-done.1
  9.1 0.3 shard_map.83
  9.4 2.1 %collective-permute-start.5 = (f32[112,128]{1,0:T(8,128)S(1)}, f32[112,128]{1,0:T(8,128)S(1)}, u32[]{:S(2)}, u32[]{:S(2)}) collective-permute-start(f32[112,128]{1,0:T(8,128)S(1)} %shard_map.83), channel_id=1, source_target_pairs={{0,16},{1,17},{2,18},{3,19},{4,20},{5,21},{6,22},{7,23},{8,24},{9,... | collective-permute-start | bytes 172040 | tf_op jit(solution)/shard_map/ppermute | solution.py:225
  11.5 0.0 collective-permute-start
  11.6 2.2 %collective-permute-done.5 = f32[112,128]{1,0:T(8,128)S(1)} collective-permute-done((f32[112,128]{1,0:T(8,128)S(1)}, f32[112,128]{1,0:T(8,128)S(1)}, u32[]{:S(2)}, u32[]{:S(2)}) %collective-permute-start.5) | collective-permute-done | bytes 57376 | tf_op jit(solution)/shard_map/ppermute | solution.py:225
  13.7 2.2 %collective-permute-start.6 = (f32[144,128]{1,0:T(8,128)S(1)}, f32[144,128]{1,0:T(8,128)S(1)}, u32[]{:S(2)}, u32[]{:S(2)}) collective-permute-start(f32[144,128]{1,0:T(8,128)S(1)} %pad_maximum_fusion.1), channel_id=1, source_target_pairs={{0,2},{1,3},{2,0},{3,1},{4,6},{5,7},{6,4},{7,5},{8,10},{9,11},{10,... | collective-permute-start | bytes 221192 | tf_op jit(solution)/shard_map/ppermute | solution.py:225
  15.9 1.5 %collective-permute-start.1 = (f32[720,128]{1,0:T(8,128)S(1)}, f32[720,128]{1,0:T(8,128)S(1)}, u32[]{:S(2)}, u32[]{:S(2)}) collective-permute-start(f32[720,128]{1,0:T(8,128)S(1)} %get-tuple-element.7.refs_0_), channel_id=1, source_target_pairs={{0,8},{1,9},{2,10},{3,11},{4,12},{5,13},{6,14},{7,15},{8,0},{9,1},... | collective-permute-start | bytes 1105928 | tf_op jit(solution)/shard_map/ppermute | solution.py:225
  17.4 0.9 %collective-permute-done.6 = f32[144,128]{1,0:T(8,128)S(1)} collective-permute-done((f32[144,128]{1,0:T(8,128)S(1)}, f32[144,128]{1,0:T(8,128)S(1)}, u32[]{:S(2)}, u32[]{:S(2)}) %collective-permute-start.6) | collective-permute-done | bytes 73760 | tf_op jit(solution)/shard_map/ppermute | solution.py:225
  18.2 0.0 collective-permute-done.refs_1_
  18.2 1.9 %collective-permute-start.2 = (f32[720,128]{1,0:T(8,128)S(1)}, f32[720,128]{1,0:T(8,128)S(1)}, u32[]{:S(2)}, u32[]{:S(2)}) collective-permute-start(f32[720,128]{1,0:T(8,128)S(1)} %collective-permute-done.refs_1_), channel_id=1, source_target_pairs={{0,8},{1,9},{2,10},{3,11},{4,12},{5,13},{6,14},{7,15},{8,0},{9,1},... | collective-permute-start | bytes 1105928 | tf_op jit(solution)/shard_map/ppermute | solution.py:225
  20.2 3.1 %collective-permute-start.7 = (f32[208,128]{1,0:T(8,128)S(1)}, f32[208,128]{1,0:T(8,128)S(1)}, u32[]{:S(2)}, u32[]{:S(2)}) collective-permute-start(f32[208,128]{1,0:T(8,128)S(1)} %pad_maximum_fusion.refs_7_), channel_id=1, source_target_pairs={{0,4},{1,5},{2,6},{3,7},{4,0},{5,1},{6,2},{7,3},{8,12},{9,13},{10,... | collective-permute-start | bytes 319496 | tf_op jit(solution)/shard_map/ppermute | solution.py:225
  23.3 3.8 %collective-permute-done.7.refs_8_ = f32[208,128]{1,0:T(8,128)S(1)} collective-permute-done((f32[208,128]{1,0:T(8,128)S(1)}, f32[208,128]{1,0:T(8,128)S(1)}, u32[]{:S(2)}, u32[]{:S(2)}) %collective-permute-start.7) | collective-permute-done | bytes 106528 | tf_op jit(solution)/shard_map/ppermute | solution.py:225
  27.1 0.3 collective-permute-done.1.refs_2_
  27.4 4.4 %collective-permute-done.2.refs_3_ = f32[720,128]{1,0:T(8,128)S(1)} collective-permute-done((f32[720,128]{1,0:T(8,128)S(1)}, f32[720,128]{1,0:T(8,128)S(1)}, u32[]{:S(2)}, u32[]{:S(2)}) %collective-permute-start.2) | collective-permute-done | bytes 368672 | tf_op jit(solution)/shard_map/ppermute | solution.py:225
  31.9 2.1 %shard_map.84 = f32[8,64]{1,0:T(8,128)S(1)} custom-call(s32[1]{0:T(128)} %bitcast.pos_ref, f32[720,128]{1,0:T(8,128)S(1)} %get-tuple-element.7.refs_0_, f32[720,128]{1,0:T(8,128)S(1)} %collective-permute-done.refs_1_, f32[720,128]{1,0:T(8,128)S(1)} %collective-permute-done.1.refs_2_, f32[720,128]{1,0:T(8,128)S(1)} %collective-permute-done.2.refs_3_, ...), custom_call_target="tpu_custom_call" | custom-call | flops 743178240 | bytes 1771524 | tf_op jit(solution)/shard_map/pallas_call | solution.py:203
  33.9 2.6 %collective-permute-start.8 = (f32[8,64]{1,0:T(8,128)S(1)}, f32[8,64]{1,0:T(8,128)S(1)}, u32[]{:S(2)}, u32[]{:S(2)}) collective-permute-start(f32[8,64]{1,0:T(8,128)S(1)} %shard_map.84), channel_id=1, source_target_pairs={{0,4},{1,5},{2,6},{3,7},{4,0},{5,1},{6,2},{7,3},{8,12},{9,13},{10,... | collective-permute-start | bytes 6152 | tf_op jit(solution)/shard_map/ppermute | solution.py:225
  36.5 1.9 %collective-permute-done.8 = f32[8,64]{1,0:T(8,128)S(1)} collective-permute-done((f32[8,64]{1,0:T(8,128)S(1)}, f32[8,64]{1,0:T(8,128)S(1)}, u32[]{:S(2)}, u32[]{:S(2)}) %collective-permute-start.8) | collective-permute-done | bytes 2080 | tf_op jit(solution)/shard_map/ppermute | solution.py:225
  38.4 0.4 collective-permute-start.9
  38.9 3.2 %collective-permute-done.9 = f32[8,64]{1,0:T(8,128)S(1)} collective-permute-done((f32[8,64]{1,0:T(8,128)S(1)}, f32[8,64]{1,0:T(8,128)S(1)}, u32[]{:S(2)}, u32[]{:S(2)}) %collective-permute-start.9) | collective-permute-done | bytes 2080 | tf_op jit(solution)/shard_map/ppermute | solution.py:225
  42.0 1.5 %collective-permute-start.10 = (f32[8,64]{1,0:T(8,128)S(1)}, f32[8,64]{1,0:T(8,128)S(1)}, u32[]{:S(2)}, u32[]{:S(2)}) collective-permute-start(f32[8,64]{1,0:T(8,128)S(1)} %add.31), channel_id=1, source_target_pairs={{0,16},{1,17},{2,18},{3,19},{4,20},{5,21},{6,22},{7,23},{8,24},{9,... | collective-permute-start | bytes 6152 | tf_op jit(solution)/shard_map/ppermute | solution.py:225
  43.6 2.1 %collective-permute-done.10 = f32[8,64]{1,0:T(8,128)S(1)} collective-permute-done((f32[8,64]{1,0:T(8,128)S(1)}, f32[8,64]{1,0:T(8,128)S(1)}, u32[]{:S(2)}, u32[]{:S(2)}) %collective-permute-start.10) | collective-permute-done | bytes 2080 | tf_op jit(solution)/shard_map/ppermute | solution.py:225
  45.7 0.5 %constant_dynamic-slice_fusion = f32[1,64]{1,0:T(1,128)} fusion(f32[8,64]{1,0:T(8,128)S(1)} %add.32, s32[]{:T(128)S(6)} %select_n.16), kind=kLoop, calls=%fused_computation.5 | loop fusion | bytes 516 | tf_op jit(solution)/shard_map/dynamic_slice | solution.py:259
  (11 shorter events, 0.1 us)
Async XLA Ops:
  0.0 0.7 %copy-start.2 = (s32[32,24]{0,1:T(8,128)S(1)}, s32[32,24]{0,1:T(8,128)}, u32[]{:S(2)}) copy-start(s32[32,24]{0,1:T(8,128)} %param.13) | copy-start | bytes 9220
  0.0 0.7 %copy-start.7 = (s32[32,1]{0,1:T(1,128)S(1)}, s32[32,1]{0,1:T(1,128)}, u32[]{:S(2)}) copy-start(s32[32,1]{0,1:T(1,128)} %param.15) | copy-start | bytes 388
  0.0 0.7 %copy-start.3 = (s32[4,180]{1,0:T(4,128)S(1)}, s32[4,180]{1,0:T(4,128)}, u32[]{:S(2)}) copy-start(s32[4,180]{1,0:T(4,128)} %clusters_ref.1) | copy-start | bytes 8644
  0.0 0.7 %copy-start.4 = (s32[32,3]{0,1:T(4,128)S(1)}, s32[32,3]{0,1:T(4,128)}, u32[]{:S(2)}) copy-start(s32[32,3]{0,1:T(4,128)} %param.12) | copy-start | bytes 1156
  0.0 0.7 %copy-start.5 = (s32[32,2]{0,1:T(2,128)S(1)}, s32[32,2]{0,1:T(2,128)}, u32[]{:S(2)}) copy-start(s32[32,2]{0,1:T(2,128)} %param.14) | copy-start | bytes 772
  0.0 0.7 %copy-start.6 = (s32[4]{0:T(128)S(1)}, s32[4]{0:T(128)}, u32[]{:S(2)}) copy-start(s32[4]{0:T(128)} %len_ref.1) | copy-start | bytes 52
  0.7 1.0 %copy-start = (f32[4,180,128]{2,0,1:T(4,128)S(1)}, f32[4,180,128]{2,0,1:T(4,128)}, u32[]{:S(2)}) copy-start(f32[4,180,128]{2,0,1:T(4,128)} %param.9) | copy-start | bytes 1105924
  3.0 6.1 %copy-start.1 = (f32[1,32,128]{2,1,0:T(8,128)S(1)}, f32[1,32,128]{2,1,0:T(8,128)}, u32[]{:S(2)}) copy-start(f32[1,32,128]{2,1,0:T(8,128)} %param.8) | copy-start | bytes 49156
  3.0 1.3 %collective-permute-start.3 = (f32[40,128]{1,0:T(8,128)S(1)}, f32[40,128]{1,0:T(8,128)S(1)}, u32[]{:S(2)}, u32[]{:S(2)}) collective-permute-start(f32[40,128]{1,0:T(8,128)S(1)} %get-tuple-element.8.refs_0_.refs_4_), channel_id=1, source_target_pairs={{0,1},{1,0},{2,3},{3,2},{4,5},{5,4},{6,7},{7,6},{8,9},{9,8},{10,11... | collective-permute-start | bytes 61448 | tf_op jit(solution)/shard_map/ppermute | solution.py:225
  4.3 4.8 %collective-permute-start.4 = (f32[80,128]{1,0:T(8,128)S(1)}, f32[80,128]{1,0:T(8,128)S(1)}, u32[]{:S(2)}, u32[]{:S(2)}) collective-permute-start(f32[80,128]{1,0:T(8,128)S(1)} %pad_maximum_fusion.2), channel_id=1, source_target_pairs={{0,8},{1,9},{2,10},{3,11},{4,12},{5,13},{6,14},{7,15},{8,0},{9,1},... | collective-permute-start | bytes 122888 | tf_op jit(solution)/shard_map/ppermute | solution.py:225
  9.4 4.3 %collective-permute-start.5 = (f32[112,128]{1,0:T(8,128)S(1)}, f32[112,128]{1,0:T(8,128)S(1)}, u32[]{:S(2)}, u32[]{:S(2)}) collective-permute-start(f32[112,128]{1,0:T(8,128)S(1)} %shard_map.83), channel_id=1, source_target_pairs={{0,16},{1,17},{2,18},{3,19},{4,20},{5,21},{6,22},{7,23},{8,24},{9,... | collective-permute-start | bytes 172040 | tf_op jit(solution)/shard_map/ppermute | solution.py:225
  11.5 6.7 %collective-permute-start = (f32[720,128]{1,0:T(8,128)S(1)}, f32[720,128]{1,0:T(8,128)S(1)}, u32[]{:S(2)}, u32[]{:S(2)}) collective-permute-start(f32[720,128]{1,0:T(8,128)S(1)} %get-tuple-element.7.refs_0_), channel_id=1, source_target_pairs={{0,1},{1,0},{2,3},{3,2},{4,5},{5,4},{6,7},{7,6},{8,9},{9,8},{10,11... | collective-permute-start | bytes 1105928 | tf_op jit(solution)/shard_map/ppermute | solution.py:225
  13.7 4.5 %collective-permute-start.6 = (f32[144,128]{1,0:T(8,128)S(1)}, f32[144,128]{1,0:T(8,128)S(1)}, u32[]{:S(2)}, u32[]{:S(2)}) collective-permute-start(f32[144,128]{1,0:T(8,128)S(1)} %pad_maximum_fusion.1), channel_id=1, source_target_pairs={{0,2},{1,3},{2,0},{3,1},{4,6},{5,7},{6,4},{7,5},{8,10},{9,11},{10,... | collective-permute-start | bytes 221192 | tf_op jit(solution)/shard_map/ppermute | solution.py:225
  15.9 11.5 %collective-permute-start.1 = (f32[720,128]{1,0:T(8,128)S(1)}, f32[720,128]{1,0:T(8,128)S(1)}, u32[]{:S(2)}, u32[]{:S(2)}) collective-permute-start(f32[720,128]{1,0:T(8,128)S(1)} %get-tuple-element.7.refs_0_), channel_id=1, source_target_pairs={{0,8},{1,9},{2,10},{3,11},{4,12},{5,13},{6,14},{7,15},{8,0},{9,1},... | collective-permute-start | bytes 1105928 | tf_op jit(solution)/shard_map/ppermute | solution.py:225
  18.2 13.6 %collective-permute-start.2 = (f32[720,128]{1,0:T(8,128)S(1)}, f32[720,128]{1,0:T(8,128)S(1)}, u32[]{:S(2)}, u32[]{:S(2)}) collective-permute-start(f32[720,128]{1,0:T(8,128)S(1)} %collective-permute-done.refs_1_), channel_id=1, source_target_pairs={{0,8},{1,9},{2,10},{3,11},{4,12},{5,13},{6,14},{7,15},{8,0},{9,1},... | collective-permute-start | bytes 1105928 | tf_op jit(solution)/shard_map/ppermute | solution.py:225
  20.2 6.9 %collective-permute-start.7 = (f32[208,128]{1,0:T(8,128)S(1)}, f32[208,128]{1,0:T(8,128)S(1)}, u32[]{:S(2)}, u32[]{:S(2)}) collective-permute-start(f32[208,128]{1,0:T(8,128)S(1)} %pad_maximum_fusion.refs_7_), channel_id=1, source_target_pairs={{0,4},{1,5},{2,6},{3,7},{4,0},{5,1},{6,2},{7,3},{8,12},{9,13},{10,... | collective-permute-start | bytes 319496 | tf_op jit(solution)/shard_map/ppermute | solution.py:225
  33.9 4.5 %collective-permute-start.8 = (f32[8,64]{1,0:T(8,128)S(1)}, f32[8,64]{1,0:T(8,128)S(1)}, u32[]{:S(2)}, u32[]{:S(2)}) collective-permute-start(f32[8,64]{1,0:T(8,128)S(1)} %shard_map.84), channel_id=1, source_target_pairs={{0,4},{1,5},{2,6},{3,7},{4,0},{5,1},{6,2},{7,3},{8,12},{9,13},{10,... | collective-permute-start | bytes 6152 | tf_op jit(solution)/shard_map/ppermute | solution.py:225
  38.4 3.6 %collective-permute-start.9 = (f32[8,64]{1,0:T(8,128)S(1)}, f32[8,64]{1,0:T(8,128)S(1)}, u32[]{:S(2)}, u32[]{:S(2)}) collective-permute-start(f32[8,64]{1,0:T(8,128)S(1)} %add.30), channel_id=1, source_target_pairs={{0,2},{1,3},{2,0},{3,1},{4,6},{5,7},{6,4},{7,5},{8,10},{9,11},{10,... | collective-permute-start | bytes 6152 | tf_op jit(solution)/shard_map/ppermute | solution.py:225
  42.0 3.6 %collective-permute-start.10 = (f32[8,64]{1,0:T(8,128)S(1)}, f32[8,64]{1,0:T(8,128)S(1)}, u32[]{:S(2)}, u32[]{:S(2)}) collective-permute-start(f32[8,64]{1,0:T(8,128)S(1)} %add.31), channel_id=1, source_target_pairs={{0,16},{1,17},{2,18},{3,19},{4,20},{5,21},{6,22},{7,23},{8,24},{9,... | collective-permute-start | bytes 6152 | tf_op jit(solution)/shard_map/ppermute | solution.py:225

commit v2 on v1

--- a/solution.py
+++ b/solution.py
@@ -88,7 +88,7 @@
 
 
 def combine_kernel(inner, outer, pos_ref, *refs):
-    *pays, tokens_ref, out_ref = refs
+    *pays, out_ref = refs
     pos = pos_ref[0]
     inside = sum(inner)
     rows = (1 << len(outer)) * EXP
@@ -104,8 +104,7 @@
             block = pay[at:at + 32, :]
             block = jnp.where(iota((32, DIM), 0) < FB * EXP, block, 0.0)
             total += jnp.dot(pick, block, precision=HIGHEST, preferred_element_type=jnp.float32)
-    out_ref[0:rows, :] = total
-    out_ref[rows:rows + QL, :] = tokens_ref[...]
+    out_ref[...] = total
 
 
 def pay_rows_of(pays):
@@ -121,22 +120,22 @@
     return high, (x - high.astype(jnp.float32)).astype(jnp.bfloat16)
 
 
-def score_kernel(inner, outer, queries_n, held, tokens, n_tiles, n_pays, pos_ref, *refs):
+def score_kernel(inner, outer, queries_n, held, tokens, n_tiles, n_pays, n_asks, pos_ref, *refs):
     tile_refs = refs[:n_tiles]
     pay_refs = refs[n_tiles:n_tiles + n_pays]
-    mine_ref, theirs_ref, out_ref = refs[n_tiles + n_pays:]
+    ask_refs = refs[n_tiles + n_pays:n_tiles + n_pays + n_asks]
+    mine_ref, theirs_ref, out_ref = refs[n_tiles + n_pays + n_asks:]
     pos = pos_ref[0]
     inside, outside = sum(inner), sum(outer)
     n_in, n_out = 1 << len(inner), 1 << len(outer)
     me_in = gather_bits(pos, inner)
     me_out = gather_bits(pos, outer)
-    rows = n_out * EXP
-    sums = mine_ref[0:rows, :] + theirs_ref[0:rows, :]
+    sums = mine_ref[...] + theirs_ref[...]
     scale = lax.rsqrt(jnp.mean(sums * sums, axis=1, keepdims=True) + 1e-05)
-    order = (iota((rows, 1), 0) % EXP).astype(jnp.float32)
+    order = (iota((n_out * EXP, 1), 0) % EXP).astype(jnp.float32)
     weight = BETA * jnp.log((NCENT + 1.0) / (order + 1.0))
     extra = sums * (scale * weight)
-    expanded = jnp.concatenate([mine_ref[rows:, :], theirs_ref[rows:, :], extra], axis=0)
+    expanded = jnp.concatenate([ask[...] for ask in ask_refs] + [extra], axis=0)
     total = expanded.shape[0]
     lefts = []
     for ref in tile_refs:
@@ -216,8 +215,8 @@
     n_corpus = lax.axis_size("corpus")
     devices = lax.axis_size("query") * n_corpus
     masks = [1 << k for k in range(devices.bit_length() - 1)]
-    inner = [1, n_corpus]
-    outer = [2 * n_corpus] + [m for m in masks if m not in inner and m != 2 * n_corpus]
+    inner = [n_corpus, 1]
+    outer = [m for m in reversed(masks) if m not in inner and m != 2 * n_corpus] + [2 * n_corpus]
     n_out = 1 << len(outer)
     pos = lax.axis_index(AXES).astype(jnp.int32).reshape(1)
 
@@ -236,21 +235,31 @@
         [struct(tokens * held), struct(pay_rows)],
         pos, lengths, tiles, clusters, feedback.T, ranks.T, cand_local.T, cand_count.T,
     )
-    blocks, pays = [masked], [pay]
-    for mask in inner:
-        blocks = blocks + [swap(b, mask) for b in blocks]
-        joined = pays[0] if len(pays) == 1 else jnp.concatenate(pays, axis=0)
-        pays = pays + [swap(joined, mask)]
-    send = call(functools.partial(combine_kernel, inner, outer), [struct(n_out * EXP + QL)], pos, *pays, queries[0])
-    rows = n_out * EXP
-    for mask in outer[:-1]:
-        came = swap(send, mask)
-        send = jnp.concatenate([send[:rows] + came[:rows], send[rows:], came[rows:]], axis=0)
-    came = swap(send, outer[-1])
+    asks = [queries[0]]
+
+    def ask(mask):
+        joined = asks[0] if len(asks) == 1 else jnp.concatenate(asks, axis=0)
+        return asks + [swap(joined, mask)]
+
+    def together(*xs):
+        return lax.optimization_barrier(xs)
+
+    asks = ask(outer[0])
+    pays = [pay, swap(pay, inner[0])]
+    masked, _ = together(masked, pays)
+    far = swap(masked, inner[0])
+    pays = pays + [swap(jnp.concatenate(pays, axis=0), inner[1])]
+    sums = call(functools.partial(combine_kernel, inner, outer), [struct(n_out * EXP)], pos, *pays)
+    for mask, coming in zip(outer[:-1], outer[1:]):
+        asks = ask(coming)
+        sums = sums + swap(sums, mask)
+    masked, far, asks, _ = together(masked, far, asks, sums)
+    blocks = [masked, far, swap(masked, inner[1]), swap(far, inner[1])]
+    came = swap(sums, outer[-1])
     table = call(
-        functools.partial(score_kernel, inner, outer, queries_n, held, tokens, len(blocks), len(pays)),
+        functools.partial(score_kernel, inner, outer, queries_n, held, tokens, len(blocks), len(pays), len(asks)),
         [struct(n_out, devices * CAP)],
-        pos, *blocks, *pays, send, came,
+        pos, *blocks, *pays, *asks, sums, came,
         flops=2 * 3 * n_out * (QL + EXP) * len(blocks) * held * tokens * DIM,
     )
     for mask in reversed(outer):

time: 46.4 us -> 40.9 us (0.88)
  waiting for transfers between devices: 21.6 us -> 15.9 us
    ppermute x11 -> x14, waiting for transfers between devices: 21.6 us -> 15.9 us  [swap(): return lax.ppermute(x, AXES, [(i, i ^ mask) for i in range(devices)])]
    ppermute x11 -> x14, starting transfers between devices: 18.6 us -> 18.8 us  [swap(): return lax.ppermute(x, AXES, [(i, i ^ mask) for i in range(devices)])]
  transfers between devices with their start and end apart: 11 -> 14, of which waited for: 10 -> 7; matrix products, arithmetic and copies ran while one was open for 0% -> 0% of each run, Pallas kernels for 0% -> 1%
where the time goes in v2:
time: 40.9 us; the launch traced here: 40.7 us
  starting transfers between devices  18.8 us (46%)
  waiting for transfers between devices  15.9 us (39%)
  Pallas kernels  3.64 us (9%)
  local copies, waits for them, and re-layouts  2.24 us (5%)
    ppermute x14, starting transfers between devices, swap(): return lax.ppermute(x, AXES, [(i, i ^ mask) for i in range(devices)])  18.8 us
    ppermute x14, waiting for transfers between devices, swap(): return lax.ppermute(x, AXES, [(i, i ^ mask) for i in range(devices)])  15.9 us
    pallas_call x3, Pallas kernels, call(): pl.pallas_call(kernel, out_shape=outs if len(outs) > 1 else outs[0], in_s...  3.64 us
    unnamed x16, local copies, waits for them, and re-layouts  1.72 us
  transfers between devices with their start and end apart: 14, of which 7 were waited for; matrix products, arithmetic and copies ran while one was open for 0% of the time, Pallas kernels for 1%

profile of v2, /device:TPU:0, one launch (start us, length us, event | category | flops | bytes accessed | tf_op | source)
XLA Modules:
  0.0 40.7 jit_solution(15963625014159935640)
XLA Ops:
  0.0 0.0 copy-start.2
  0.0 0.0 copy-start.7
  0.0 0.0 copy-start.3
  0.0 0.0 copy-start.4
  0.0 0.0 copy-start.5
  0.0 0.0 copy-start.6
  0.0 0.7 %copy-done.2 = s32[32,24]{0,1:T(8,128)S(1)} copy-done((s32[32,24]{0,1:T(8,128)S(1)}, s32[32,24]{0,1:T(8,128)}, u32[]{:S(2)}) %copy-start.2) | copy-done | bytes 3096
  0.7 0.0 copy-done.7
  0.7 0.0 copy-done.3
  0.7 0.0 copy-done.4
  0.7 0.0 copy-done.5
  0.7 0.0 copy-done.6
  0.7 0.0 copy-start
  0.7 1.0 %copy-done = f32[4,180,128]{2,0,1:T(4,128)S(1)} copy-done((f32[4,180,128]{2,0,1:T(4,128)S(1)}, f32[4,180,128]{2,0,1:T(4,128)}, u32[]{:S(2)}) %copy-start) | copy-done | bytes 368664
  1.7 0.0 copy-start.1
  1.7 1.3 %shard_map.82 = (f32[720,128]{1,0:T(8,128)S(1)}, f32[40,128]{1,0:T(8,128)S(1)}) custom-call(s32[1]{0:T(128)} %bitcast.pos_ref, s32[4]{0:T(128)S(1)} %copy-done.6, f32[720,128]{1,0:T(8,128)S(1)} %bitcast.9, s32[4,180]{1,0:T(4,128)S(1)} %copy-done.3, s32[3,32]{1,0:T(4,128)S(1)} %bitcast.15, s32[24,32]{1,0:T(8,128)S(1)} %bitcast.14, s32[2,32]{1,0:T(2,128)S(1)} %bitcast.16, ...), custom_call_target="tpu_custom_call" | custom-call | bytes 764500 | tf_op jit(solution)/shard_map/pallas_call | solution.py:202
  3.0 2.9 %collective-permute-start = (f32[40,128]{1,0:T(8,128)S(1)}, f32[40,128]{1,0:T(8,128)S(1)}, u32[]{:S(2)}, u32[]{:S(2)}) collective-permute-start(f32[40,128]{1,0:T(8,128)S(1)} %get-tuple-element.15.refs_0_.refs_4_), channel_id=1, source_target_pairs={{0,8},{1,9},{2,10},{3,11},{4,12},{5,13},{6,14},{7,15},{8,0},{9,1},... | collective-permute-start | bytes 61448 | tf_op jit(solution)/shard_map/ppermute | solution.py:224
  5.9 0.0 copy-done.1
  5.9 2.6 %collective-permute-start.2 = (f32[32,128]{1,0:T(8,128)S(1)}, f32[32,128]{1,0:T(8,128)S(1)}, u32[]{:S(2)}, u32[]{:S(2)}) collective-permute-start(f32[32,128]{1,0:T(8,128)S(1)} %bitcast.10), channel_id=1, source_target_pairs={{0,4},{1,5},{2,6},{3,7},{4,0},{5,1},{6,2},{7,3},{8,12},{9,13},{10,... | collective-permute-start | bytes 49160 | tf_op jit(solution)/shard_map/ppermute | solution.py:224
  8.5 0.0 collective-permute-done.refs_1_.refs_5_
  8.5 1.2 %collective-permute-start.1 = (f32[720,128]{1,0:T(8,128)S(1)}, f32[720,128]{1,0:T(8,128)S(1)}, u32[]{:S(2)}, u32[]{:S(2)}) collective-permute-start(f32[720,128]{1,0:T(8,128)S(1)} %get-tuple-element.17.refs_0_), channel_id=1, source_target_pairs={{0,8},{1,9},{2,10},{3,11},{4,12},{5,13},{6,14},{7,15},{8,0},{9,1},... | collective-permute-start | bytes 1105928 | tf_op jit(solution)/shard_map/ppermute | solution.py:224
  9.7 0.0 collective-permute-start.5
  9.7 0.8 %collective-permute-done.2.refs_8_ = f32[32,128]{1,0:T(8,128)S(1)} collective-permute-done((f32[32,128]{1,0:T(8,128)S(1)}, f32[32,128]{1,0:T(8,128)S(1)}, u32[]{:S(2)}, u32[]{:S(2)}) %collective-permute-start.2) | collective-permute-done | bytes 16416 | tf_op jit(solution)/shard_map/ppermute | solution.py:224
  10.6 1.6 %collective-permute-start.3 = (f32[64,128]{1,0:T(8,128)S(1)}, f32[64,128]{1,0:T(8,128)S(1)}, u32[]{:S(2)}, u32[]{:S(2)}) collective-permute-start(f32[64,128]{1,0:T(8,128)S(1)} %pad_maximum_fusion.2), channel_id=1, source_target_pairs={{0,2},{1,3},{2,0},{3,1},{4,6},{5,7},{6,4},{7,5},{8,10},{9,11},{10,... | collective-permute-start | bytes 98312 | tf_op jit(solution)/shard_map/ppermute | solution.py:224
  12.2 0.0 collective-permute-done.5.refs_2_.refs_6_
  12.2 0.3 shard_map.83
  12.5 2.7 %collective-permute-start.6 = (f32[80,128]{1,0:T(8,128)S(1)}, f32[80,128]{1,0:T(8,128)S(1)}, u32[]{:S(2)}, u32[]{:S(2)}) collective-permute-start(f32[80,128]{1,0:T(8,128)S(1)} %shard_map.83), channel_id=1, source_target_pairs={{0,4},{1,5},{2,6},{3,7},{4,0},{5,1},{6,2},{7,3},{8,12},{9,13},{10,... | collective-permute-start | bytes 122888 | tf_op jit(solution)/shard_map/ppermute | solution.py:224
  15.2 0.0 collective-permute-done.3.refs_9_
  15.2 1.6 %collective-permute-start.4 = (f32[128,128]{1,0:T(8,128)S(1)}, f32[128,128]{1,0:T(8,128)S(1)}, u32[]{:S(2)}, u32[]{:S(2)}) collective-permute-start(f32[128,128]{1,0:T(8,128)S(1)} %pad_maximum_fusion), channel_id=1, source_target_pairs={{0,16},{1,17},{2,18},{3,19},{4,20},{5,21},{6,22},{7,23},{8,24},{9,... | collective-permute-start | bytes 196616 | tf_op jit(solution)/shard_map/ppermute | solution.py:224
  16.8 1.0 %collective-permute-done.6 = f32[80,128]{1,0:T(8,128)S(1)} collective-permute-done((f32[80,128]{1,0:T(8,128)S(1)}, f32[80,128]{1,0:T(8,128)S(1)}, u32[]{:S(2)}, u32[]{:S(2)}) %collective-permute-start.6) | collective-permute-done | bytes 40992 | tf_op jit(solution)/shard_map/ppermute | solution.py:224
  17.8 0.2 collective-permute-start.7
  17.9 3.8 %collective-permute-done.7 = f32[80,128]{1,0:T(8,128)S(1)} collective-permute-done((f32[80,128]{1,0:T(8,128)S(1)}, f32[80,128]{1,0:T(8,128)S(1)}, u32[]{:S(2)}, u32[]{:S(2)}) %collective-permute-start.7) | collective-permute-done | bytes 40992 | tf_op jit(solution)/shard_map/ppermute | solution.py:224
  21.8 0.0 collective-permute-done.4.refs_10_
  21.8 0.0 collective-permute-done.1.refs_1_
  21.8 0.1 collective-permute-start.8
  21.9 0.5 %collective-permute-start.9 = (f32[720,128]{1,0:T(8,128)S(1)}, f32[720,128]{1,0:T(8,128)S(1)}, u32[]{:S(2)}, u32[]{:S(2)}) collective-permute-start(f32[720,128]{1,0:T(8,128)S(1)} %collective-permute-done.1.refs_1_), channel_id=1, source_target_pairs={{0,1},{1,0},{2,3},{3,2},{4,5},{5,4},{6,7},{7,6},{8,9},{9,8},{10,11... | collective-permute-start | bytes 1105928 | tf_op jit(solution)/shard_map/ppermute | solution.py:224
  22.4 1.5 %collective-permute-start.10 = (f32[80,128]{1,0:T(8,128)S(1)}, f32[80,128]{1,0:T(8,128)S(1)}, u32[]{:S(2)}, u32[]{:S(2)}) collective-permute-start(f32[80,128]{1,0:T(8,128)S(1)} %add.29.refs_11_), channel_id=1, source_target_pairs={{0,16},{1,17},{2,18},{3,19},{4,20},{5,21},{6,22},{7,23},{8,24},{9,... | collective-permute-start | bytes 122888 | tf_op jit(solution)/shard_map/ppermute | solution.py:224
  23.9 2.5 %collective-permute-done.10.refs_12_ = f32[80,128]{1,0:T(8,128)S(1)} collective-permute-done((f32[80,128]{1,0:T(8,128)S(1)}, f32[80,128]{1,0:T(8,128)S(1)}, u32[]{:S(2)}, u32[]{:S(2)}) %collective-permute-start.10) | collective-permute-done | bytes 40992 | tf_op jit(solution)/shard_map/ppermute | solution.py:224
  26.4 0.0 collective-permute-done.8.refs_2_
  26.4 0.0 collective-permute-done.9.refs_3_
  26.4 2.1 %shard_map.84 = f32[8,64]{1,0:T(8,128)S(1)} custom-call(s32[1]{0:T(128)} %bitcast.pos_ref, f32[720,128]{1,0:T(8,128)S(1)} %get-tuple-element.17.refs_0_, f32[720,128]{1,0:T(8,128)S(1)} %collective-permute-done.1.refs_1_, f32[720,128]{1,0:T(8,128)S(1)} %collective-permute-done.8.refs_2_, f32[720,128]{1,0:T(8,128)S(1)} %collective-permute-done.9.refs_3_, ...), custom_call_target="tpu_custom_call" | custom-call | flops 743178240 | bytes 1771524 | tf_op jit(solution)/shard_map/pallas_call | solution.py:202
  28.5 1.5 %collective-permute-start.11 = (f32[8,64]{1,0:T(8,128)S(1)}, f32[8,64]{1,0:T(8,128)S(1)}, u32[]{:S(2)}, u32[]{:S(2)}) collective-permute-start(f32[8,64]{1,0:T(8,128)S(1)} %shard_map.84), channel_id=1, source_target_pairs={{0,16},{1,17},{2,18},{3,19},{4,20},{5,21},{6,22},{7,23},{8,24},{9,... | collective-permute-start | bytes 6152 | tf_op jit(solution)/shard_map/ppermute | solution.py:224
  30.0 2.1 %collective-permute-done.11 = f32[8,64]{1,0:T(8,128)S(1)} collective-permute-done((f32[8,64]{1,0:T(8,128)S(1)}, f32[8,64]{1,0:T(8,128)S(1)}, u32[]{:S(2)}, u32[]{:S(2)}) %collective-permute-start.11) | collective-permute-done | bytes 2080 | tf_op jit(solution)/shard_map/ppermute | solution.py:224
  32.1 0.1 collective-permute-start.12
  32.2 3.5 %collective-permute-done.12 = f32[8,64]{1,0:T(8,128)S(1)} collective-permute-done((f32[8,64]{1,0:T(8,128)S(1)}, f32[8,64]{1,0:T(8,128)S(1)}, u32[]{:S(2)}, u32[]{:S(2)}) %collective-permute-start.12) | collective-permute-done | bytes 2080 | tf_op jit(solution)/shard_map/ppermute | solution.py:224
  35.7 2.3 %collective-permute-start.13 = (f32[8,64]{1,0:T(8,128)S(1)}, f32[8,64]{1,0:T(8,128)S(1)}, u32[]{:S(2)}, u32[]{:S(2)}) collective-permute-start(f32[8,64]{1,0:T(8,128)S(1)} %add.31), channel_id=1, source_target_pairs={{0,4},{1,5},{2,6},{3,7},{4,0},{5,1},{6,2},{7,3},{8,12},{9,13},{10,... | collective-permute-start | bytes 6152 | tf_op jit(solution)/shard_map/ppermute | solution.py:224
  38.0 2.2 %collective-permute-done.13 = f32[8,64]{1,0:T(8,128)S(1)} collective-permute-done((f32[8,64]{1,0:T(8,128)S(1)}, f32[8,64]{1,0:T(8,128)S(1)}, u32[]{:S(2)}, u32[]{:S(2)}) %collective-permute-start.13) | collective-permute-done | bytes 2080 | tf_op jit(solution)/shard_map/ppermute | solution.py:224
  40.2 0.5 %constant_dynamic-slice_fusion = f32[1,64]{1,0:T(1,128)} fusion(f32[8,64]{1,0:T(8,128)S(1)} %add.32, s32[]{:T(128)S(6)} %select_n.16), kind=kLoop, calls=%fused_computation.3 | loop fusion | bytes 516 | tf_op jit(solution)/shard_map/dynamic_slice | solution.py:268
  (8 shorter events, 0.0 us)
Async XLA Ops:
  0.0 0.7 %copy-start.2 = (s32[32,24]{0,1:T(8,128)S(1)}, s32[32,24]{0,1:T(8,128)}, u32[]{:S(2)}) copy-start(s32[32,24]{0,1:T(8,128)} %param.13) | copy-start | bytes 9220
  0.0 0.7 %copy-start.7 = (s32[32,1]{0,1:T(1,128)S(1)}, s32[32,1]{0,1:T(1,128)}, u32[]{:S(2)}) copy-start(s32[32,1]{0,1:T(1,128)} %param.15) | copy-start | bytes 388
  0.0 0.7 %copy-start.3 = (s32[4,180]{1,0:T(4,128)S(1)}, s32[4,180]{1,0:T(4,128)}, u32[]{:S(2)}) copy-start(s32[4,180]{1,0:T(4,128)} %clusters_ref.1) | copy-start | bytes 8644
  0.0 0.7 %copy-start.4 = (s32[32,3]{0,1:T(4,128)S(1)}, s32[32,3]{0,1:T(4,128)}, u32[]{:S(2)}) copy-start(s32[32,3]{0,1:T(4,128)} %param.12) | copy-start | bytes 1156
  0.0 0.7 %copy-start.5 = (s32[32,2]{0,1:T(2,128)S(1)}, s32[32,2]{0,1:T(2,128)}, u32[]{:S(2)}) copy-start(s32[32,2]{0,1:T(2,128)} %param.14) | copy-start | bytes 772
  0.0 0.7 %copy-start.6 = (s32[4]{0:T(128)S(1)}, s32[4]{0:T(128)}, u32[]{:S(2)}) copy-start(s32[4]{0:T(128)} %len_ref.1) | copy-start | bytes 52
  0.7 1.0 %copy-start = (f32[4,180,128]{2,0,1:T(4,128)S(1)}, f32[4,180,128]{2,0,1:T(4,128)}, u32[]{:S(2)}) copy-start(f32[4,180,128]{2,0,1:T(4,128)} %param.9) | copy-start | bytes 1105924
  1.7 4.2 %copy-start.1 = (f32[1,32,128]{2,1,0:T(8,128)S(1)}, f32[1,32,128]{2,1,0:T(8,128)}, u32[]{:S(2)}) copy-start(f32[1,32,128]{2,1,0:T(8,128)} %param.8) | copy-start | bytes 49156
  3.0 5.5 %collective-permute-start = (f32[40,128]{1,0:T(8,128)S(1)}, f32[40,128]{1,0:T(8,128)S(1)}, u32[]{:S(2)}, u32[]{:S(2)}) collective-permute-start(f32[40,128]{1,0:T(8,128)S(1)} %get-tuple-element.15.refs_0_.refs_4_), channel_id=1, source_target_pairs={{0,8},{1,9},{2,10},{3,11},{4,12},{5,13},{6,14},{7,15},{8,0},{9,1},... | collective-permute-start | bytes 61448 | tf_op jit(solution)/shard_map/ppermute | solution.py:224
  5.9 4.6 %collective-permute-start.2 = (f32[32,128]{1,0:T(8,128)S(1)}, f32[32,128]{1,0:T(8,128)S(1)}, u32[]{:S(2)}, u32[]{:S(2)}) collective-permute-start(f32[32,128]{1,0:T(8,128)S(1)} %bitcast.10), channel_id=1, source_target_pairs={{0,4},{1,5},{2,6},{3,7},{4,0},{5,1},{6,2},{7,3},{8,12},{9,13},{10,... | collective-permute-start | bytes 49160 | tf_op jit(solution)/shard_map/ppermute | solution.py:224
  8.5 13.3 %collective-permute-start.1 = (f32[720,128]{1,0:T(8,128)S(1)}, f32[720,128]{1,0:T(8,128)S(1)}, u32[]{:S(2)}, u32[]{:S(2)}) collective-permute-start(f32[720,128]{1,0:T(8,128)S(1)} %get-tuple-element.17.refs_0_), channel_id=1, source_target_pairs={{0,8},{1,9},{2,10},{3,11},{4,12},{5,13},{6,14},{7,15},{8,0},{9,1},... | collective-permute-start | bytes 1105928 | tf_op jit(solution)/shard_map/ppermute | solution.py:224
  9.7 2.4 %collective-permute-start.5 = (f32[80,128]{1,0:T(8,128)S(1)}, f32[80,128]{1,0:T(8,128)S(1)}, u32[]{:S(2)}, u32[]{:S(2)}) collective-permute-start(f32[80,128]{1,0:T(8,128)S(1)} %pad_maximum_fusion.1), channel_id=1, source_target_pairs={{0,1},{1,0},{2,3},{3,2},{4,5},{5,4},{6,7},{7,6},{8,9},{9,8},{10,11... | collective-permute-start | bytes 122888 | tf_op jit(solution)/shard_map/ppermute | solution.py:224
  10.6 4.6 %collective-permute-start.3 = (f32[64,128]{1,0:T(8,128)S(1)}, f32[64,128]{1,0:T(8,128)S(1)}, u32[]{:S(2)}, u32[]{:S(2)}) collective-permute-start(f32[64,128]{1,0:T(8,128)S(1)} %pad_maximum_fusion.2), channel_id=1, source_target_pairs={{0,2},{1,3},{2,0},{3,1},{4,6},{5,7},{6,4},{7,5},{8,10},{9,11},{10,... | collective-permute-start | bytes 98312 | tf_op jit(solution)/shard_map/ppermute | solution.py:224
  12.5 5.3 %collective-permute-start.6 = (f32[80,128]{1,0:T(8,128)S(1)}, f32[80,128]{1,0:T(8,128)S(1)}, u32[]{:S(2)}, u32[]{:S(2)}) collective-permute-start(f32[80,128]{1,0:T(8,128)S(1)} %shard_map.83), channel_id=1, source_target_pairs={{0,4},{1,5},{2,6},{3,7},{4,0},{5,1},{6,2},{7,3},{8,12},{9,13},{10,... | collective-permute-start | bytes 122888 | tf_op jit(solution)/shard_map/ppermute | solution.py:224
  15.2 6.6 %collective-permute-start.4 = (f32[128,128]{1,0:T(8,128)S(1)}, f32[128,128]{1,0:T(8,128)S(1)}, u32[]{:S(2)}, u32[]{:S(2)}) collective-permute-start(f32[128,128]{1,0:T(8,128)S(1)} %pad_maximum_fusion), channel_id=1, source_target_pairs={{0,16},{1,17},{2,18},{3,19},{4,20},{5,21},{6,22},{7,23},{8,24},{9,... | collective-permute-start | bytes 196616 | tf_op jit(solution)/shard_map/ppermute | solution.py:224
  17.8 4.0 %collective-permute-start.7 = (f32[80,128]{1,0:T(8,128)S(1)}, f32[80,128]{1,0:T(8,128)S(1)}, u32[]{:S(2)}, u32[]{:S(2)}) collective-permute-start(f32[80,128]{1,0:T(8,128)S(1)} %add.28), channel_id=1, source_target_pairs={{0,2},{1,3},{2,0},{3,1},{4,6},{5,7},{6,4},{7,5},{8,10},{9,11},{10,... | collective-permute-start | bytes 122888 | tf_op jit(solution)/shard_map/ppermute | solution.py:224
  21.8 4.6 %collective-permute-start.8 = (f32[720,128]{1,0:T(8,128)S(1)}, f32[720,128]{1,0:T(8,128)S(1)}, u32[]{:S(2)}, u32[]{:S(2)}) collective-permute-start(f32[720,128]{1,0:T(8,128)S(1)} %get-tuple-element.17.refs_0_), channel_id=1, source_target_pairs={{0,1},{1,0},{2,3},{3,2},{4,5},{5,4},{6,7},{7,6},{8,9},{9,8},{10,11... | collective-permute-start | bytes 1105928 | tf_op jit(solution)/shard_map/ppermute | solution.py:224
  21.9 4.5 %collective-permute-start.9 = (f32[720,128]{1,0:T(8,128)S(1)}, f32[720,128]{1,0:T(8,128)S(1)}, u32[]{:S(2)}, u32[]{:S(2)}) collective-permute-start(f32[720,128]{1,0:T(8,128)S(1)} %collective-permute-done.1.refs_1_), channel_id=1, source_target_pairs={{0,1},{1,0},{2,3},{3,2},{4,5},{5,4},{6,7},{7,6},{8,9},{9,8},{10,11... | collective-permute-start | bytes 1105928 | tf_op jit(solution)/shard_map/ppermute | solution.py:224
  22.4 4.0 %collective-permute-start.10 = (f32[80,128]{1,0:T(8,128)S(1)}, f32[80,128]{1,0:T(8,128)S(1)}, u32[]{:S(2)}, u32[]{:S(2)}) collective-permute-start(f32[80,128]{1,0:T(8,128)S(1)} %add.29.refs_11_), channel_id=1, source_target_pairs={{0,16},{1,17},{2,18},{3,19},{4,20},{5,21},{6,22},{7,23},{8,24},{9,... | collective-permute-start | bytes 122888 | tf_op jit(solution)/shard_map/ppermute | solution.py:224
  28.5 3.6 %collective-permute-start.11 = (f32[8,64]{1,0:T(8,128)S(1)}, f32[8,64]{1,0:T(8,128)S(1)}, u32[]{:S(2)}, u32[]{:S(2)}) collective-permute-start(f32[8,64]{1,0:T(8,128)S(1)} %shard_map.84), channel_id=1, source_target_pairs={{0,16},{1,17},{2,18},{3,19},{4,20},{5,21},{6,22},{7,23},{8,24},{9,... | collective-permute-start | bytes 6152 | tf_op jit(solution)/shard_map/ppermute | solution.py:224
  32.1 3.6 %collective-permute-start.12 = (f32[8,64]{1,0:T(8,128)S(1)}, f32[8,64]{1,0:T(8,128)S(1)}, u32[]{:S(2)}, u32[]{:S(2)}) collective-permute-start(f32[8,64]{1,0:T(8,128)S(1)} %add.30), channel_id=1, source_target_pairs={{0,2},{1,3},{2,0},{3,1},{4,6},{5,7},{6,4},{7,5},{8,10},{9,11},{10,... | collective-permute-start | bytes 6152 | tf_op jit(solution)/shard_map/ppermute | solution.py:224
  35.7 4.5 %collective-permute-start.13 = (f32[8,64]{1,0:T(8,128)S(1)}, f32[8,64]{1,0:T(8,128)S(1)}, u32[]{:S(2)}, u32[]{:S(2)}) collective-permute-start(f32[8,64]{1,0:T(8,128)S(1)} %add.31), channel_id=1, source_target_pairs={{0,4},{1,5},{2,6},{3,7},{4,0},{5,1},{6,2},{7,3},{8,12},{9,13},{10,... | collective-permute-start | bytes 6152 | tf_op jit(solution)/shard_map/ppermute | solution.py:224

commit v3 on v2

v3 whole, which is shorter than its diff:
```python
import functools

import jax
import jax.numpy as jnp
from jax import lax
from jax.experimental import pallas as pl
from jax.experimental.pallas import tpu as pltpu
from jax.sharding import PartitionSpec as P

DIM = 128
QL = 32
NCENT = 24
EXP = 10
CAP = 2
FB = 3
BETA = 0.5
AXES = ("query", "corpus")
ID_ROW = 31
CAND_ROW = 32
ASK_ROW = 40
HIGHEST = lax.Precision.HIGHEST


def iota(shape, axis):
    return lax.broadcasted_iota(jnp.int32, shape, axis)


def spread(index, masks):
    total = 0
    for k, mask in enumerate(masks):
        total = total | (((index >> k) & 1) * mask)
    return total


def gather_bits(device, masks):
    total = 0
    for k, mask in enumerate(masks):
        total = total | (jnp.where((device & mask) != 0, 1, 0) << k)
    return total


def pairs_kernel(queries_n, held, tokens, pos_ref, *refs):
    sources, (masked_ref, pay_ref) = refs[:7], refs[7:9]
    landed, sems = refs[9:16], refs[16]
    copies = [pltpu.make_async_copy(a, b, sems.at[k]) for k, (a, b) in enumerate(zip(sources, landed))]
    for copy in copies:
        copy.start()
    for copy in copies:
        copy.wait()
    len_ref, tiles_ref, clusters_ref, feedback_ref, ranks_ref, local_ref, count_ref = landed
    pos = pos_ref[0]
    per_tile = 8 // held
    row = iota((8, DIM), 0)
    limit = jnp.zeros((8, DIM), jnp.int32)
    for p in range(held):
        limit = jnp.where(row % held == p, len_ref[p], limit)
    first = tiles_ref[0:held, :]
    first = jnp.concatenate([first] * per_tile, axis=0)
    groups = tokens * held // 8
    token = iota((groups, 8, DIM), 0) * per_tile + (iota((groups, 8, DIM), 1) // held)
    tiles = tiles_ref[...].reshape(groups, 8, DIM)
    masked_ref[...] = jnp.where(token < limit[None], tiles, first[None]).reshape(groups * 8, DIM)

    nearby = feedback_ref[...] - pos * held
    number = (iota(nearby.shape, 0) * queries_n + iota(nearby.shape, 1)) * held + nearby
    far = 1e9
    key = jnp.where((nearby >= 0) & (nearby < held), number.astype(jnp.float32), far)
    ranks = ranks_ref[...].astype(jnp.float32)
    lane = iota(ranks.shape, 1)
    pay_ref[:ASK_ROW, :] = jnp.zeros((ASK_ROW, DIM), jnp.float32)
    ids = jnp.zeros((1, DIM), jnp.float32)
    slot = iota((1, DIM), 1) // EXP
    kinds = iota((NCENT, tokens), 0)
    times = iota((EXP, tokens), 1)
    wanted = iota((EXP, tokens), 0).astype(jnp.float32)
    for s in range(FB):
        best = jnp.min(key)
        key = jnp.where(key > best, key, far)
        whole = best.astype(jnp.int32)
        p = whole % held
        q = (whole // held) % queries_n
        ids = jnp.where(slot == s, q.astype(jnp.float32), ids)
        rank = jnp.sum(jnp.where(lane == q, ranks, 0.0), axis=1, keepdims=True)
        kind = clusters_ref[pl.ds(p, 1), :]
        of_token = jnp.sum(jnp.where(kind == kinds, rank, 0.0), axis=0, keepdims=True)
        chosen = jnp.where((of_token == wanted) & (times < len_ref[p]), 1.0, 0.0)
        passage = tiles_ref[pl.ds(p, tokens, stride=held), :]
        pay_ref[s * EXP:(s + 1) * EXP, :] = jnp.dot(
            chosen, passage, precision=HIGHEST, preferred_element_type=jnp.float32)
    pay_ref[ID_ROW:ID_ROW + 1, :] = ids
    for c, at in enumerate(range(0, queries_n, DIM)):
        width = min(DIM, queries_n - at)
        top = CAND_ROW + (CAP + 1) * c
        pay_ref[top:top + CAP, 0:width] = local_ref[:, at:at + width].astype(jnp.float32)
        pay_ref[top + CAP:top + CAP + 1, 0:width] = count_ref[:, at:at + width].astype(jnp.float32)


def combine_kernel(side, outer, pos_ref, *refs):
    *pays, keep_ref, send_ref = refs
    pos = pos_ref[0]
    half = (1 << len(outer)) * EXP
    rows = 2 * half
    row = iota((rows, DIM), 0)
    owner = ((pos ^ ((row // half) * side)) & (1 | side)) | spread(row % half // EXP, outer)
    owner = owner.astype(jnp.float32)
    places = [(pay, 0) for pay in pays]
    total = jnp.zeros((rows, DIM), jnp.float32)
    for group in range(0, len(places), 8):
        some = places[group:group + 8]
        ids = jnp.concatenate([pay[at + ID_ROW:at + ID_ROW + 1, :CAND_ROW] for pay, at in some], axis=1)
        col = iota((rows, ids.shape[1]), 1) % CAND_ROW
        pick = (col % EXP == row[:, :1] % EXP) & (col < FB * EXP) & (ids == owner[:, :1])
        pick = jnp.where(pick, 1.0, 0.0).astype(jnp.bfloat16)
        block = jnp.concatenate([pay[at:at + CAND_ROW, :] for pay, at in some], axis=0)
        high, low = split(block)
        rest = (block - high.astype(jnp.float32) - low.astype(jnp.float32)).astype(jnp.bfloat16)
        for piece in (rest, low, high):
            total += jnp.dot(pick, piece, preferred_element_type=jnp.float32)
    for ref, sums in ((keep_ref, total[:rows // 2]), (send_ref, total[rows // 2:])):
        ref[:rows // 2, :] = sums
        ref[rows // 2:rows // 2 + 8, :] = pays[0][CAND_ROW:ASK_ROW, :]
        ref[rows // 2 + 8:, :] = pays[-1][CAND_ROW:ASK_ROW, :]


def nt_dot(a, b, precision=None):
    return lax.dot_general(a, b, (((1,), (1,)), ((), ())), precision=precision, preferred_element_type=jnp.float32)


def split(x):
    high = x.astype(jnp.bfloat16)
    return high, (x - high.astype(jnp.float32)).astype(jnp.bfloat16)


def score_kernel(side, outer, asking, queries_n, held, n_tiles, n_asks, pos_ref, *refs):
    tile_refs, ask_refs = refs[:n_tiles], refs[n_tiles:n_tiles + n_asks]
    keep_ref, from_side_ref, mine_ref, theirs_ref, out_ref = refs[n_tiles + n_asks:]
    pos = pos_ref[0]
    n_in, n_out = 4, 1 << len(outer)
    me_out = gather_bits(pos, outer)
    half = n_out * EXP
    sums = mine_ref[...] + theirs_ref[...]
    scale = lax.rsqrt(jnp.mean(sums * sums, axis=1, keepdims=True) + 1e-05)
    order = (iota((half, 1), 0) % EXP).astype(jnp.float32)
    weight = BETA * jnp.log((NCENT + 1.0) / (order + 1.0))
    extra = sums * (scale * weight)
    expanded = jnp.concatenate([ask[...] for ask in ask_refs] + [extra], axis=0)
    total = expanded.shape[0]
    lefts = []
    for ref in tile_refs:
        high, low = split(ref[...])
        lefts.append((high, jnp.concatenate([high, low], axis=1)))
    parts = [[] for _ in lefts]
    for at in range(0, total, 256):
        high, low = split(expanded[at:at + 256])
        twice = jnp.concatenate([high, high], axis=1)
        for i, (left, wide) in enumerate(lefts):
            similar = nt_dot(wide, twice) + nt_dot(left, low)
            groups = similar.shape[0] // 8
            parts[i].append(jnp.max(similar.reshape(groups, 8, similar.shape[1]), axis=0))
    largest = []
    for part in parts:
        top = jnp.concatenate(part, axis=1)
        step = held
        while step < 8:
            top = jnp.maximum(top, pltpu.roll(top, step, 0))
            step *= 2
        largest.append(top)
    largest = jnp.concatenate(largest, axis=0)
    col = iota((n_out, total), 1)
    of_ask = gather_bits(spread(col // QL, asking), outer) ^ me_out
    of_col = jnp.where(col < n_out * QL, of_ask, (col - n_out * QL) // EXP)
    member = jnp.where(of_col == iota((n_out, total), 0), 1.0 / QL, 0.0)
    values = nt_dot(member, largest, HIGHEST)

    cands = jnp.concatenate([keep_ref[half:, :], from_side_ref[half:, :]], axis=0)
    own = (pos & ~sum(outer)) | spread(iota((n_out, DIM), 0), outer)
    slots = out_ref.shape[1]
    device = iota((n_in * 8, slots), 1) // CAP
    which = iota((n_in * 8, slots), 1) % CAP
    entry = iota((n_in * 8, slots), 0)

    def at_device(steps):
        place = jnp.zeros((n_in * 8, slots), jnp.int32)
        for i, away in enumerate(steps):
            place = jnp.where(entry // 8 == i, pos ^ away, place)
        return place == device

    same = at_device([0, 1, side, side | 1])
    local = jnp.zeros((n_out, slots), jnp.float32)
    count = jnp.zeros((n_out, slots), jnp.float32)
    for c, at in enumerate(range(0, queries_n, DIM)):
        found = nt_dot(jnp.where(own - at == iota((n_out, DIM), 1), 1.0, 0.0), cands, HIGHEST)
        top = (CAP + 1) * c
        pick = jnp.where(same & (entry % 8 == top + which), 1.0, 0.0)
        local += jnp.dot(found, pick, precision=HIGHEST, preferred_element_type=jnp.float32)
        pick = jnp.where(same & (entry % 8 == top + CAP), 1.0, 0.0)
        count += jnp.dot(found, pick, precision=HIGHEST, preferred_element_type=jnp.float32)
    same = at_device([0, side, 1, side | 1])
    result = jnp.zeros((n_out, slots), jnp.float32)
    for p in range(held):
        pick = jnp.where(same & (entry % 8 == p), 1.0, 0.0)
        value = jnp.dot(values, pick, precision=HIGHEST, preferred_element_type=jnp.float32)
        result = jnp.where(local == float(p), value, result)
    out_ref[...] = jnp.where((iota((n_out, slots), 1) % CAP).astype(jnp.float32) < count, result, 0.0)


def call(kernel, outs, *args, copied=False):
    smem = pl.BlockSpec(memory_space=pltpu.SMEM)
    vmem = pl.BlockSpec(memory_space=pltpu.VMEM)
    specs = [smem if a.ndim == 1 else vmem for a in args]
    scratch = []
    if copied:
        specs[1:] = [pl.BlockSpec(memory_space=pltpu.HBM)] * (len(args) - 1)
        scratch = [(pltpu.SMEM if a.ndim == 1 else pltpu.VMEM)(a.shape, a.dtype) for a in args[1:]]
        scratch += [pltpu.SemaphoreType.DMA((len(args) - 1,))]
        args = args[:1] + tuple(pltpu.with_memory_space_constraint(a, pltpu.HBM) for a in args[1:])
    return pl.pallas_call(
        kernel,
        out_shape=[pltpu.VMEM(o.shape, o.dtype) for o in outs] if len(outs) > 1 else outs[0],
        in_specs=specs,
        out_specs=[vmem] * len(outs) if len(outs) > 1 else vmem,
        scratch_shapes=scratch,
        compiler_params=pltpu.CompilerParams(vmem_limit_bytes=24 * 1024 * 1024),
    )(*args)


def body(queries, passages, clusters, lengths, feedback, ranks, cand_local, cand_count):
    held, tokens, _ = passages.shape
    queries_n = feedback.shape[0]
    n_corpus = lax.axis_size("corpus")
    devices = lax.axis_size("query") * n_corpus
    side, last = n_corpus, 2 * n_corpus
    masks = [1 << k for k in range(devices.bit_length() - 1)]
    outer = [m for m in reversed(masks) if 1 < m < n_corpus] + [m for m in masks if m >= last]
    asking = outer[1:] + outer[:1]
    n_out = 1 << len(outer)
    pos = lax.axis_index(AXES).astype(jnp.int32).reshape(1)

    def swap(x, mask):
        return lax.ppermute(x, AXES, [(i, i ^ mask) for i in range(devices)])

    def struct(rows, cols=DIM):
        return jax.ShapeDtypeStruct((rows, cols), jnp.float32)

    chunks = -(-queries_n // DIM)
    pay_rows = ASK_ROW
    assert (CAP + 1) * chunks <= 8 and queries.shape[0] == 1 and 8 % held == 0
    tiles = jnp.transpose(passages, (1, 0, 2)).reshape(tokens * held, DIM)
    masked, pay = call(
        functools.partial(pairs_kernel, queries_n, held, tokens),
        [struct(tokens * held), struct(pay_rows)],
        pos, lengths, tiles, clusters, feedback.T, ranks.T, cand_local.T, cand_count.T, copied=True,
    )
    def together(*xs):
        return lax.optimization_barrier(xs)

    def joined(xs):
        return xs[0] if len(xs) == 1 else jnp.concatenate(xs, axis=0)

    beside = swap(pay, 1)
    half = n_out * EXP
    keep, send = call(functools.partial(combine_kernel, side, outer), [struct(half + 16)] * 2, pos, pay, beside)
    from_side = swap(send, side)
    sums = keep[:half] + from_side[:half]
    asks = [queries[0]]
    for mask in asking:
        asks = asks + [swap(joined(asks), mask)]
    masked, _ = lax.optimization_barrier((masked, asks[1]))
    far = swap(masked, side)
    for mask in outer[:-1]:
        sums = sums + swap(sums, mask)
    far, sums, asks = lax.optimization_barrier((far, sums, asks))
    came = swap(sums, outer[-1])
    tiles = [masked, far]
    tiles = tiles + [swap(t, 1) for t in tiles]
    table = call(
        functools.partial(score_kernel, side, outer, asking, queries_n, held, len(tiles), len(asks)),
        [struct(n_out, devices * CAP)],
        pos, *tiles, *asks, keep, from_side, sums, came,
    )
    for mask in reversed(outer):
        table = table + swap(table, mask)
    mine = sum(jnp.where((pos[0] & mask) != 0, 1 << k, 0) for k, mask in enumerate(outer))
    return lax.dynamic_slice(table, (mine, 0), (1, devices * CAP))


def solution(mesh):
    in_specs = (
        P(AXES, None, None),
        P(AXES, None, None),
        P(AXES, None),
        P(AXES),
        P(),
        P(),
        P(None, AXES),
        P(None, AXES),
    )
    return jax.shard_map(body, mesh=mesh, in_specs=in_specs, out_specs=P(AXES, None), check_vma=False)
```

time: 40.9 us -> 38.1 us (0.932)
  local copies, waits for them, and re-layouts: 2.24 us -> 0.52 us
  waiting for transfers between devices: 15.9 us -> 14.5 us
  Pallas kernels: 3.64 us -> 4.13 us
    unnamed x16 -> x2, local copies, waits for them, and re-layouts: 1.72 us -> 0.01 us
    ppermute x14, waiting for transfers between devices: 15.9 us -> 14.5 us  [swap(): return lax.ppermute(x, AXES, [(i, i ^ mask) for i in range(devices)])]
    pallas_call x3, Pallas kernels: 3.64 us -> 4.13 us  [call(): pl.pallas_call(kernel, out_shape=[pltpu.VMEM(o.shape, o.dtype) for o in o...]
  transfers between devices with their start and end apart: 14 -> 14, of which waited for: 7 -> 6; matrix products, arithmetic and copies ran while one was open for 0% -> 0% of each run, Pallas kernels for 1% -> 1%
where the time goes in v3:
time: 38.1 us; the launch traced here: 37.9 us
  starting transfers between devices  18.6 us (49%)
  waiting for transfers between devices  14.5 us (38%)
  Pallas kernels  4.13 us (11%)
  local copies, waits for them, and re-layouts  0.52 us (1%)
    ppermute x14, starting transfers between devices, swap(): return lax.ppermute(x, AXES, [(i, i ^ mask) for i in range(devices)])  18.6 us
    ppermute x14, waiting for transfers between devices, swap(): return lax.ppermute(x, AXES, [(i, i ^ mask) for i in range(devices)])  14.5 us
    pallas_call x3, Pallas kernels, call(): pl.pallas_call(kernel, out_shape=[pltpu.VMEM(o.shape, o.dtype) for o in o...  4.13 us
  transfers between devices with their start and end apart: 14, of which 6 were waited for; matrix products, arithmetic and copies ran while one was open for 0% of the time, Pallas kernels for 1%

profile of v3, /device:TPU:0, one launch (start us, length us, event | category | flops | bytes accessed | tf_op | source)
XLA Modules:
  0.0 37.9 jit_solution(13278387216926724720)
XLA Ops:
  0.0 0.0 copy-start
  0.0 1.8 %shard_map.82 = (f32[720,128]{1,0:T(8,128)S(1)}, f32[40,128]{1,0:T(8,128)S(1)}) custom-call(s32[1]{0:T(128)} %bitcast.pos_ref, s32[4]{0:T(128)} %refs_0_.1, f32[720,128]{1,0:T(8,128)} %bitcast.13, s32[4,180]{1,0:T(4,128)} %refs_2_.1, s32[3,32]{1,0:T(4,128)} %bitcast.15, s32[24,32]{1,0:T(8,128)} %bitcast.14, s32[2,32]{1,0:T(2,128)} %bitcast.16, s32[1,32]{1,0:T(1,128)} %bitcast.17), custom_call_target="tpu_custom_call" | custom-call | tf_op jit(solution)/shard_map/pallas_call | solution.py:217
  1.8 0.5 %collective-permute-start.2 = (f32[40,128]{1,0:T(8,128)S(1)}, f32[40,128]{1,0:T(8,128)S(1)}, u32[]{:S(2)}, u32[]{:S(2)}) collective-permute-start(f32[40,128]{1,0:T(8,128)S(1)} %get-tuple-element.18.refs_0_), channel_id=1, source_target_pairs={{0,1},{1,0},{2,3},{3,2},{4,5},{5,4},{6,7},{7,6},{8,9},{9,8},{10,11... | collective-permute-start | bytes 61448 | tf_op jit(solution)/shard_map/ppermute | solution.py:240
  2.3 0.0 copy-done
  2.3 2.7 %collective-permute-start = (f32[32,128]{1,0:T(8,128)S(1)}, f32[32,128]{1,0:T(8,128)S(1)}, u32[]{:S(2)}, u32[]{:S(2)}) collective-permute-start(f32[32,128]{1,0:T(8,128)S(1)} %bitcast.9), channel_id=1, source_target_pairs={{0,2},{1,3},{2,0},{3,1},{4,6},{5,7},{6,4},{7,5},{8,10},{9,11},{10,... | collective-permute-start | bytes 49160 | tf_op jit(solution)/shard_map/ppermute | solution.py:240
  5.0 0.0 collective-permute-done.2.refs_1_
  5.0 0.3 shard_map.83
  5.3 1.6 %collective-permute-start.3 = (f32[96,128]{1,0:T(8,128)S(1)}, f32[96,128]{1,0:T(8,128)S(1)}, u32[]{:S(2)}, u32[]{:S(2)}) collective-permute-start(f32[96,128]{1,0:T(8,128)S(1)} %get-tuple-element.20), channel_id=1, source_target_pairs={{0,8},{1,9},{2,10},{3,11},{4,12},{5,13},{6,14},{7,15},{8,0},{9,1},... | collective-permute-start | bytes 147464 | tf_op jit(solution)/shard_map/ppermute | solution.py:240
  6.8 0.0 collective-permute-done.refs_5_
  6.9 1.8 %collective-permute-start.6 = (f32[64,128]{1,0:T(8,128)S(1)}, f32[64,128]{1,0:T(8,128)S(1)}, u32[]{:S(2)}, u32[]{:S(2)}) collective-permute-start(f32[64,128]{1,0:T(8,128)S(1)} %pad_maximum_fusion.1), channel_id=1, source_target_pairs={{0,16},{1,17},{2,18},{3,19},{4,20},{5,21},{6,22},{7,23},{8,24},{9,... | collective-permute-start | bytes 98312 | tf_op jit(solution)/shard_map/ppermute | solution.py:240
  8.7 1.5 %collective-permute-start.1 = (f32[720,128]{1,0:T(8,128)S(1)}, f32[720,128]{1,0:T(8,128)S(1)}, u32[]{:S(2)}, u32[]{:S(2)}) collective-permute-start(f32[720,128]{1,0:T(8,128)S(1)} %get-tuple-element.17.refs_0_), channel_id=1, source_target_pairs={{0,8},{1,9},{2,10},{3,11},{4,12},{5,13},{6,14},{7,15},{8,0},{9,1},... | collective-permute-start | bytes 1105928 | tf_op jit(solution)/shard_map/ppermute | solution.py:240
  10.2 0.0 collective-permute-done.3.refs_9_
  10.2 2.7 %collective-permute-start.4 = (f32[80,128]{1,0:T(8,128)S(1)}, f32[80,128]{1,0:T(8,128)S(1)}, u32[]{:S(2)}, u32[]{:S(2)}) collective-permute-start(f32[80,128]{1,0:T(8,128)S(1)} %slice_add_fusion), channel_id=1, source_target_pairs={{0,4},{1,5},{2,6},{3,7},{4,0},{5,1},{6,2},{7,3},{8,12},{9,13},{10,... | collective-permute-start | bytes 122888 | tf_op jit(solution)/shard_map/ppermute | solution.py:240
  12.8 0.0 collective-permute-done.6.refs_6_
  12.8 0.8 %collective-permute-start.7 = (f32[128,128]{1,0:T(8,128)S(1)}, f32[128,128]{1,0:T(8,128)S(1)}, u32[]{:S(2)}, u32[]{:S(2)}) collective-permute-start(f32[128,128]{1,0:T(8,128)S(1)} %pad_maximum_fusion), channel_id=1, source_target_pairs={{0,4},{1,5},{2,6},{3,7},{4,0},{5,1},{6,2},{7,3},{8,12},{9,13},{10,... | collective-permute-start | bytes 196616 | tf_op jit(solution)/shard_map/ppermute | solution.py:240
  13.7 1.8 %collective-permute-done.4 = f32[80,128]{1,0:T(8,128)S(1)} collective-permute-done((f32[80,128]{1,0:T(8,128)S(1)}, f32[80,128]{1,0:T(8,128)S(1)}, u32[]{:S(2)}, u32[]{:S(2)}) %collective-permute-start.4) | collective-permute-done | bytes 40992 | tf_op jit(solution)/shard_map/ppermute | solution.py:240
  15.4 1.7 %collective-permute-start.5 = (f32[80,128]{1,0:T(8,128)S(1)}, f32[80,128]{1,0:T(8,128)S(1)}, u32[]{:S(2)}, u32[]{:S(2)}) collective-permute-start(f32[80,128]{1,0:T(8,128)S(1)} %add.32), channel_id=1, source_target_pairs={{0,2},{1,3},{2,0},{3,1},{4,6},{5,7},{6,4},{7,5},{8,10},{9,11},{10,... | collective-permute-start | bytes 122888 | tf_op jit(solution)/shard_map/ppermute | solution.py:240
  17.1 0.0 collective-permute-start.8
  17.1 2.3 %collective-permute-done.5 = f32[80,128]{1,0:T(8,128)S(1)} collective-permute-done((f32[80,128]{1,0:T(8,128)S(1)}, f32[80,128]{1,0:T(8,128)S(1)}, u32[]{:S(2)}, u32[]{:S(2)}) %collective-permute-start.5) | collective-permute-done | bytes 40992 | tf_op jit(solution)/shard_map/ppermute | solution.py:240
  19.4 0.0 collective-permute-done.7.refs_7_
  19.4 0.0 collective-permute-done.1.refs_1_
  19.5 0.1 collective-permute-start.9
  19.5 0.6 %collective-permute-start.10 = (f32[80,128]{1,0:T(8,128)S(1)}, f32[80,128]{1,0:T(8,128)S(1)}, u32[]{:S(2)}, u32[]{:S(2)}) collective-permute-start(f32[80,128]{1,0:T(8,128)S(1)} %add.33.refs_10_), channel_id=1, source_target_pairs={{0,16},{1,17},{2,18},{3,19},{4,20},{5,21},{6,22},{7,23},{8,24},{9,... | collective-permute-start | bytes 122888 | tf_op jit(solution)/shard_map/ppermute | solution.py:240
  20.1 0.0 collective-permute-done.8.refs_2_
  20.1 3.5 %collective-permute-done.10.refs_11_ = f32[80,128]{1,0:T(8,128)S(1)} collective-permute-done((f32[80,128]{1,0:T(8,128)S(1)}, f32[80,128]{1,0:T(8,128)S(1)}, u32[]{:S(2)}, u32[]{:S(2)}) %collective-permute-start.10) | collective-permute-done | bytes 40992 | tf_op jit(solution)/shard_map/ppermute | solution.py:240
  23.6 0.0 collective-permute-done.9.refs_3_
  23.6 2.0 %shard_map.84 = f32[8,64]{1,0:T(8,128)S(1)} custom-call(s32[1]{0:T(128)} %bitcast.pos_ref, f32[720,128]{1,0:T(8,128)S(1)} %get-tuple-element.17.refs_0_, f32[720,128]{1,0:T(8,128)S(1)} %collective-permute-done.1.refs_1_, f32[720,128]{1,0:T(8,128)S(1)} %collective-permute-done.8.refs_2_, f32[720,128]{1,0:T(8,128)S(1)} %collective-permute-done.9.refs_3_, ...), custom_call_target="tpu_custom_call" | custom-call | tf_op jit(solution)/shard_map/pallas_call | solution.py:217
  25.6 0.6 %collective-permute-start.11 = (f32[8,64]{1,0:T(8,128)S(1)}, f32[8,64]{1,0:T(8,128)S(1)}, u32[]{:S(2)}, u32[]{:S(2)}) collective-permute-start(f32[8,64]{1,0:T(8,128)S(1)} %shard_map.84), channel_id=1, source_target_pairs={{0,16},{1,17},{2,18},{3,19},{4,20},{5,21},{6,22},{7,23},{8,24},{9,... | collective-permute-start | bytes 6152 | tf_op jit(solution)/shard_map/ppermute | solution.py:240
  26.2 3.0 %collective-permute-done.11 = f32[8,64]{1,0:T(8,128)S(1)} collective-permute-done((f32[8,64]{1,0:T(8,128)S(1)}, f32[8,64]{1,0:T(8,128)S(1)}, u32[]{:S(2)}, u32[]{:S(2)}) %collective-permute-start.11) | collective-permute-done | bytes 2080 | tf_op jit(solution)/shard_map/ppermute | solution.py:240
  29.3 1.7 %collective-permute-start.12 = (f32[8,64]{1,0:T(8,128)S(1)}, f32[8,64]{1,0:T(8,128)S(1)}, u32[]{:S(2)}, u32[]{:S(2)}) collective-permute-start(f32[8,64]{1,0:T(8,128)S(1)} %add.34), channel_id=1, source_target_pairs={{0,2},{1,3},{2,0},{3,1},{4,6},{5,7},{6,4},{7,5},{8,10},{9,11},{10,... | collective-permute-start | bytes 6152 | tf_op jit(solution)/shard_map/ppermute | solution.py:240
  31.0 1.9 %collective-permute-done.12 = f32[8,64]{1,0:T(8,128)S(1)} collective-permute-done((f32[8,64]{1,0:T(8,128)S(1)}, f32[8,64]{1,0:T(8,128)S(1)}, u32[]{:S(2)}, u32[]{:S(2)}) %collective-permute-start.12) | collective-permute-done | bytes 2080 | tf_op jit(solution)/shard_map/ppermute | solution.py:240
  32.9 2.5 %collective-permute-start.13 = (f32[8,64]{1,0:T(8,128)S(1)}, f32[8,64]{1,0:T(8,128)S(1)}, u32[]{:S(2)}, u32[]{:S(2)}) collective-permute-start(f32[8,64]{1,0:T(8,128)S(1)} %add.35), channel_id=1, source_target_pairs={{0,4},{1,5},{2,6},{3,7},{4,0},{5,1},{6,2},{7,3},{8,12},{9,13},{10,... | collective-permute-start | bytes 6152 | tf_op jit(solution)/shard_map/ppermute | solution.py:240
  35.4 2.0 %collective-permute-done.13 = f32[8,64]{1,0:T(8,128)S(1)} collective-permute-done((f32[8,64]{1,0:T(8,128)S(1)}, f32[8,64]{1,0:T(8,128)S(1)}, u32[]{:S(2)}, u32[]{:S(2)}) %collective-permute-start.13) | collective-permute-done | bytes 2080 | tf_op jit(solution)/shard_map/ppermute | solution.py:240
  37.4 0.5 %constant_dynamic-slice_fusion = f32[1,64]{1,0:T(1,128)} fusion(f32[8,64]{1,0:T(8,128)S(1)} %add.36, s32[]{:T(128)S(6)} %select_n.16), kind=kLoop, calls=%fused_computation.3 | loop fusion | bytes 516 | tf_op jit(solution)/shard_map/dynamic_slice | solution.py:284
  (8 shorter events, 0.0 us)
Async XLA Ops:
  0.0 2.3 %copy-start = (f32[1,32,128]{2,1,0:T(8,128)S(1)}, f32[1,32,128]{2,1,0:T(8,128)}, u32[]{:S(2)}) copy-start(f32[1,32,128]{2,1,0:T(8,128)} %param.8) | copy-start | bytes 49156
  1.8 3.2 %collective-permute-start.2 = (f32[40,128]{1,0:T(8,128)S(1)}, f32[40,128]{1,0:T(8,128)S(1)}, u32[]{:S(2)}, u32[]{:S(2)}) collective-permute-start(f32[40,128]{1,0:T(8,128)S(1)} %get-tuple-element.18.refs_0_), channel_id=1, source_target_pairs={{0,1},{1,0},{2,3},{3,2},{4,5},{5,4},{6,7},{7,6},{8,9},{9,8},{10,11... | collective-permute-start | bytes 61448 | tf_op jit(solution)/shard_map/ppermute | solution.py:240
  2.3 4.5 %collective-permute-start = (f32[32,128]{1,0:T(8,128)S(1)}, f32[32,128]{1,0:T(8,128)S(1)}, u32[]{:S(2)}, u32[]{:S(2)}) collective-permute-start(f32[32,128]{1,0:T(8,128)S(1)} %bitcast.9), channel_id=1, source_target_pairs={{0,2},{1,3},{2,0},{3,1},{4,6},{5,7},{6,4},{7,5},{8,10},{9,11},{10,... | collective-permute-start | bytes 49160 | tf_op jit(solution)/shard_map/ppermute | solution.py:240
  5.3 4.9 %collective-permute-start.3 = (f32[96,128]{1,0:T(8,128)S(1)}, f32[96,128]{1,0:T(8,128)S(1)}, u32[]{:S(2)}, u32[]{:S(2)}) collective-permute-start(f32[96,128]{1,0:T(8,128)S(1)} %get-tuple-element.20), channel_id=1, source_target_pairs={{0,8},{1,9},{2,10},{3,11},{4,12},{5,13},{6,14},{7,15},{8,0},{9,1},... | collective-permute-start | bytes 147464 | tf_op jit(solution)/shard_map/ppermute | solution.py:240
  6.9 6.0 %collective-permute-start.6 = (f32[64,128]{1,0:T(8,128)S(1)}, f32[64,128]{1,0:T(8,128)S(1)}, u32[]{:S(2)}, u32[]{:S(2)}) collective-permute-start(f32[64,128]{1,0:T(8,128)S(1)} %pad_maximum_fusion.1), channel_id=1, source_target_pairs={{0,16},{1,17},{2,18},{3,19},{4,20},{5,21},{6,22},{7,23},{8,24},{9,... | collective-permute-start | bytes 98312 | tf_op jit(solution)/shard_map/ppermute | solution.py:240
  8.7 10.8 %collective-permute-start.1 = (f32[720,128]{1,0:T(8,128)S(1)}, f32[720,128]{1,0:T(8,128)S(1)}, u32[]{:S(2)}, u32[]{:S(2)}) collective-permute-start(f32[720,128]{1,0:T(8,128)S(1)} %get-tuple-element.17.refs_0_), channel_id=1, source_target_pairs={{0,8},{1,9},{2,10},{3,11},{4,12},{5,13},{6,14},{7,15},{8,0},{9,1},... | collective-permute-start | bytes 1105928 | tf_op jit(solution)/shard_map/ppermute | solution.py:240
  10.2 5.3 %collective-permute-start.4 = (f32[80,128]{1,0:T(8,128)S(1)}, f32[80,128]{1,0:T(8,128)S(1)}, u32[]{:S(2)}, u32[]{:S(2)}) collective-permute-start(f32[80,128]{1,0:T(8,128)S(1)} %slice_add_fusion), channel_id=1, source_target_pairs={{0,4},{1,5},{2,6},{3,7},{4,0},{5,1},{6,2},{7,3},{8,12},{9,13},{10,... | collective-permute-start | bytes 122888 | tf_op jit(solution)/shard_map/ppermute | solution.py:240
  12.8 6.6 %collective-permute-start.7 = (f32[128,128]{1,0:T(8,128)S(1)}, f32[128,128]{1,0:T(8,128)S(1)}, u32[]{:S(2)}, u32[]{:S(2)}) collective-permute-start(f32[128,128]{1,0:T(8,128)S(1)} %pad_maximum_fusion), channel_id=1, source_target_pairs={{0,4},{1,5},{2,6},{3,7},{4,0},{5,1},{6,2},{7,3},{8,12},{9,13},{10,... | collective-permute-start | bytes 196616 | tf_op jit(solution)/shard_map/ppermute | solution.py:240
  15.4 4.0 %collective-permute-start.5 = (f32[80,128]{1,0:T(8,128)S(1)}, f32[80,128]{1,0:T(8,128)S(1)}, u32[]{:S(2)}, u32[]{:S(2)}) collective-permute-start(f32[80,128]{1,0:T(8,128)S(1)} %add.32), channel_id=1, source_target_pairs={{0,2},{1,3},{2,0},{3,1},{4,6},{5,7},{6,4},{7,5},{8,10},{9,11},{10,... | collective-permute-start | bytes 122888 | tf_op jit(solution)/shard_map/ppermute | solution.py:240
  17.1 3.0 %collective-permute-start.8 = (f32[720,128]{1,0:T(8,128)S(1)}, f32[720,128]{1,0:T(8,128)S(1)}, u32[]{:S(2)}, u32[]{:S(2)}) collective-permute-start(f32[720,128]{1,0:T(8,128)S(1)} %get-tuple-element.17.refs_0_), channel_id=1, source_target_pairs={{0,1},{1,0},{2,3},{3,2},{4,5},{5,4},{6,7},{7,6},{8,9},{9,8},{10,11... | collective-permute-start | bytes 1105928 | tf_op jit(solution)/shard_map/ppermute | solution.py:240
  19.5 4.1 %collective-permute-start.9 = (f32[720,128]{1,0:T(8,128)S(1)}, f32[720,128]{1,0:T(8,128)S(1)}, u32[]{:S(2)}, u32[]{:S(2)}) collective-permute-start(f32[720,128]{1,0:T(8,128)S(1)} %collective-permute-done.1.refs_1_), channel_id=1, source_target_pairs={{0,1},{1,0},{2,3},{3,2},{4,5},{5,4},{6,7},{7,6},{8,9},{9,8},{10,11... | collective-permute-start | bytes 1105928 | tf_op jit(solution)/shard_map/ppermute | solution.py:240
  19.5 4.1 %collective-permute-start.10 = (f32[80,128]{1,0:T(8,128)S(1)}, f32[80,128]{1,0:T(8,128)S(1)}, u32[]{:S(2)}, u32[]{:S(2)}) collective-permute-start(f32[80,128]{1,0:T(8,128)S(1)} %add.33.refs_10_), channel_id=1, source_target_pairs={{0,16},{1,17},{2,18},{3,19},{4,20},{5,21},{6,22},{7,23},{8,24},{9,... | collective-permute-start | bytes 122888 | tf_op jit(solution)/shard_map/ppermute | solution.py:240
  25.6 3.6 %collective-permute-start.11 = (f32[8,64]{1,0:T(8,128)S(1)}, f32[8,64]{1,0:T(8,128)S(1)}, u32[]{:S(2)}, u32[]{:S(2)}) collective-permute-start(f32[8,64]{1,0:T(8,128)S(1)} %shard_map.84), channel_id=1, source_target_pairs={{0,16},{1,17},{2,18},{3,19},{4,20},{5,21},{6,22},{7,23},{8,24},{9,... | collective-permute-start | bytes 6152 | tf_op jit(solution)/shard_map/ppermute | solution.py:240
  29.3 3.6 %collective-permute-start.12 = (f32[8,64]{1,0:T(8,128)S(1)}, f32[8,64]{1,0:T(8,128)S(1)}, u32[]{:S(2)}, u32[]{:S(2)}) collective-permute-start(f32[8,64]{1,0:T(8,128)S(1)} %add.34), channel_id=1, source_target_pairs={{0,2},{1,3},{2,0},{3,1},{4,6},{5,7},{6,4},{7,5},{8,10},{9,11},{10,... | collective-permute-start | bytes 6152 | tf_op jit(solution)/shard_map/ppermute | solution.py:240
  32.9 4.5 %collective-permute-start.13 = (f32[8,64]{1,0:T(8,128)S(1)}, f32[8,64]{1,0:T(8,128)S(1)}, u32[]{:S(2)}, u32[]{:S(2)}) collective-permute-start(f32[8,64]{1,0:T(8,128)S(1)} %add.35), channel_id=1, source_target_pairs={{0,4},{1,5},{2,6},{3,7},{4,0},{5,1},{6,2},{7,3},{8,12},{9,13},{10,... | collective-permute-start | bytes 6152 | tf_op jit(solution)/shard_map/ppermute | solution.py:240

commit v4 on v3

--- a/solution.py
+++ b/solution.py
@@ -85,8 +85,9 @@
         of_token = jnp.sum(jnp.where(kind == kinds, rank, 0.0), axis=0, keepdims=True)
         chosen = jnp.where((of_token == wanted) & (times < len_ref[p]), 1.0, 0.0)
         passage = tiles_ref[pl.ds(p, tokens, stride=held), :]
-        pay_ref[s * EXP:(s + 1) * EXP, :] = jnp.dot(
-            chosen, passage, precision=HIGHEST, preferred_element_type=jnp.float32)
+        pieces = jnp.dot(chosen.astype(jnp.bfloat16), jnp.concatenate(thirds(passage), axis=1),
+                         preferred_element_type=jnp.float32)
+        pay_ref[s * EXP:(s + 1) * EXP, :] = pieces[:, 2 * DIM:] + pieces[:, DIM:2 * DIM] + pieces[:, :DIM]
     pay_ref[ID_ROW:ID_ROW + 1, :] = ids
     for c, at in enumerate(range(0, queries_n, DIM)):
         width = min(DIM, queries_n - at)
@@ -112,9 +113,7 @@
         pick = (col % EXP == row[:, :1] % EXP) & (col < FB * EXP) & (ids == owner[:, :1])
         pick = jnp.where(pick, 1.0, 0.0).astype(jnp.bfloat16)
         block = jnp.concatenate([pay[at:at + CAND_ROW, :] for pay, at in some], axis=0)
-        high, low = split(block)
-        rest = (block - high.astype(jnp.float32) - low.astype(jnp.float32)).astype(jnp.bfloat16)
-        for piece in (rest, low, high):
+        for piece in thirds(block)[::-1]:
             total += jnp.dot(pick, piece, preferred_element_type=jnp.float32)
     for ref, sums in ((keep_ref, total[:rows // 2]), (send_ref, total[rows // 2:])):
         ref[:rows // 2, :] = sums
@@ -126,82 +125,127 @@
     return lax.dot_general(a, b, (((1,), (1,)), ((), ())), precision=precision, preferred_element_type=jnp.float32)
 
 
+def thirds(x):
+    high, low = split(x)
+    return high, low, (x - high.astype(jnp.float32) - low.astype(jnp.float32)).astype(jnp.bfloat16)
+
+
 def split(x):
     high = x.astype(jnp.bfloat16)
     return high, (x - high.astype(jnp.float32)).astype(jnp.bfloat16)
 
 
-def score_kernel(side, outer, asking, queries_n, held, n_tiles, n_asks, pos_ref, *refs):
-    tile_refs, ask_refs = refs[:n_tiles], refs[n_tiles:n_tiles + n_asks]
-    keep_ref, from_side_ref, mine_ref, theirs_ref, out_ref = refs[n_tiles + n_asks:]
-    pos = pos_ref[0]
-    n_in, n_out = 4, 1 << len(outer)
-    me_out = gather_bits(pos, outer)
-    half = n_out * EXP
-    sums = mine_ref[...] + theirs_ref[...]
-    scale = lax.rsqrt(jnp.mean(sums * sums, axis=1, keepdims=True) + 1e-05)
-    order = (iota((half, 1), 0) % EXP).astype(jnp.float32)
-    weight = BETA * jnp.log((NCENT + 1.0) / (order + 1.0))
-    extra = sums * (scale * weight)
-    expanded = jnp.concatenate([ask[...] for ask in ask_refs] + [extra], axis=0)
-    total = expanded.shape[0]
-    lefts = []
-    for ref in tile_refs:
-        high, low = split(ref[...])
-        lefts.append((high, jnp.concatenate([high, low], axis=1)))
-    parts = [[] for _ in lefts]
-    for at in range(0, total, 256):
-        high, low = split(expanded[at:at + 256])
-        twice = jnp.concatenate([high, high], axis=1)
-        for i, (left, wide) in enumerate(lefts):
-            similar = nt_dot(wide, twice) + nt_dot(left, low)
-            groups = similar.shape[0] // 8
-            parts[i].append(jnp.max(similar.reshape(groups, 8, similar.shape[1]), axis=0))
-    largest = []
-    for part in parts:
-        top = jnp.concatenate(part, axis=1)
+def at_steps(pos, steps, device, entry):
+    place = jnp.zeros(entry.shape, jnp.int32)
+    for i, away in enumerate(steps):
+        place = jnp.where(entry // 8 == i, pos ^ away, place)
+    return place == device
+
+
+def largest_rows(parts, held):
+    rows = []
+    for top in parts:
         step = held
         while step < 8:
             top = jnp.maximum(top, pltpu.roll(top, step, 0))
             step *= 2
-        largest.append(top)
-    largest = jnp.concatenate(largest, axis=0)
-    col = iota((n_out, total), 1)
-    of_ask = gather_bits(spread(col // QL, asking), outer) ^ me_out
-    of_col = jnp.where(col < n_out * QL, of_ask, (col - n_out * QL) // EXP)
+        rows.append(top)
+    return jnp.concatenate(rows, axis=0)
+
+
+def over_tokens(similar):
+    return jnp.max(similar.reshape(similar.shape[0] // 8, 8, similar.shape[1]), axis=0)
+
+
+def match_kernel(side, outer, asking, queries_n, held, n_tiles, n_asks, pos_ref, *refs):
+    tile_refs, ask_refs = refs[:n_tiles], refs[n_tiles:n_tiles + n_asks]
+    keep_ref, from_side_ref = refs[n_tiles + n_asks:n_tiles + n_asks + 2]
+    *wide_refs, values_ref, chosen_ref = refs[n_tiles + n_asks + 2:]
+    pos = pos_ref[0]
+    n_out = 1 << len(outer)
+    me_out = gather_bits(pos, outer)
+    half = n_out * EXP
+    tokens = jnp.concatenate([ask[...] for ask in ask_refs], axis=0)
+    total = tokens.shape[0]
+    lefts = []
+    for ref, wide_ref in zip(tile_refs, wide_refs):
+        high, low = split(ref[...])
+        wide = jnp.concatenate([high, low], axis=1)
+        wide_ref[...] = wide
+        lefts.append((high, wide))
+    parts = [[] for _ in lefts]
+    for at in range(0, total, 256):
+        high, low = split(tokens[at:at + 256])
+        twice = jnp.concatenate([high, high], axis=1)
+        for i, (left, wide) in enumerate(lefts):
+            parts[i].append(over_tokens(nt_dot(wide, twice) + nt_dot(left, low)))
+    largest = largest_rows([jnp.concatenate(part, axis=1) for part in parts], held)
+    of_col = gather_bits(spread(iota((n_out, total), 1) // QL, asking), outer) ^ me_out
     member = jnp.where(of_col == iota((n_out, total), 0), 1.0 / QL, 0.0)
-    values = nt_dot(member, largest, HIGHEST)
+    values_ref[...] = nt_dot(member, largest, HIGHEST)
 
     cands = jnp.concatenate([keep_ref[half:, :], from_side_ref[half:, :]], axis=0)
+    entries = cands.shape[0]
     own = (pos & ~sum(outer)) | spread(iota((n_out, DIM), 0), outer)
-    slots = out_ref.shape[1]
-    device = iota((n_in * 8, slots), 1) // CAP
-    which = iota((n_in * 8, slots), 1) % CAP
-    entry = iota((n_in * 8, slots), 0)
-
-    def at_device(steps):
-        place = jnp.zeros((n_in * 8, slots), jnp.int32)
-        for i, away in enumerate(steps):
-            place = jnp.where(entry // 8 == i, pos ^ away, place)
-        return place == device
-
-    same = at_device([0, 1, side, side | 1])
+    slots = chosen_ref.shape[1]
+    slot = iota((entries, slots), 1)
+    entry = iota((entries, slots), 0)
+    same = at_steps(pos, [0, 1, side, side | 1], slot // CAP, entry)
     local = jnp.zeros((n_out, slots), jnp.float32)
     count = jnp.zeros((n_out, slots), jnp.float32)
     for c, at in enumerate(range(0, queries_n, DIM)):
         found = nt_dot(jnp.where(own - at == iota((n_out, DIM), 1), 1.0, 0.0), cands, HIGHEST)
         top = (CAP + 1) * c
-        pick = jnp.where(same & (entry % 8 == top + which), 1.0, 0.0)
+        pick = jnp.where(same & (entry % 8 == top + slot % CAP), 1.0, 0.0)
         local += jnp.dot(found, pick, precision=HIGHEST, preferred_element_type=jnp.float32)
         pick = jnp.where(same & (entry % 8 == top + CAP), 1.0, 0.0)
         count += jnp.dot(found, pick, precision=HIGHEST, preferred_element_type=jnp.float32)
-    same = at_device([0, side, 1, side | 1])
+    live = (iota((n_out, slots), 1) % CAP).astype(jnp.float32) < count
+    for p in range(held):
+        chosen_ref[p * n_out:(p + 1) * n_out, :] = jnp.where(live & (local == float(p)), 1.0, 0.0)
+
+
+def score_kernel(side, outer, held, n_tiles, pos_ref, *refs):
+    wide_refs = refs[:n_tiles]
+    values_ref, chosen_ref, mine_ref, theirs_ref, out_ref = refs[n_tiles:]
+    pos = pos_ref[0]
+    n_out = 1 << len(outer)
+    half = n_out * EXP
+    sums = mine_ref[...] + theirs_ref[...]
+    scale = lax.rsqrt(jnp.mean(sums * sums, axis=1, keepdims=True) + 1e-05)
+    order = (iota((half, 1), 0) % EXP).astype(jnp.float32)
+    extra = sums * (scale * (BETA * jnp.log((NCENT + 1.0) / (order + 1.0))))
+    if half % DIM > 0:
+        extra = jnp.concatenate([extra, jnp.zeros((-half % DIM, DIM), jnp.float32)], axis=0)
+    parts = [[] for _ in wide_refs]
+    for at in range(0, half, DIM):
+        high, low = split(extra[at:at + DIM])
+        right = jnp.concatenate([
+            jnp.concatenate([high, high], axis=1),
+            jnp.concatenate([low, jnp.zeros_like(low)], axis=1),
+        ], axis=0)
+        for i, wide in enumerate(wide_refs):
+            both = nt_dot(wide[...], right)
+            parts[i].append(over_tokens(both[:, :DIM] + both[:, DIM:]))
+    largest = largest_rows([jnp.concatenate(part, axis=1) for part in parts], held)
+    total = largest.shape[1]
+    col = iota((n_out, 3 * total), 1) % total
+    member = jnp.where(col // EXP == iota((n_out, 3 * total), 0), 1.0 / QL, 0.0).astype(jnp.bfloat16)
+    values = values_ref[...] + nt_dot(member, jnp.concatenate(thirds(largest), axis=1))
+    slots = out_ref.shape[1]
+    padded = slots + (-slots % DIM)
+    shape = (n_tiles * 8, held * padded)
+    entry = iota(shape, 0)
+    col = iota(shape, 1)
+    same = at_steps(pos, [0, side, 1, side | 1], col % padded // CAP, entry) & (col % padded < slots)
+    pick = jnp.where(same & (entry % 8 == col // padded), 1.0, 0.0).astype(jnp.bfloat16)
+    found = jnp.dot(jnp.concatenate(thirds(values), axis=0), pick, preferred_element_type=jnp.float32)
+    found = found[:n_out] + found[n_out:2 * n_out] + found[2 * n_out:]
     result = jnp.zeros((n_out, slots), jnp.float32)
     for p in range(held):
-        pick = jnp.where(same & (entry % 8 == p), 1.0, 0.0)
-        value = jnp.dot(values, pick, precision=HIGHEST, preferred_element_type=jnp.float32)
-        result = jnp.where(local == float(p), value, result)
-    out_ref[...] = jnp.where((iota((n_out, slots), 1) % CAP).astype(jnp.float32) < count, result, 0.0)
+        value = found[:, p * padded:p * padded + slots]
+        result = jnp.where(chosen_ref[p * n_out:(p + 1) * n_out, :] > 0.5, value, result)
+    out_ref[...] = result
 
 
 def call(kernel, outs, *args, copied=False):
@@ -273,10 +317,16 @@
     came = swap(sums, outer[-1])
     tiles = [masked, far]
     tiles = tiles + [swap(t, 1) for t in tiles]
+    slots = devices * CAP
+    wide = jax.ShapeDtypeStruct((tokens * held, 2 * DIM), jnp.bfloat16)
+    *tiles, values, chosen = call(
+        functools.partial(match_kernel, side, outer, asking, queries_n, held, len(tiles), len(asks)),
+        [wide] * len(tiles) + [struct(n_out, 8 * len(tiles)), struct(held * n_out, slots)],
+        pos, *tiles, *asks, keep, from_side,
+    )
     table = call(
-        functools.partial(score_kernel, side, outer, asking, queries_n, held, len(tiles), len(asks)),
-        [struct(n_out, devices * CAP)],
-        pos, *tiles, *asks, keep, from_side, sums, came,
+        functools.partial(score_kernel, side, outer, held, len(tiles)), [struct(n_out, slots)],
+        pos, *tiles, values, chosen, sums, came,
     )
     for mask in reversed(outer):
         table = table + swap(table, mask)

time: 38.1 us -> 36.8 us (0.966)
  waiting for transfers between devices: 14.5 us -> 13.4 us
    ppermute x14, waiting for transfers between devices: 14.5 us -> 13.4 us  [swap(): return lax.ppermute(x, AXES, [(i, i ^ mask) for i in range(devices)])]
    pallas_call x3 -> x4, Pallas kernels: 4.13 us -> 4.03 us  [call(): pl.pallas_call(kernel, out_shape=[pltpu.VMEM(o.shape, o.dtype) for o in o...]
  transfers between devices with their start and end apart: 14 -> 14, of which waited for: 6 -> 7; matrix products, arithmetic and copies ran while one was open for 0% -> 0% of each run, Pallas kernels for 1% -> 4%
where the time goes in v4:
time: 36.8 us; the launch traced here: 36.7 us
  starting transfers between devices  18.6 us (51%)
  waiting for transfers between devices  13.4 us (36%)
  Pallas kernels  4.03 us (11%)
  local copies, waits for them, and re-layouts  0.52 us (1%)
    ppermute x14, starting transfers between devices, swap(): return lax.ppermute(x, AXES, [(i, i ^ mask) for i in range(devices)])  18.6 us
    ppermute x14, waiting for transfers between devices, swap(): return lax.ppermute(x, AXES, [(i, i ^ mask) for i in range(devices)])  13.4 us
    pallas_call x4, Pallas kernels, call(): pl.pallas_call(kernel, out_shape=[pltpu.VMEM(o.shape, o.dtype) for o in o...  4.03 us
  transfers between devices with their start and end apart: 14, of which 7 were waited for; matrix products, arithmetic and copies ran while one was open for 0% of the time, Pallas kernels for 4%

profile of v4, /device:TPU:0, one launch (start us, length us, event | category | flops | bytes accessed | tf_op | source)
XLA Modules:
  0.0 36.7 jit_solution(13993005148662398627)
XLA Ops:
  0.0 0.0 copy-start
  0.0 1.7 %shard_map.82 = (f32[720,128]{1,0:T(8,128)S(1)}, f32[40,128]{1,0:T(8,128)S(1)}) custom-call(s32[1]{0:T(128)} %bitcast.pos_ref, s32[4]{0:T(128)} %refs_0_.1, f32[720,128]{1,0:T(8,128)} %bitcast.13, s32[4,180]{1,0:T(4,128)} %refs_2_.1, s32[3,32]{1,0:T(4,128)} %bitcast.15, s32[24,32]{1,0:T(8,128)} %bitcast.14, s32[2,32]{1,0:T(2,128)} %bitcast.16, s32[1,32]{1,0:T(1,128)} %bitcast.17), custom_call_target="tpu_custom_call" | custom-call | tf_op jit(solution)/shard_map/pallas_call | solution.py:261
  1.7 0.5 %collective-permute-start.2 = (f32[40,128]{1,0:T(8,128)S(1)}, f32[40,128]{1,0:T(8,128)S(1)}, u32[]{:S(2)}, u32[]{:S(2)}) collective-permute-start(f32[40,128]{1,0:T(8,128)S(1)} %get-tuple-element.24.refs_0_), channel_id=1, source_target_pairs={{0,1},{1,0},{2,3},{3,2},{4,5},{5,4},{6,7},{7,6},{8,9},{9,8},{10,11... | collective-permute-start | bytes 61448 | tf_op jit(solution)/shard_map/ppermute | solution.py:284
  2.2 0.0 copy-done
  2.2 2.7 %collective-permute-start = (f32[32,128]{1,0:T(8,128)S(1)}, f32[32,128]{1,0:T(8,128)S(1)}, u32[]{:S(2)}, u32[]{:S(2)}) collective-permute-start(f32[32,128]{1,0:T(8,128)S(1)} %bitcast.9), channel_id=1, source_target_pairs={{0,2},{1,3},{2,0},{3,1},{4,6},{5,7},{6,4},{7,5},{8,10},{9,11},{10,... | collective-permute-start | bytes 49160 | tf_op jit(solution)/shard_map/ppermute | solution.py:284
  4.8 0.0 collective-permute-done.2.refs_1_
  4.8 0.3 shard_map.83
  5.2 1.6 %collective-permute-start.3 = (f32[96,128]{1,0:T(8,128)S(1)}, f32[96,128]{1,0:T(8,128)S(1)}, u32[]{:S(2)}, u32[]{:S(2)}) collective-permute-start(f32[96,128]{1,0:T(8,128)S(1)} %get-tuple-element.26), channel_id=1, source_target_pairs={{0,8},{1,9},{2,10},{3,11},{4,12},{5,13},{6,14},{7,15},{8,0},{9,1},... | collective-permute-start | bytes 147464 | tf_op jit(solution)/shard_map/ppermute | solution.py:284
  6.7 0.0 collective-permute-done.refs_5_
  6.7 1.8 %collective-permute-start.6 = (f32[64,128]{1,0:T(8,128)S(1)}, f32[64,128]{1,0:T(8,128)S(1)}, u32[]{:S(2)}, u32[]{:S(2)}) collective-permute-start(f32[64,128]{1,0:T(8,128)S(1)} %pad_maximum_fusion.1), channel_id=1, source_target_pairs={{0,16},{1,17},{2,18},{3,19},{4,20},{5,21},{6,22},{7,23},{8,24},{9,... | collective-permute-start | bytes 98312 | tf_op jit(solution)/shard_map/ppermute | solution.py:284
  8.5 1.5 %collective-permute-start.1 = (f32[720,128]{1,0:T(8,128)S(1)}, f32[720,128]{1,0:T(8,128)S(1)}, u32[]{:S(2)}, u32[]{:S(2)}) collective-permute-start(f32[720,128]{1,0:T(8,128)S(1)} %get-tuple-element.23.refs_0_), channel_id=1, source_target_pairs={{0,8},{1,9},{2,10},{3,11},{4,12},{5,13},{6,14},{7,15},{8,0},{9,1},... | collective-permute-start | bytes 1105928 | tf_op jit(solution)/shard_map/ppermute | solution.py:284
  10.0 0.0 collective-permute-done.3.refs_9_
  10.0 2.7 %collective-permute-start.4 = (f32[80,128]{1,0:T(8,128)S(1)}, f32[80,128]{1,0:T(8,128)S(1)}, u32[]{:S(2)}, u32[]{:S(2)}) collective-permute-start(f32[80,128]{1,0:T(8,128)S(1)} %slice_add_fusion), channel_id=1, source_target_pairs={{0,4},{1,5},{2,6},{3,7},{4,0},{5,1},{6,2},{7,3},{8,12},{9,13},{10,... | collective-permute-start | bytes 122888 | tf_op jit(solution)/shard_map/ppermute | solution.py:284
  12.7 0.0 collective-permute-done.6.refs_6_
  12.7 0.8 %collective-permute-start.7 = (f32[128,128]{1,0:T(8,128)S(1)}, f32[128,128]{1,0:T(8,128)S(1)}, u32[]{:S(2)}, u32[]{:S(2)}) collective-permute-start(f32[128,128]{1,0:T(8,128)S(1)} %pad_maximum_fusion), channel_id=1, source_target_pairs={{0,4},{1,5},{2,6},{3,7},{4,0},{5,1},{6,2},{7,3},{8,12},{9,13},{10,... | collective-permute-start | bytes 196616 | tf_op jit(solution)/shard_map/ppermute | solution.py:284
  13.5 1.8 %collective-permute-done.4 = f32[80,128]{1,0:T(8,128)S(1)} collective-permute-done((f32[80,128]{1,0:T(8,128)S(1)}, f32[80,128]{1,0:T(8,128)S(1)}, u32[]{:S(2)}, u32[]{:S(2)}) %collective-permute-start.4) | collective-permute-done | bytes 40992 | tf_op jit(solution)/shard_map/ppermute | solution.py:284
  15.3 1.7 %collective-permute-start.5 = (f32[80,128]{1,0:T(8,128)S(1)}, f32[80,128]{1,0:T(8,128)S(1)}, u32[]{:S(2)}, u32[]{:S(2)}) collective-permute-start(f32[80,128]{1,0:T(8,128)S(1)} %add.32), channel_id=1, source_target_pairs={{0,2},{1,3},{2,0},{3,1},{4,6},{5,7},{6,4},{7,5},{8,10},{9,11},{10,... | collective-permute-start | bytes 122888 | tf_op jit(solution)/shard_map/ppermute | solution.py:284
  17.0 0.0 collective-permute-start.8
  17.0 2.3 %collective-permute-done.5 = f32[80,128]{1,0:T(8,128)S(1)} collective-permute-done((f32[80,128]{1,0:T(8,128)S(1)}, f32[80,128]{1,0:T(8,128)S(1)}, u32[]{:S(2)}, u32[]{:S(2)}) %collective-permute-start.5) | collective-permute-done | bytes 40992 | tf_op jit(solution)/shard_map/ppermute | solution.py:284
  19.3 0.0 collective-permute-done.7.refs_7_
  19.3 0.0 collective-permute-done.1.refs_1_
  19.3 0.1 collective-permute-start.9
  19.4 0.6 %collective-permute-start.10 = (f32[80,128]{1,0:T(8,128)S(1)}, f32[80,128]{1,0:T(8,128)S(1)}, u32[]{:S(2)}, u32[]{:S(2)}) collective-permute-start(f32[80,128]{1,0:T(8,128)S(1)} %add.33.refs_6_), channel_id=1, source_target_pairs={{0,16},{1,17},{2,18},{3,19},{4,20},{5,21},{6,22},{7,23},{8,24},{9,... | collective-permute-start | bytes 122888 | tf_op jit(solution)/shard_map/ppermute | solution.py:284
  20.0 0.0 collective-permute-done.8.refs_2_
  20.0 1.1 %collective-permute-done.9.refs_3_ = f32[720,128]{1,0:T(8,128)S(1)} collective-permute-done((f32[720,128]{1,0:T(8,128)S(1)}, f32[720,128]{1,0:T(8,128)S(1)}, u32[]{:S(2)}, u32[]{:S(2)}) %collective-permute-start.9) | collective-permute-done | bytes 368672 | tf_op jit(solution)/shard_map/ppermute | solution.py:284
  21.1 1.1 %shard_map.84 = (bf16[720,256]{1,0:T(8,128)(2,1)S(1)}, bf16[720,256]{1,0:T(8,128)(2,1)S(1)}, bf16[720,256]{1,0:T(8,128)(2,1)S(1)}, bf16[720,256]{1,0:T(8,128)(2,...) custom-call(s32[1]{0:T(128)} %bitcast.pos_ref, f32[720,128]{1,0:T(8,128)S(1)} %get-tuple-element.23.refs_0_, ...), custom_call_target="tpu_custom_call" | custom-call | tf_op jit(solution)/shard_map/pallas_call | solution.py:261
  22.2 1.2 %collective-permute-done.10.refs_7_ = f32[80,128]{1,0:T(8,128)S(1)} collective-permute-done((f32[80,128]{1,0:T(8,128)S(1)}, f32[80,128]{1,0:T(8,128)S(1)}, u32[]{:S(2)}, u32[]{:S(2)}) %collective-permute-start.10) | collective-permute-done | bytes 40992 | tf_op jit(solution)/shard_map/ppermute | solution.py:284
  23.5 0.9 %shard_map.85 = f32[8,64]{1,0:T(8,128)S(1)} custom-call(s32[1]{0:T(128)} %bitcast.pos_ref, bf16[720,256]{1,0:T(8,128)(2,1)S(1)} %get-tuple-element.32.refs_0_, bf16[720,256]{1,0:T(8,128)(2,1)S(1)} %get-tuple-element.33.refs_1_, bf16[720,256]{1,0:T(8,128)(2,1)S(1)} %get-tuple-element.34.refs_2_, bf16[720,256]{1,0:T(8,128)(2,1)S(1)} %get-tuple-element.35.refs_3_, ...), custom_call_target="tpu_custom_call" | custom-call | tf_op jit(solution)/shard_map/pallas_call | solution.py:261
  24.4 0.6 %collective-permute-start.11 = (f32[8,64]{1,0:T(8,128)S(1)}, f32[8,64]{1,0:T(8,128)S(1)}, u32[]{:S(2)}, u32[]{:S(2)}) collective-permute-start(f32[8,64]{1,0:T(8,128)S(1)} %shard_map.85), channel_id=1, source_target_pairs={{0,16},{1,17},{2,18},{3,19},{4,20},{5,21},{6,22},{7,23},{8,24},{9,... | collective-permute-start | bytes 6152 | tf_op jit(solution)/shard_map/ppermute | solution.py:284
  24.9 3.1 %collective-permute-done.11 = f32[8,64]{1,0:T(8,128)S(1)} collective-permute-done((f32[8,64]{1,0:T(8,128)S(1)}, f32[8,64]{1,0:T(8,128)S(1)}, u32[]{:S(2)}, u32[]{:S(2)}) %collective-permute-start.11) | collective-permute-done | bytes 2080 | tf_op jit(solution)/shard_map/ppermute | solution.py:284
  28.0 1.7 %collective-permute-start.12 = (f32[8,64]{1,0:T(8,128)S(1)}, f32[8,64]{1,0:T(8,128)S(1)}, u32[]{:S(2)}, u32[]{:S(2)}) collective-permute-start(f32[8,64]{1,0:T(8,128)S(1)} %add.34), channel_id=1, source_target_pairs={{0,2},{1,3},{2,0},{3,1},{4,6},{5,7},{6,4},{7,5},{8,10},{9,11},{10,... | collective-permute-start | bytes 6152 | tf_op jit(solution)/shard_map/ppermute | solution.py:284
  29.7 1.9 %collective-permute-done.12 = f32[8,64]{1,0:T(8,128)S(1)} collective-permute-done((f32[8,64]{1,0:T(8,128)S(1)}, f32[8,64]{1,0:T(8,128)S(1)}, u32[]{:S(2)}, u32[]{:S(2)}) %collective-permute-start.12) | collective-permute-done | bytes 2080 | tf_op jit(solution)/shard_map/ppermute | solution.py:284
  31.6 2.5 %collective-permute-start.13 = (f32[8,64]{1,0:T(8,128)S(1)}, f32[8,64]{1,0:T(8,128)S(1)}, u32[]{:S(2)}, u32[]{:S(2)}) collective-permute-start(f32[8,64]{1,0:T(8,128)S(1)} %add.35), channel_id=1, source_target_pairs={{0,4},{1,5},{2,6},{3,7},{4,0},{5,1},{6,2},{7,3},{8,12},{9,13},{10,... | collective-permute-start | bytes 6152 | tf_op jit(solution)/shard_map/ppermute | solution.py:284
  34.1 2.0 %collective-permute-done.13 = f32[8,64]{1,0:T(8,128)S(1)} collective-permute-done((f32[8,64]{1,0:T(8,128)S(1)}, f32[8,64]{1,0:T(8,128)S(1)}, u32[]{:S(2)}, u32[]{:S(2)}) %collective-permute-start.13) | collective-permute-done | bytes 2080 | tf_op jit(solution)/shard_map/ppermute | solution.py:284
  36.1 0.5 %constant_dynamic-slice_fusion = f32[1,64]{1,0:T(1,128)} fusion(f32[8,64]{1,0:T(8,128)S(1)} %add.36, s32[]{:T(128)S(6)} %select_n.16), kind=kLoop, calls=%fused_computation.3 | loop fusion | bytes 516 | tf_op jit(solution)/shard_map/dynamic_slice | solution.py:334
  (8 shorter events, 0.0 us)
Async XLA Ops:
  0.0 2.2 %copy-start = (f32[1,32,128]{2,1,0:T(8,128)S(1)}, f32[1,32,128]{2,1,0:T(8,128)}, u32[]{:S(2)}) copy-start(f32[1,32,128]{2,1,0:T(8,128)} %param.8) | copy-start | bytes 49156
  1.7 3.2 %collective-permute-start.2 = (f32[40,128]{1,0:T(8,128)S(1)}, f32[40,128]{1,0:T(8,128)S(1)}, u32[]{:S(2)}, u32[]{:S(2)}) collective-permute-start(f32[40,128]{1,0:T(8,128)S(1)} %get-tuple-element.24.refs_0_), channel_id=1, source_target_pairs={{0,1},{1,0},{2,3},{3,2},{4,5},{5,4},{6,7},{7,6},{8,9},{9,8},{10,11... | collective-permute-start | bytes 61448 | tf_op jit(solution)/shard_map/ppermute | solution.py:284
  2.2 4.5 %collective-permute-start = (f32[32,128]{1,0:T(8,128)S(1)}, f32[32,128]{1,0:T(8,128)S(1)}, u32[]{:S(2)}, u32[]{:S(2)}) collective-permute-start(f32[32,128]{1,0:T(8,128)S(1)} %bitcast.9), channel_id=1, source_target_pairs={{0,2},{1,3},{2,0},{3,1},{4,6},{5,7},{6,4},{7,5},{8,10},{9,11},{10,... | collective-permute-start | bytes 49160 | tf_op jit(solution)/shard_map/ppermute | solution.py:284
  5.2 4.9 %collective-permute-start.3 = (f32[96,128]{1,0:T(8,128)S(1)}, f32[96,128]{1,0:T(8,128)S(1)}, u32[]{:S(2)}, u32[]{:S(2)}) collective-permute-start(f32[96,128]{1,0:T(8,128)S(1)} %get-tuple-element.26), channel_id=1, source_target_pairs={{0,8},{1,9},{2,10},{3,11},{4,12},{5,13},{6,14},{7,15},{8,0},{9,1},... | collective-permute-start | bytes 147464 | tf_op jit(solution)/shard_map/ppermute | solution.py:284
  6.7 6.0 %collective-permute-start.6 = (f32[64,128]{1,0:T(8,128)S(1)}, f32[64,128]{1,0:T(8,128)S(1)}, u32[]{:S(2)}, u32[]{:S(2)}) collective-permute-start(f32[64,128]{1,0:T(8,128)S(1)} %pad_maximum_fusion.1), channel_id=1, source_target_pairs={{0,16},{1,17},{2,18},{3,19},{4,20},{5,21},{6,22},{7,23},{8,24},{9,... | collective-permute-start | bytes 98312 | tf_op jit(solution)/shard_map/ppermute | solution.py:284
  8.5 10.8 %collective-permute-start.1 = (f32[720,128]{1,0:T(8,128)S(1)}, f32[720,128]{1,0:T(8,128)S(1)}, u32[]{:S(2)}, u32[]{:S(2)}) collective-permute-start(f32[720,128]{1,0:T(8,128)S(1)} %get-tuple-element.23.refs_0_), channel_id=1, source_target_pairs={{0,8},{1,9},{2,10},{3,11},{4,12},{5,13},{6,14},{7,15},{8,0},{9,1},... | collective-permute-start | bytes 1105928 | tf_op jit(solution)/shard_map/ppermute | solution.py:284
  10.0 5.3 %collective-permute-start.4 = (f32[80,128]{1,0:T(8,128)S(1)}, f32[80,128]{1,0:T(8,128)S(1)}, u32[]{:S(2)}, u32[]{:S(2)}) collective-permute-start(f32[80,128]{1,0:T(8,128)S(1)} %slice_add_fusion), channel_id=1, source_target_pairs={{0,4},{1,5},{2,6},{3,7},{4,0},{5,1},{6,2},{7,3},{8,12},{9,13},{10,... | collective-permute-start | bytes 122888 | tf_op jit(solution)/shard_map/ppermute | solution.py:284
  12.7 6.6 %collective-permute-start.7 = (f32[128,128]{1,0:T(8,128)S(1)}, f32[128,128]{1,0:T(8,128)S(1)}, u32[]{:S(2)}, u32[]{:S(2)}) collective-permute-start(f32[128,128]{1,0:T(8,128)S(1)} %pad_maximum_fusion), channel_id=1, source_target_pairs={{0,4},{1,5},{2,6},{3,7},{4,0},{5,1},{6,2},{7,3},{8,12},{9,13},{10,... | collective-permute-start | bytes 196616 | tf_op jit(solution)/shard_map/ppermute | solution.py:284
  15.3 4.0 %collective-permute-start.5 = (f32[80,128]{1,0:T(8,128)S(1)}, f32[80,128]{1,0:T(8,128)S(1)}, u32[]{:S(2)}, u32[]{:S(2)}) collective-permute-start(f32[80,128]{1,0:T(8,128)S(1)} %add.32), channel_id=1, source_target_pairs={{0,2},{1,3},{2,0},{3,1},{4,6},{5,7},{6,4},{7,5},{8,10},{9,11},{10,... | collective-permute-start | bytes 122888 | tf_op jit(solution)/shard_map/ppermute | solution.py:284
  17.0 3.0 %collective-permute-start.8 = (f32[720,128]{1,0:T(8,128)S(1)}, f32[720,128]{1,0:T(8,128)S(1)}, u32[]{:S(2)}, u32[]{:S(2)}) collective-permute-start(f32[720,128]{1,0:T(8,128)S(1)} %get-tuple-element.23.refs_0_), channel_id=1, source_target_pairs={{0,1},{1,0},{2,3},{3,2},{4,5},{5,4},{6,7},{7,6},{8,9},{9,8},{10,11... | collective-permute-start | bytes 1105928 | tf_op jit(solution)/shard_map/ppermute | solution.py:284
  19.3 1.8 %collective-permute-start.9 = (f32[720,128]{1,0:T(8,128)S(1)}, f32[720,128]{1,0:T(8,128)S(1)}, u32[]{:S(2)}, u32[]{:S(2)}) collective-permute-start(f32[720,128]{1,0:T(8,128)S(1)} %collective-permute-done.1.refs_1_), channel_id=1, source_target_pairs={{0,1},{1,0},{2,3},{3,2},{4,5},{5,4},{6,7},{7,6},{8,9},{9,8},{10,11... | collective-permute-start | bytes 1105928 | tf_op jit(solution)/shard_map/ppermute | solution.py:284
  19.4 4.1 %collective-permute-start.10 = (f32[80,128]{1,0:T(8,128)S(1)}, f32[80,128]{1,0:T(8,128)S(1)}, u32[]{:S(2)}, u32[]{:S(2)}) collective-permute-start(f32[80,128]{1,0:T(8,128)S(1)} %add.33.refs_6_), channel_id=1, source_target_pairs={{0,16},{1,17},{2,18},{3,19},{4,20},{5,21},{6,22},{7,23},{8,24},{9,... | collective-permute-start | bytes 122888 | tf_op jit(solution)/shard_map/ppermute | solution.py:284
  24.4 3.6 %collective-permute-start.11 = (f32[8,64]{1,0:T(8,128)S(1)}, f32[8,64]{1,0:T(8,128)S(1)}, u32[]{:S(2)}, u32[]{:S(2)}) collective-permute-start(f32[8,64]{1,0:T(8,128)S(1)} %shard_map.85), channel_id=1, source_target_pairs={{0,16},{1,17},{2,18},{3,19},{4,20},{5,21},{6,22},{7,23},{8,24},{9,... | collective-permute-start | bytes 6152 | tf_op jit(solution)/shard_map/ppermute | solution.py:284
  28.0 3.6 %collective-permute-start.12 = (f32[8,64]{1,0:T(8,128)S(1)}, f32[8,64]{1,0:T(8,128)S(1)}, u32[]{:S(2)}, u32[]{:S(2)}) collective-permute-start(f32[8,64]{1,0:T(8,128)S(1)} %add.34), channel_id=1, source_target_pairs={{0,2},{1,3},{2,0},{3,1},{4,6},{5,7},{6,4},{7,5},{8,10},{9,11},{10,... | collective-permute-start | bytes 6152 | tf_op jit(solution)/shard_map/ppermute | solution.py:284
  31.6 4.5 %collective-permute-start.13 = (f32[8,64]{1,0:T(8,128)S(1)}, f32[8,64]{1,0:T(8,128)S(1)}, u32[]{:S(2)}, u32[]{:S(2)}) collective-permute-start(f32[8,64]{1,0:T(8,128)S(1)} %add.35), channel_id=1, source_target_pairs={{0,4},{1,5},{2,6},{3,7},{4,0},{5,1},{6,2},{7,3},{8,12},{9,13},{10,... | collective-permute-start | bytes 6152 | tf_op jit(solution)/shard_map/ppermute | solution.py:284

commit v5 on v4

--- a/solution.py
+++ b/solution.py
@@ -43,12 +43,42 @@
     sources, (masked_ref, pay_ref) = refs[:7], refs[7:9]
     landed, sems = refs[9:16], refs[16]
     copies = [pltpu.make_async_copy(a, b, sems.at[k]) for k, (a, b) in enumerate(zip(sources, landed))]
-    for copy in copies:
+    for copy in copies[::-1]:
         copy.start()
-    for copy in copies:
+    for copy in copies[:1] + copies[2:]:
         copy.wait()
     len_ref, tiles_ref, clusters_ref, feedback_ref, ranks_ref, local_ref, count_ref = landed
     pos = pos_ref[0]
+    nearby = feedback_ref[...] - pos * held
+    number = (iota(nearby.shape, 0) * queries_n + iota(nearby.shape, 1)) * held + nearby
+    here = (nearby >= 0) & (nearby < held)
+    key = jnp.where(here, number, 0).astype(jnp.float32)
+    least = jnp.min(jnp.where(here, key, 1e9))
+    most = jnp.max(key)
+    keys = [least, jnp.sum(key) - least - most, most]
+    ranks = ranks_ref[...].astype(jnp.float32)
+    lane = iota(ranks.shape, 1)
+    pay_ref[:ASK_ROW, :] = jnp.zeros((ASK_ROW, DIM), jnp.float32)
+    ids = jnp.zeros((1, DIM), jnp.float32)
+    slot = iota((1, DIM), 1) // EXP
+    kinds = iota((NCENT, tokens), 0)
+    times = iota((EXP, tokens), 1)
+    wanted = iota((EXP, tokens), 0).astype(jnp.float32)
+    pairs = []
+    for s in range(FB):
+        whole = keys[s].astype(jnp.int32)
+        p = whole % held
+        q = (whole // held) % queries_n
+        ids = jnp.where(slot == s, q.astype(jnp.float32), ids)
+        rank = jnp.sum(jnp.where(lane == q, ranks, 0.0), axis=1, keepdims=True)
+        kind = clusters_ref[pl.ds(p, 1), :]
+        of_token = jnp.sum(jnp.where(kind == kinds, rank, 0.0), axis=0, keepdims=True)
+        pairs.append((p, jnp.where((of_token == wanted) & (times < len_ref[p]), 1.0, 0.0).astype(jnp.bfloat16)))
+    copies[1].wait()
+    for s, (p, chosen) in enumerate(pairs):
+        passage = tiles_ref[pl.ds(p, tokens, stride=held), :]
+        pieces = jnp.dot(chosen, jnp.concatenate(thirds(passage), axis=1), preferred_element_type=jnp.float32)
+        pay_ref[s * EXP:(s + 1) * EXP, :] = pieces[:, 2 * DIM:] + pieces[:, DIM:2 * DIM] + pieces[:, :DIM]
     per_tile = 8 // held
     row = iota((8, DIM), 0)
     limit = jnp.zeros((8, DIM), jnp.int32)
@@ -61,33 +91,6 @@
     tiles = tiles_ref[...].reshape(groups, 8, DIM)
     masked_ref[...] = jnp.where(token < limit[None], tiles, first[None]).reshape(groups * 8, DIM)
 
-    nearby = feedback_ref[...] - pos * held
-    number = (iota(nearby.shape, 0) * queries_n + iota(nearby.shape, 1)) * held + nearby
-    far = 1e9
-    key = jnp.where((nearby >= 0) & (nearby < held), number.astype(jnp.float32), far)
-    ranks = ranks_ref[...].astype(jnp.float32)
-    lane = iota(ranks.shape, 1)
-    pay_ref[:ASK_ROW, :] = jnp.zeros((ASK_ROW, DIM), jnp.float32)
-    ids = jnp.zeros((1, DIM), jnp.float32)
-    slot = iota((1, DIM), 1) // EXP
-    kinds = iota((NCENT, tokens), 0)
-    times = iota((EXP, tokens), 1)
-    wanted = iota((EXP, tokens), 0).astype(jnp.float32)
-    for s in range(FB):
-        best = jnp.min(key)
-        key = jnp.where(key > best, key, far)
-        whole = best.astype(jnp.int32)
-        p = whole % held
-        q = (whole // held) % queries_n
-        ids = jnp.where(slot == s, q.astype(jnp.float32), ids)
-        rank = jnp.sum(jnp.where(lane == q, ranks, 0.0), axis=1, keepdims=True)
-        kind = clusters_ref[pl.ds(p, 1), :]
-        of_token = jnp.sum(jnp.where(kind == kinds, rank, 0.0), axis=0, keepdims=True)
-        chosen = jnp.where((of_token == wanted) & (times < len_ref[p]), 1.0, 0.0)
-        passage = tiles_ref[pl.ds(p, tokens, stride=held), :]
-        pieces = jnp.dot(chosen.astype(jnp.bfloat16), jnp.concatenate(thirds(passage), axis=1),
-                         preferred_element_type=jnp.float32)
-        pay_ref[s * EXP:(s + 1) * EXP, :] = pieces[:, 2 * DIM:] + pieces[:, DIM:2 * DIM] + pieces[:, :DIM]
     pay_ref[ID_ROW:ID_ROW + 1, :] = ids
     for c, at in enumerate(range(0, queries_n, DIM)):
         width = min(DIM, queries_n - at)

time: 36.8 us -> 36.5 us (level)
  no operation moved by 1% of the time
where the time goes in v5:
time: 36.5 us; the launch traced here: 36.4 us
  starting transfers between devices  18.6 us (51%)
  waiting for transfers between devices  13.4 us (37%)
  Pallas kernels  3.78 us (10%)
  local copies, waits for them, and re-layouts  0.52 us (1%)
    ppermute x14, starting transfers between devices, swap(): return lax.ppermute(x, AXES, [(i, i ^ mask) for i in range(devices)])  18.6 us
    ppermute x14, waiting for transfers between devices, swap(): return lax.ppermute(x, AXES, [(i, i ^ mask) for i in range(devices)])  13.4 us
    pallas_call x4, Pallas kernels, call(): pl.pallas_call(kernel, out_shape=[pltpu.VMEM(o.shape, o.dtype) for o in o...  3.78 us
  transfers between devices with their start and end apart: 14, of which 7 were waited for; matrix products, arithmetic and copies ran while one was open for 0% of the time, Pallas kernels for 4%

profile of v5, /device:TPU:0, one launch (start us, length us, event | category | flops | bytes accessed | tf_op | source)
XLA Modules:
  0.0 36.4 jit_solution(1111370316410536095)
XLA Ops:
  0.0 0.0 copy-start
  0.0 1.4 %shard_map.82 = (f32[720,128]{1,0:T(8,128)S(1)}, f32[40,128]{1,0:T(8,128)S(1)}) custom-call(s32[1]{0:T(128)} %bitcast.pos_ref, s32[4]{0:T(128)} %refs_0_.1, f32[720,128]{1,0:T(8,128)} %bitcast.13, s32[4,180]{1,0:T(4,128)} %refs_2_.1, s32[3,32]{1,0:T(4,128)} %bitcast.15, s32[24,32]{1,0:T(8,128)} %bitcast.14, s32[2,32]{1,0:T(2,128)} %bitcast.16, s32[1,32]{1,0:T(1,128)} %bitcast.17), custom_call_target="tpu_custom_call" | custom-call | tf_op jit(solution)/shard_map/pallas_call | solution.py:264
  1.4 0.5 %collective-permute-start.2 = (f32[40,128]{1,0:T(8,128)S(1)}, f32[40,128]{1,0:T(8,128)S(1)}, u32[]{:S(2)}, u32[]{:S(2)}) collective-permute-start(f32[40,128]{1,0:T(8,128)S(1)} %get-tuple-element.24.refs_0_), channel_id=1, source_target_pairs={{0,1},{1,0},{2,3},{3,2},{4,5},{5,4},{6,7},{7,6},{8,9},{9,8},{10,11... | collective-permute-start | bytes 61448 | tf_op jit(solution)/shard_map/ppermute | solution.py:287
  1.9 0.0 copy-done
  1.9 2.7 %collective-permute-start = (f32[32,128]{1,0:T(8,128)S(1)}, f32[32,128]{1,0:T(8,128)S(1)}, u32[]{:S(2)}, u32[]{:S(2)}) collective-permute-start(f32[32,128]{1,0:T(8,128)S(1)} %bitcast.9), channel_id=1, source_target_pairs={{0,2},{1,3},{2,0},{3,1},{4,6},{5,7},{6,4},{7,5},{8,10},{9,11},{10,... | collective-permute-start | bytes 49160 | tf_op jit(solution)/shard_map/ppermute | solution.py:287
  4.6 0.0 collective-permute-done.2.refs_1_
  4.6 0.3 shard_map.83
  4.9 1.6 %collective-permute-start.3 = (f32[96,128]{1,0:T(8,128)S(1)}, f32[96,128]{1,0:T(8,128)S(1)}, u32[]{:S(2)}, u32[]{:S(2)}) collective-permute-start(f32[96,128]{1,0:T(8,128)S(1)} %get-tuple-element.26), channel_id=1, source_target_pairs={{0,8},{1,9},{2,10},{3,11},{4,12},{5,13},{6,14},{7,15},{8,0},{9,1},... | collective-permute-start | bytes 147464 | tf_op jit(solution)/shard_map/ppermute | solution.py:287
  6.5 0.0 collective-permute-done.refs_5_
  6.5 1.8 %collective-permute-start.6 = (f32[64,128]{1,0:T(8,128)S(1)}, f32[64,128]{1,0:T(8,128)S(1)}, u32[]{:S(2)}, u32[]{:S(2)}) collective-permute-start(f32[64,128]{1,0:T(8,128)S(1)} %pad_maximum_fusion.1), channel_id=1, source_target_pairs={{0,16},{1,17},{2,18},{3,19},{4,20},{5,21},{6,22},{7,23},{8,24},{9,... | collective-permute-start | bytes 98312 | tf_op jit(solution)/shard_map/ppermute | solution.py:287
  8.3 1.5 %collective-permute-start.1 = (f32[720,128]{1,0:T(8,128)S(1)}, f32[720,128]{1,0:T(8,128)S(1)}, u32[]{:S(2)}, u32[]{:S(2)}) collective-permute-start(f32[720,128]{1,0:T(8,128)S(1)} %get-tuple-element.23.refs_0_), channel_id=1, source_target_pairs={{0,8},{1,9},{2,10},{3,11},{4,12},{5,13},{6,14},{7,15},{8,0},{9,1},... | collective-permute-start | bytes 1105928 | tf_op jit(solution)/shard_map/ppermute | solution.py:287
  9.8 0.0 collective-permute-done.3.refs_9_
  9.8 2.7 %collective-permute-start.4 = (f32[80,128]{1,0:T(8,128)S(1)}, f32[80,128]{1,0:T(8,128)S(1)}, u32[]{:S(2)}, u32[]{:S(2)}) collective-permute-start(f32[80,128]{1,0:T(8,128)S(1)} %slice_add_fusion), channel_id=1, source_target_pairs={{0,4},{1,5},{2,6},{3,7},{4,0},{5,1},{6,2},{7,3},{8,12},{9,13},{10,... | collective-permute-start | bytes 122888 | tf_op jit(solution)/shard_map/ppermute | solution.py:287
  12.4 0.0 collective-permute-done.6.refs_6_
  12.4 0.8 %collective-permute-start.7 = (f32[128,128]{1,0:T(8,128)S(1)}, f32[128,128]{1,0:T(8,128)S(1)}, u32[]{:S(2)}, u32[]{:S(2)}) collective-permute-start(f32[128,128]{1,0:T(8,128)S(1)} %pad_maximum_fusion), channel_id=1, source_target_pairs={{0,4},{1,5},{2,6},{3,7},{4,0},{5,1},{6,2},{7,3},{8,12},{9,13},{10,... | collective-permute-start | bytes 196616 | tf_op jit(solution)/shard_map/ppermute | solution.py:287
  13.3 1.8 %collective-permute-done.4 = f32[80,128]{1,0:T(8,128)S(1)} collective-permute-done((f32[80,128]{1,0:T(8,128)S(1)}, f32[80,128]{1,0:T(8,128)S(1)}, u32[]{:S(2)}, u32[]{:S(2)}) %collective-permute-start.4) | collective-permute-done | bytes 40992 | tf_op jit(solution)/shard_map/ppermute | solution.py:287
  15.0 1.7 %collective-permute-start.5 = (f32[80,128]{1,0:T(8,128)S(1)}, f32[80,128]{1,0:T(8,128)S(1)}, u32[]{:S(2)}, u32[]{:S(2)}) collective-permute-start(f32[80,128]{1,0:T(8,128)S(1)} %add.32), channel_id=1, source_target_pairs={{0,2},{1,3},{2,0},{3,1},{4,6},{5,7},{6,4},{7,5},{8,10},{9,11},{10,... | collective-permute-start | bytes 122888 | tf_op jit(solution)/shard_map/ppermute | solution.py:287
  16.7 0.0 collective-permute-start.8
  16.7 2.3 %collective-permute-done.5 = f32[80,128]{1,0:T(8,128)S(1)} collective-permute-done((f32[80,128]{1,0:T(8,128)S(1)}, f32[80,128]{1,0:T(8,128)S(1)}, u32[]{:S(2)}, u32[]{:S(2)}) %collective-permute-start.5) | collective-permute-done | bytes 40992 | tf_op jit(solution)/shard_map/ppermute | solution.py:287
  19.1 0.0 collective-permute-done.7.refs_7_
  19.1 0.0 collective-permute-done.1.refs_1_
  19.1 0.1 collective-permute-start.9
  19.2 0.6 %collective-permute-start.10 = (f32[80,128]{1,0:T(8,128)S(1)}, f32[80,128]{1,0:T(8,128)S(1)}, u32[]{:S(2)}, u32[]{:S(2)}) collective-permute-start(f32[80,128]{1,0:T(8,128)S(1)} %add.33.refs_6_), channel_id=1, source_target_pairs={{0,16},{1,17},{2,18},{3,19},{4,20},{5,21},{6,22},{7,23},{8,24},{9,... | collective-permute-start | bytes 122888 | tf_op jit(solution)/shard_map/ppermute | solution.py:287
  19.8 0.0 collective-permute-done.8.refs_2_
  19.8 1.1 %collective-permute-done.9.refs_3_ = f32[720,128]{1,0:T(8,128)S(1)} collective-permute-done((f32[720,128]{1,0:T(8,128)S(1)}, f32[720,128]{1,0:T(8,128)S(1)}, u32[]{:S(2)}, u32[]{:S(2)}) %collective-permute-start.9) | collective-permute-done | bytes 368672 | tf_op jit(solution)/shard_map/ppermute | solution.py:287
  20.8 1.2 %shard_map.84 = (bf16[720,256]{1,0:T(8,128)(2,1)S(1)}, bf16[720,256]{1,0:T(8,128)(2,1)S(1)}, bf16[720,256]{1,0:T(8,128)(2,1)S(1)}, bf16[720,256]{1,0:T(8,128)(2,...) custom-call(s32[1]{0:T(128)} %bitcast.pos_ref, f32[720,128]{1,0:T(8,128)S(1)} %get-tuple-element.23.refs_0_, ...), custom_call_target="tpu_custom_call" | custom-call | tf_op jit(solution)/shard_map/pallas_call | solution.py:264
  22.0 1.2 %collective-permute-done.10.refs_7_ = f32[80,128]{1,0:T(8,128)S(1)} collective-permute-done((f32[80,128]{1,0:T(8,128)S(1)}, f32[80,128]{1,0:T(8,128)S(1)}, u32[]{:S(2)}, u32[]{:S(2)}) %collective-permute-start.10) | collective-permute-done | bytes 40992 | tf_op jit(solution)/shard_map/ppermute | solution.py:287
  23.2 0.9 %shard_map.85 = f32[8,64]{1,0:T(8,128)S(1)} custom-call(s32[1]{0:T(128)} %bitcast.pos_ref, bf16[720,256]{1,0:T(8,128)(2,1)S(1)} %get-tuple-element.32.refs_0_, bf16[720,256]{1,0:T(8,128)(2,1)S(1)} %get-tuple-element.33.refs_1_, bf16[720,256]{1,0:T(8,128)(2,1)S(1)} %get-tuple-element.34.refs_2_, bf16[720,256]{1,0:T(8,128)(2,1)S(1)} %get-tuple-element.35.refs_3_, ...), custom_call_target="tpu_custom_call" | custom-call | tf_op jit(solution)/shard_map/pallas_call | solution.py:264
  24.1 0.6 %collective-permute-start.11 = (f32[8,64]{1,0:T(8,128)S(1)}, f32[8,64]{1,0:T(8,128)S(1)}, u32[]{:S(2)}, u32[]{:S(2)}) collective-permute-start(f32[8,64]{1,0:T(8,128)S(1)} %shard_map.85), channel_id=1, source_target_pairs={{0,16},{1,17},{2,18},{3,19},{4,20},{5,21},{6,22},{7,23},{8,24},{9,... | collective-permute-start | bytes 6152 | tf_op jit(solution)/shard_map/ppermute | solution.py:287
  24.7 3.1 %collective-permute-done.11 = f32[8,64]{1,0:T(8,128)S(1)} collective-permute-done((f32[8,64]{1,0:T(8,128)S(1)}, f32[8,64]{1,0:T(8,128)S(1)}, u32[]{:S(2)}, u32[]{:S(2)}) %collective-permute-start.11) | collective-permute-done | bytes 2080 | tf_op jit(solution)/shard_map/ppermute | solution.py:287
  27.8 1.7 %collective-permute-start.12 = (f32[8,64]{1,0:T(8,128)S(1)}, f32[8,64]{1,0:T(8,128)S(1)}, u32[]{:S(2)}, u32[]{:S(2)}) collective-permute-start(f32[8,64]{1,0:T(8,128)S(1)} %add.34), channel_id=1, source_target_pairs={{0,2},{1,3},{2,0},{3,1},{4,6},{5,7},{6,4},{7,5},{8,10},{9,11},{10,... | collective-permute-start | bytes 6152 | tf_op jit(solution)/shard_map/ppermute | solution.py:287
  29.4 1.9 %collective-permute-done.12 = f32[8,64]{1,0:T(8,128)S(1)} collective-permute-done((f32[8,64]{1,0:T(8,128)S(1)}, f32[8,64]{1,0:T(8,128)S(1)}, u32[]{:S(2)}, u32[]{:S(2)}) %collective-permute-start.12) | collective-permute-done | bytes 2080 | tf_op jit(solution)/shard_map/ppermute | solution.py:287
  31.4 2.5 %collective-permute-start.13 = (f32[8,64]{1,0:T(8,128)S(1)}, f32[8,64]{1,0:T(8,128)S(1)}, u32[]{:S(2)}, u32[]{:S(2)}) collective-permute-start(f32[8,64]{1,0:T(8,128)S(1)} %add.35), channel_id=1, source_target_pairs={{0,4},{1,5},{2,6},{3,7},{4,0},{5,1},{6,2},{7,3},{8,12},{9,13},{10,... | collective-permute-start | bytes 6152 | tf_op jit(solution)/shard_map/ppermute | solution.py:287
  33.9 2.0 %collective-permute-done.13 = f32[8,64]{1,0:T(8,128)S(1)} collective-permute-done((f32[8,64]{1,0:T(8,128)S(1)}, f32[8,64]{1,0:T(8,128)S(1)}, u32[]{:S(2)}, u32[]{:S(2)}) %collective-permute-start.13) | collective-permute-done | bytes 2080 | tf_op jit(solution)/shard_map/ppermute | solution.py:287
  35.9 0.5 %constant_dynamic-slice_fusion = f32[1,64]{1,0:T(1,128)} fusion(f32[8,64]{1,0:T(8,128)S(1)} %add.36, s32[]{:T(128)S(6)} %select_n.16), kind=kLoop, calls=%fused_computation.3 | loop fusion | bytes 516 | tf_op jit(solution)/shard_map/dynamic_slice | solution.py:337
  (8 shorter events, 0.0 us)
Async XLA Ops:
  0.0 1.9 %copy-start = (f32[1,32,128]{2,1,0:T(8,128)S(1)}, f32[1,32,128]{2,1,0:T(8,128)}, u32[]{:S(2)}) copy-start(f32[1,32,128]{2,1,0:T(8,128)} %param.8) | copy-start | bytes 49156
  1.4 3.2 %collective-permute-start.2 = (f32[40,128]{1,0:T(8,128)S(1)}, f32[40,128]{1,0:T(8,128)S(1)}, u32[]{:S(2)}, u32[]{:S(2)}) collective-permute-start(f32[40,128]{1,0:T(8,128)S(1)} %get-tuple-element.24.refs_0_), channel_id=1, source_target_pairs={{0,1},{1,0},{2,3},{3,2},{4,5},{5,4},{6,7},{7,6},{8,9},{9,8},{10,11... | collective-permute-start | bytes 61448 | tf_op jit(solution)/shard_map/ppermute | solution.py:287
  1.9 4.5 %collective-permute-start = (f32[32,128]{1,0:T(8,128)S(1)}, f32[32,128]{1,0:T(8,128)S(1)}, u32[]{:S(2)}, u32[]{:S(2)}) collective-permute-start(f32[32,128]{1,0:T(8,128)S(1)} %bitcast.9), channel_id=1, source_target_pairs={{0,2},{1,3},{2,0},{3,1},{4,6},{5,7},{6,4},{7,5},{8,10},{9,11},{10,... | collective-permute-start | bytes 49160 | tf_op jit(solution)/shard_map/ppermute | solution.py:287
  4.9 4.9 %collective-permute-start.3 = (f32[96,128]{1,0:T(8,128)S(1)}, f32[96,128]{1,0:T(8,128)S(1)}, u32[]{:S(2)}, u32[]{:S(2)}) collective-permute-start(f32[96,128]{1,0:T(8,128)S(1)} %get-tuple-element.26), channel_id=1, source_target_pairs={{0,8},{1,9},{2,10},{3,11},{4,12},{5,13},{6,14},{7,15},{8,0},{9,1},... | collective-permute-start | bytes 147464 | tf_op jit(solution)/shard_map/ppermute | solution.py:287
  6.5 6.0 %collective-permute-start.6 = (f32[64,128]{1,0:T(8,128)S(1)}, f32[64,128]{1,0:T(8,128)S(1)}, u32[]{:S(2)}, u32[]{:S(2)}) collective-permute-start(f32[64,128]{1,0:T(8,128)S(1)} %pad_maximum_fusion.1), channel_id=1, source_target_pairs={{0,16},{1,17},{2,18},{3,19},{4,20},{5,21},{6,22},{7,23},{8,24},{9,... | collective-permute-start | bytes 98312 | tf_op jit(solution)/shard_map/ppermute | solution.py:287
  8.3 10.8 %collective-permute-start.1 = (f32[720,128]{1,0:T(8,128)S(1)}, f32[720,128]{1,0:T(8,128)S(1)}, u32[]{:S(2)}, u32[]{:S(2)}) collective-permute-start(f32[720,128]{1,0:T(8,128)S(1)} %get-tuple-element.23.refs_0_), channel_id=1, source_target_pairs={{0,8},{1,9},{2,10},{3,11},{4,12},{5,13},{6,14},{7,15},{8,0},{9,1},... | collective-permute-start | bytes 1105928 | tf_op jit(solution)/shard_map/ppermute | solution.py:287
  9.8 5.3 %collective-permute-start.4 = (f32[80,128]{1,0:T(8,128)S(1)}, f32[80,128]{1,0:T(8,128)S(1)}, u32[]{:S(2)}, u32[]{:S(2)}) collective-permute-start(f32[80,128]{1,0:T(8,128)S(1)} %slice_add_fusion), channel_id=1, source_target_pairs={{0,4},{1,5},{2,6},{3,7},{4,0},{5,1},{6,2},{7,3},{8,12},{9,13},{10,... | collective-permute-start | bytes 122888 | tf_op jit(solution)/shard_map/ppermute | solution.py:287
  12.4 6.6 %collective-permute-start.7 = (f32[128,128]{1,0:T(8,128)S(1)}, f32[128,128]{1,0:T(8,128)S(1)}, u32[]{:S(2)}, u32[]{:S(2)}) collective-permute-start(f32[128,128]{1,0:T(8,128)S(1)} %pad_maximum_fusion), channel_id=1, source_target_pairs={{0,4},{1,5},{2,6},{3,7},{4,0},{5,1},{6,2},{7,3},{8,12},{9,13},{10,... | collective-permute-start | bytes 196616 | tf_op jit(solution)/shard_map/ppermute | solution.py:287
  15.0 4.0 %collective-permute-start.5 = (f32[80,128]{1,0:T(8,128)S(1)}, f32[80,128]{1,0:T(8,128)S(1)}, u32[]{:S(2)}, u32[]{:S(2)}) collective-permute-start(f32[80,128]{1,0:T(8,128)S(1)} %add.32), channel_id=1, source_target_pairs={{0,2},{1,3},{2,0},{3,1},{4,6},{5,7},{6,4},{7,5},{8,10},{9,11},{10,... | collective-permute-start | bytes 122888 | tf_op jit(solution)/shard_map/ppermute | solution.py:287
  16.7 3.0 %collective-permute-start.8 = (f32[720,128]{1,0:T(8,128)S(1)}, f32[720,128]{1,0:T(8,128)S(1)}, u32[]{:S(2)}, u32[]{:S(2)}) collective-permute-start(f32[720,128]{1,0:T(8,128)S(1)} %get-tuple-element.23.refs_0_), channel_id=1, source_target_pairs={{0,1},{1,0},{2,3},{3,2},{4,5},{5,4},{6,7},{7,6},{8,9},{9,8},{10,11... | collective-permute-start | bytes 1105928 | tf_op jit(solution)/shard_map/ppermute | solution.py:287
  19.1 1.8 %collective-permute-start.9 = (f32[720,128]{1,0:T(8,128)S(1)}, f32[720,128]{1,0:T(8,128)S(1)}, u32[]{:S(2)}, u32[]{:S(2)}) collective-permute-start(f32[720,128]{1,0:T(8,128)S(1)} %collective-permute-done.1.refs_1_), channel_id=1, source_target_pairs={{0,1},{1,0},{2,3},{3,2},{4,5},{5,4},{6,7},{7,6},{8,9},{9,8},{10,11... | collective-permute-start | bytes 1105928 | tf_op jit(solution)/shard_map/ppermute | solution.py:287
  19.2 4.1 %collective-permute-start.10 = (f32[80,128]{1,0:T(8,128)S(1)}, f32[80,128]{1,0:T(8,128)S(1)}, u32[]{:S(2)}, u32[]{:S(2)}) collective-permute-start(f32[80,128]{1,0:T(8,128)S(1)} %add.33.refs_6_), channel_id=1, source_target_pairs={{0,16},{1,17},{2,18},{3,19},{4,20},{5,21},{6,22},{7,23},{8,24},{9,... | collective-permute-start | bytes 122888 | tf_op jit(solution)/shard_map/ppermute | solution.py:287
  24.1 3.6 %collective-permute-start.11 = (f32[8,64]{1,0:T(8,128)S(1)}, f32[8,64]{1,0:T(8,128)S(1)}, u32[]{:S(2)}, u32[]{:S(2)}) collective-permute-start(f32[8,64]{1,0:T(8,128)S(1)} %shard_map.85), channel_id=1, source_target_pairs={{0,16},{1,17},{2,18},{3,19},{4,20},{5,21},{6,22},{7,23},{8,24},{9,... | collective-permute-start | bytes 6152 | tf_op jit(solution)/shard_map/ppermute | solution.py:287
  27.8 3.6 %collective-permute-start.12 = (f32[8,64]{1,0:T(8,128)S(1)}, f32[8,64]{1,0:T(8,128)S(1)}, u32[]{:S(2)}, u32[]{:S(2)}) collective-permute-start(f32[8,64]{1,0:T(8,128)S(1)} %add.34), channel_id=1, source_target_pairs={{0,2},{1,3},{2,0},{3,1},{4,6},{5,7},{6,4},{7,5},{8,10},{9,11},{10,... | collective-permute-start | bytes 6152 | tf_op jit(solution)/shard_map/ppermute | solution.py:287
  31.4 4.5 %collective-permute-start.13 = (f32[8,64]{1,0:T(8,128)S(1)}, f32[8,64]{1,0:T(8,128)S(1)}, u32[]{:S(2)}, u32[]{:S(2)}) collective-permute-start(f32[8,64]{1,0:T(8,128)S(1)} %add.35), channel_id=1, source_target_pairs={{0,4},{1,5},{2,6},{3,7},{4,0},{5,1},{6,2},{7,3},{8,12},{9,13},{10,... | collective-permute-start | bytes 6152 | tf_op jit(solution)/shard_map/ppermute | solution.py:287

commit v6 on v5

--- a/solution.py
+++ b/solution.py
@@ -25,18 +25,26 @@
     return lax.broadcasted_iota(jnp.int32, shape, axis)
 
 
-def spread(index, masks):
+def spread(index, steps):
     total = 0
-    for k, mask in enumerate(masks):
-        total = total | (((index >> k) & 1) * mask)
+    for k, step in enumerate(steps):
+        total = total ^ (((index >> k) & 1) * step)
     return total
 
 
-def gather_bits(device, masks):
+def gather_bits(device, bits):
     total = 0
-    for k, mask in enumerate(masks):
-        total = total | (jnp.where((device & mask) != 0, 1, 0) << k)
+    for k, bit in enumerate(bits):
+        total = total | (jnp.where((device & bit) != 0, 1, 0) << k)
     return total
+
+
+def steps_of(bits):
+    return [bit | 1 for bit in bits]
+
+
+def owner_of(pos, index, bits):
+    return pos ^ spread(gather_bits(pos, bits) ^ index, steps_of(bits))
 
 
 def pairs_kernel(queries_n, held, tokens, pos_ref, *refs):
@@ -105,7 +113,7 @@
     half = (1 << len(outer)) * EXP
     rows = 2 * half
     row = iota((rows, DIM), 0)
-    owner = ((pos ^ ((row // half) * side)) & (1 | side)) | spread(row % half // EXP, outer)
+    owner = owner_of(pos, row % half // EXP, outer) ^ ((row // half) * side)
     owner = owner.astype(jnp.float32)
     places = [(pay, 0) for pay in pays]
     total = jnp.zeros((rows, DIM), jnp.float32)
@@ -183,17 +191,17 @@
         for i, (left, wide) in enumerate(lefts):
             parts[i].append(over_tokens(nt_dot(wide, twice) + nt_dot(left, low)))
     largest = largest_rows([jnp.concatenate(part, axis=1) for part in parts], held)
-    of_col = gather_bits(spread(iota((n_out, total), 1) // QL, asking), outer) ^ me_out
+    of_col = gather_bits(spread(iota((n_out, total), 1) // QL, steps_of(asking)), outer) ^ me_out
     member = jnp.where(of_col == iota((n_out, total), 0), 1.0 / QL, 0.0)
     values_ref[...] = nt_dot(member, largest, HIGHEST)
 
     cands = jnp.concatenate([keep_ref[half:, :], from_side_ref[half:, :]], axis=0)
     entries = cands.shape[0]
-    own = (pos & ~sum(outer)) | spread(iota((n_out, DIM), 0), outer)
+    own = owner_of(pos, iota((n_out, DIM), 0), outer)
     slots = chosen_ref.shape[1]
     slot = iota((entries, slots), 1)
     entry = iota((entries, slots), 0)
-    same = at_steps(pos, [0, 1, side, side | 1], slot // CAP, entry)
+    same = at_steps(pos, [0, 1, side, side ^ 1], slot // CAP, entry)
     local = jnp.zeros((n_out, slots), jnp.float32)
     count = jnp.zeros((n_out, slots), jnp.float32)
     for c, at in enumerate(range(0, queries_n, DIM)):
@@ -240,7 +248,7 @@
     shape = (n_tiles * 8, held * padded)
     entry = iota(shape, 0)
     col = iota(shape, 1)
-    same = at_steps(pos, [0, side, 1, side | 1], col % padded // CAP, entry) & (col % padded < slots)
+    same = at_steps(pos, [0, side, 1, side ^ 1], col % padded // CAP, entry) & (col % padded < slots)
     pick = jnp.where(same & (entry % 8 == col // padded), 1.0, 0.0).astype(jnp.bfloat16)
     found = jnp.dot(jnp.concatenate(thirds(values), axis=0), pick, preferred_element_type=jnp.float32)
     found = found[:n_out] + found[n_out:2 * n_out] + found[2 * n_out:]
@@ -276,7 +284,7 @@
     queries_n = feedback.shape[0]
     n_corpus = lax.axis_size("corpus")
     devices = lax.axis_size("query") * n_corpus
-    side, last = n_corpus, 2 * n_corpus
+    side, last = n_corpus | 1, 2 * n_corpus
     masks = [1 << k for k in range(devices.bit_length() - 1)]
     outer = [m for m in reversed(masks) if 1 < m < n_corpus] + [m for m in masks if m >= last]
     asking = outer[1:] + outer[:1]
@@ -310,14 +318,15 @@
     from_side = swap(send, side)
     sums = keep[:half] + from_side[:half]
     asks = [queries[0]]
-    for mask in asking:
-        asks = asks + [swap(joined(asks), mask)]
+    for step in steps_of(asking):
+        asks = asks + [swap(joined(asks), step)]
     masked, _ = lax.optimization_barrier((masked, asks[1]))
     far = swap(masked, side)
-    for mask in outer[:-1]:
-        sums = sums + swap(sums, mask)
+    steps = steps_of(outer)
+    for step in steps[:-1]:
+        sums = sums + swap(sums, step)
     far, sums, asks = lax.optimization_barrier((far, sums, asks))
-    came = swap(sums, outer[-1])
+    came = swap(sums, steps[-1])
     tiles = [masked, far]
     tiles = tiles + [swap(t, 1) for t in tiles]
     slots = devices * CAP
@@ -331,10 +340,9 @@
         functools.partial(score_kernel, side, outer, held, len(tiles)), [struct(n_out, slots)],
         pos, *tiles, values, chosen, sums, came,
     )
-    for mask in reversed(outer):
-        table = table + swap(table, mask)
-    mine = sum(jnp.where((pos[0] & mask) != 0, 1 << k, 0) for k, mask in enumerate(outer))
-    return lax.dynamic_slice(table, (mine, 0), (1, devices * CAP))
+    for step in reversed(steps):
+        table = table + swap(table, step)
+    return lax.dynamic_slice(table, (gather_bits(pos[0], outer), 0), (1, slots))
 
 
 def solution(mesh):

time: 36.5 us -> 34.4 us (0.942)
  waiting for transfers between devices: 13.4 us -> 7.63 us
  starting transfers between devices: 18.6 us -> 22.3 us
    ppermute x14, waiting for transfers between devices: 13.4 us -> 7.63 us  [swap(): return lax.ppermute(x, AXES, [(i, i ^ mask) for i in range(devices)])]
    ppermute x14, starting transfers between devices: 18.6 us -> 22.3 us  [swap(): return lax.ppermute(x, AXES, [(i, i ^ mask) for i in range(devices)])]
  transfers between devices with their start and end apart: 14 -> 14, of which waited for: 7 -> 8; matrix products, arithmetic and copies ran while one was open for 0% -> 0% of each run, Pallas kernels for 4% -> 4%
where the time goes in v6:
time: 34.4 us; the launch traced here: 34.3 us
  starting transfers between devices  22.3 us (65%)
  waiting for transfers between devices  7.63 us (22%)
  Pallas kernels  3.78 us (11%)
  local copies, waits for them, and re-layouts  0.52 us (2%)
    ppermute x14, starting transfers between devices, swap(): return lax.ppermute(x, AXES, [(i, i ^ mask) for i in range(devices)])  22.3 us
    ppermute x14, waiting for transfers between devices, swap(): return lax.ppermute(x, AXES, [(i, i ^ mask) for i in range(devices)])  7.63 us
    pallas_call x4, Pallas kernels, call(): pl.pallas_call(kernel, out_shape=[pltpu.VMEM(o.shape, o.dtype) for o in o...  3.78 us
  transfers between devices with their start and end apart: 14, of which 8 were waited for; matrix products, arithmetic and copies ran while one was open for 0% of the time, Pallas kernels for 4%

profile of v6, /device:TPU:0, one launch (start us, length us, event | category | flops | bytes accessed | tf_op | source)
XLA Modules:
  0.0 34.3 jit_solution(10900991773744076118)
XLA Ops:
  0.0 0.0 copy-start
  0.0 1.4 %shard_map.82 = (f32[720,128]{1,0:T(8,128)S(1)}, f32[40,128]{1,0:T(8,128)S(1)}) custom-call(s32[1]{0:T(128)} %bitcast.pos_ref, s32[4]{0:T(128)} %refs_0_.1, f32[720,128]{1,0:T(8,128)} %bitcast.13, s32[4,180]{1,0:T(4,128)} %refs_2_.1, s32[3,32]{1,0:T(4,128)} %bitcast.15, s32[24,32]{1,0:T(8,128)} %bitcast.14, s32[2,32]{1,0:T(2,128)} %bitcast.16, s32[1,32]{1,0:T(1,128)} %bitcast.17), custom_call_target="tpu_custom_call" | custom-call | tf_op jit(solution)/shard_map/pallas_call | solution.py:272
  1.4 0.5 %collective-permute-start.2 = (f32[40,128]{1,0:T(8,128)S(1)}, f32[40,128]{1,0:T(8,128)S(1)}, u32[]{:S(2)}, u32[]{:S(2)}) collective-permute-start(f32[40,128]{1,0:T(8,128)S(1)} %get-tuple-element.24.refs_0_), channel_id=1, source_target_pairs={{0,1},{1,0},{2,3},{3,2},{4,5},{5,4},{6,7},{7,6},{8,9},{9,8},{10,11... | collective-permute-start | bytes 61448 | tf_op jit(solution)/shard_map/ppermute | solution.py:295
  1.9 0.0 copy-done
  1.9 2.7 %collective-permute-start = (f32[32,128]{1,0:T(8,128)S(1)}, f32[32,128]{1,0:T(8,128)S(1)}, u32[]{:S(2)}, u32[]{:S(2)}) collective-permute-start(f32[32,128]{1,0:T(8,128)S(1)} %bitcast.9), channel_id=1, source_target_pairs={{0,3},{1,2},{2,1},{3,0},{4,7},{5,6},{6,5},{7,4},{8,11},{9,10},{10,... | collective-permute-start | bytes 49160 | tf_op jit(solution)/shard_map/ppermute | solution.py:295
  4.6 0.0 collective-permute-done.2.refs_1_
  4.6 0.3 shard_map.83
  5.0 1.2 %collective-permute-start.3 = (f32[96,128]{1,0:T(8,128)S(1)}, f32[96,128]{1,0:T(8,128)S(1)}, u32[]{:S(2)}, u32[]{:S(2)}) collective-permute-start(f32[96,128]{1,0:T(8,128)S(1)} %get-tuple-element.26), channel_id=1, source_target_pairs={{0,9},{1,8},{2,11},{3,10},{4,13},{5,12},{6,15},{7,14},{8,1},{9,0},... | collective-permute-start | bytes 147464 | tf_op jit(solution)/shard_map/ppermute | solution.py:295
  6.2 0.0 collective-permute-done.refs_5_
  6.2 1.6 %collective-permute-start.6 = (f32[64,128]{1,0:T(8,128)S(1)}, f32[64,128]{1,0:T(8,128)S(1)}, u32[]{:S(2)}, u32[]{:S(2)}) collective-permute-start(f32[64,128]{1,0:T(8,128)S(1)} %pad_maximum_fusion.1), channel_id=1, source_target_pairs={{0,17},{1,16},{2,19},{3,18},{4,21},{5,20},{6,23},{7,22},{8,25},{9,... | collective-permute-start | bytes 98312 | tf_op jit(solution)/shard_map/ppermute | solution.py:295
  7.8 1.2 %collective-permute-start.1 = (f32[720,128]{1,0:T(8,128)S(1)}, f32[720,128]{1,0:T(8,128)S(1)}, u32[]{:S(2)}, u32[]{:S(2)}) collective-permute-start(f32[720,128]{1,0:T(8,128)S(1)} %get-tuple-element.23.refs_0_), channel_id=1, source_target_pairs={{0,9},{1,8},{2,11},{3,10},{4,13},{5,12},{6,15},{7,14},{8,1},{9,0},... | collective-permute-start | bytes 1105928 | tf_op jit(solution)/shard_map/ppermute | solution.py:295
  8.9 0.0 collective-permute-done.3.refs_9_
  8.9 2.7 %collective-permute-start.4 = (f32[80,128]{1,0:T(8,128)S(1)}, f32[80,128]{1,0:T(8,128)S(1)}, u32[]{:S(2)}, u32[]{:S(2)}) collective-permute-start(f32[80,128]{1,0:T(8,128)S(1)} %slice_add_fusion), channel_id=1, source_target_pairs={{0,5},{1,4},{2,7},{3,6},{4,1},{5,0},{6,3},{7,2},{8,13},{9,12},{10,... | collective-permute-start | bytes 122888 | tf_op jit(solution)/shard_map/ppermute | solution.py:295
  11.6 0.0 collective-permute-done.6.refs_6_
  11.6 0.5 %collective-permute-start.7 = (f32[128,128]{1,0:T(8,128)S(1)}, f32[128,128]{1,0:T(8,128)S(1)}, u32[]{:S(2)}, u32[]{:S(2)}) collective-permute-start(f32[128,128]{1,0:T(8,128)S(1)} %pad_maximum_fusion), channel_id=1, source_target_pairs={{0,5},{1,4},{2,7},{3,6},{4,1},{5,0},{6,3},{7,2},{8,13},{9,12},{10,... | collective-permute-start | bytes 196616 | tf_op jit(solution)/shard_map/ppermute | solution.py:295
  12.2 1.4 %collective-permute-done.4 = f32[80,128]{1,0:T(8,128)S(1)} collective-permute-done((f32[80,128]{1,0:T(8,128)S(1)}, f32[80,128]{1,0:T(8,128)S(1)}, u32[]{:S(2)}, u32[]{:S(2)}) %collective-permute-start.4) | collective-permute-done | bytes 40992 | tf_op jit(solution)/shard_map/ppermute | solution.py:295
  13.6 2.6 %collective-permute-start.5 = (f32[80,128]{1,0:T(8,128)S(1)}, f32[80,128]{1,0:T(8,128)S(1)}, u32[]{:S(2)}, u32[]{:S(2)}) collective-permute-start(f32[80,128]{1,0:T(8,128)S(1)} %add.26), channel_id=1, source_target_pairs={{0,3},{1,2},{2,1},{3,0},{4,7},{5,6},{6,5},{7,4},{8,11},{9,10},{10,... | collective-permute-start | bytes 122888 | tf_op jit(solution)/shard_map/ppermute | solution.py:295
  16.2 0.8 %collective-permute-start.8 = (f32[720,128]{1,0:T(8,128)S(1)}, f32[720,128]{1,0:T(8,128)S(1)}, u32[]{:S(2)}, u32[]{:S(2)}) collective-permute-start(f32[720,128]{1,0:T(8,128)S(1)} %get-tuple-element.23.refs_0_), channel_id=1, source_target_pairs={{0,1},{1,0},{2,3},{3,2},{4,5},{5,4},{6,7},{7,6},{8,9},{9,8},{10,11... | collective-permute-start | bytes 1105928 | tf_op jit(solution)/shard_map/ppermute | solution.py:295
  16.9 1.1 %collective-permute-done.5 = f32[80,128]{1,0:T(8,128)S(1)} collective-permute-done((f32[80,128]{1,0:T(8,128)S(1)}, f32[80,128]{1,0:T(8,128)S(1)}, u32[]{:S(2)}, u32[]{:S(2)}) %collective-permute-start.5) | collective-permute-done | bytes 40992 | tf_op jit(solution)/shard_map/ppermute | solution.py:295
  18.1 0.1 collective-permute-done.7.refs_7_
  18.1 0.2 collective-permute-done.1.refs_1_
  18.4 0.4 %collective-permute-start.9 = (f32[720,128]{1,0:T(8,128)S(1)}, f32[720,128]{1,0:T(8,128)S(1)}, u32[]{:S(2)}, u32[]{:S(2)}) collective-permute-start(f32[720,128]{1,0:T(8,128)S(1)} %collective-permute-done.1.refs_1_), channel_id=1, source_target_pairs={{0,1},{1,0},{2,3},{3,2},{4,5},{5,4},{6,7},{7,6},{8,9},{9,8},{10,11... | collective-permute-start | bytes 1105928 | tf_op jit(solution)/shard_map/ppermute | solution.py:295
  18.7 1.7 %collective-permute-start.10 = (f32[80,128]{1,0:T(8,128)S(1)}, f32[80,128]{1,0:T(8,128)S(1)}, u32[]{:S(2)}, u32[]{:S(2)}) collective-permute-start(f32[80,128]{1,0:T(8,128)S(1)} %add.27.refs_6_), channel_id=1, source_target_pairs={{0,17},{1,16},{2,19},{3,18},{4,21},{5,20},{6,23},{7,22},{8,25},{9,... | collective-permute-start | bytes 122888 | tf_op jit(solution)/shard_map/ppermute | solution.py:295
  20.4 0.0 collective-permute-done.8.refs_2_
  20.4 0.0 collective-permute-done.9.refs_3_
  20.5 1.2 %shard_map.84 = (bf16[720,256]{1,0:T(8,128)(2,1)S(1)}, bf16[720,256]{1,0:T(8,128)(2,1)S(1)}, bf16[720,256]{1,0:T(8,128)(2,1)S(1)}, bf16[720,256]{1,0:T(8,128)(2,...) custom-call(s32[1]{0:T(128)} %bitcast.pos_ref, f32[720,128]{1,0:T(8,128)S(1)} %get-tuple-element.23.refs_0_, ...), custom_call_target="tpu_custom_call" | custom-call | tf_op jit(solution)/shard_map/pallas_call | solution.py:272
  21.6 0.7 %collective-permute-done.10.refs_7_ = f32[80,128]{1,0:T(8,128)S(1)} collective-permute-done((f32[80,128]{1,0:T(8,128)S(1)}, f32[80,128]{1,0:T(8,128)S(1)}, u32[]{:S(2)}, u32[]{:S(2)}) %collective-permute-start.10) | collective-permute-done | bytes 40992 | tf_op jit(solution)/shard_map/ppermute | solution.py:295
  22.3 0.9 %shard_map.85 = f32[8,64]{1,0:T(8,128)S(1)} custom-call(s32[1]{0:T(128)} %bitcast.pos_ref, bf16[720,256]{1,0:T(8,128)(2,1)S(1)} %get-tuple-element.32.refs_0_, bf16[720,256]{1,0:T(8,128)(2,1)S(1)} %get-tuple-element.33.refs_1_, bf16[720,256]{1,0:T(8,128)(2,1)S(1)} %get-tuple-element.34.refs_2_, bf16[720,256]{1,0:T(8,128)(2,1)S(1)} %get-tuple-element.35.refs_3_, ...), custom_call_target="tpu_custom_call" | custom-call | tf_op jit(solution)/shard_map/pallas_call | solution.py:272
  23.2 1.6 %collective-permute-start.11 = (f32[8,64]{1,0:T(8,128)S(1)}, f32[8,64]{1,0:T(8,128)S(1)}, u32[]{:S(2)}, u32[]{:S(2)}) collective-permute-start(f32[8,64]{1,0:T(8,128)S(1)} %shard_map.85), channel_id=1, source_target_pairs={{0,17},{1,16},{2,19},{3,18},{4,21},{5,20},{6,23},{7,22},{8,25},{9,... | collective-permute-start | bytes 6152 | tf_op jit(solution)/shard_map/ppermute | solution.py:295
  24.8 1.4 %collective-permute-done.11 = f32[8,64]{1,0:T(8,128)S(1)} collective-permute-done((f32[8,64]{1,0:T(8,128)S(1)}, f32[8,64]{1,0:T(8,128)S(1)}, u32[]{:S(2)}, u32[]{:S(2)}) %collective-permute-start.11) | collective-permute-done | bytes 2080 | tf_op jit(solution)/shard_map/ppermute | solution.py:295
  26.2 2.0 %collective-permute-start.12 = (f32[8,64]{1,0:T(8,128)S(1)}, f32[8,64]{1,0:T(8,128)S(1)}, u32[]{:S(2)}, u32[]{:S(2)}) collective-permute-start(f32[8,64]{1,0:T(8,128)S(1)} %add.28), channel_id=1, source_target_pairs={{0,3},{1,2},{2,1},{3,0},{4,7},{5,6},{6,5},{7,4},{8,11},{9,10},{10,... | collective-permute-start | bytes 6152 | tf_op jit(solution)/shard_map/ppermute | solution.py:295
  28.2 1.3 %collective-permute-done.12 = f32[8,64]{1,0:T(8,128)S(1)} collective-permute-done((f32[8,64]{1,0:T(8,128)S(1)}, f32[8,64]{1,0:T(8,128)S(1)}, u32[]{:S(2)}, u32[]{:S(2)}) %collective-permute-start.12) | collective-permute-done | bytes 2080 | tf_op jit(solution)/shard_map/ppermute | solution.py:295
  29.6 2.8 %collective-permute-start.13 = (f32[8,64]{1,0:T(8,128)S(1)}, f32[8,64]{1,0:T(8,128)S(1)}, u32[]{:S(2)}, u32[]{:S(2)}) collective-permute-start(f32[8,64]{1,0:T(8,128)S(1)} %add.29), channel_id=1, source_target_pairs={{0,5},{1,4},{2,7},{3,6},{4,1},{5,0},{6,3},{7,2},{8,13},{9,12},{10,... | collective-permute-start | bytes 6152 | tf_op jit(solution)/shard_map/ppermute | solution.py:295
  32.4 1.3 %collective-permute-done.13 = f32[8,64]{1,0:T(8,128)S(1)} collective-permute-done((f32[8,64]{1,0:T(8,128)S(1)}, f32[8,64]{1,0:T(8,128)S(1)}, u32[]{:S(2)}, u32[]{:S(2)}) %collective-permute-start.13) | collective-permute-done | bytes 2080 | tf_op jit(solution)/shard_map/ppermute | solution.py:295
  33.8 0.5 %constant_dynamic-slice_fusion = f32[1,64]{1,0:T(1,128)} fusion(f32[8,64]{1,0:T(8,128)S(1)} %add.30, s32[]{:T(128)S(6)} %select_n.16), kind=kLoop, calls=%fused_computation.3 | loop fusion | bytes 516 | tf_op jit(solution)/shard_map/dynamic_slice | solution.py:345
  (8 shorter events, 0.0 us)
Async XLA Ops:
  0.0 1.9 %copy-start = (f32[1,32,128]{2,1,0:T(8,128)S(1)}, f32[1,32,128]{2,1,0:T(8,128)}, u32[]{:S(2)}) copy-start(f32[1,32,128]{2,1,0:T(8,128)} %param.8) | copy-start | bytes 49156
  1.4 3.2 %collective-permute-start.2 = (f32[40,128]{1,0:T(8,128)S(1)}, f32[40,128]{1,0:T(8,128)S(1)}, u32[]{:S(2)}, u32[]{:S(2)}) collective-permute-start(f32[40,128]{1,0:T(8,128)S(1)} %get-tuple-element.24.refs_0_), channel_id=1, source_target_pairs={{0,1},{1,0},{2,3},{3,2},{4,5},{5,4},{6,7},{7,6},{8,9},{9,8},{10,11... | collective-permute-start | bytes 61448 | tf_op jit(solution)/shard_map/ppermute | solution.py:295
  1.9 4.3 %collective-permute-start = (f32[32,128]{1,0:T(8,128)S(1)}, f32[32,128]{1,0:T(8,128)S(1)}, u32[]{:S(2)}, u32[]{:S(2)}) collective-permute-start(f32[32,128]{1,0:T(8,128)S(1)} %bitcast.9), channel_id=1, source_target_pairs={{0,3},{1,2},{2,1},{3,0},{4,7},{5,6},{6,5},{7,4},{8,11},{9,10},{10,... | collective-permute-start | bytes 49160 | tf_op jit(solution)/shard_map/ppermute | solution.py:295
  5.0 4.0 %collective-permute-start.3 = (f32[96,128]{1,0:T(8,128)S(1)}, f32[96,128]{1,0:T(8,128)S(1)}, u32[]{:S(2)}, u32[]{:S(2)}) collective-permute-start(f32[96,128]{1,0:T(8,128)S(1)} %get-tuple-element.26), channel_id=1, source_target_pairs={{0,9},{1,8},{2,11},{3,10},{4,13},{5,12},{6,15},{7,14},{8,1},{9,0},... | collective-permute-start | bytes 147464 | tf_op jit(solution)/shard_map/ppermute | solution.py:295
  6.2 5.4 %collective-permute-start.6 = (f32[64,128]{1,0:T(8,128)S(1)}, f32[64,128]{1,0:T(8,128)S(1)}, u32[]{:S(2)}, u32[]{:S(2)}) collective-permute-start(f32[64,128]{1,0:T(8,128)S(1)} %pad_maximum_fusion.1), channel_id=1, source_target_pairs={{0,17},{1,16},{2,19},{3,18},{4,21},{5,20},{6,23},{7,22},{8,25},{9,... | collective-permute-start | bytes 98312 | tf_op jit(solution)/shard_map/ppermute | solution.py:295
  7.8 10.6 %collective-permute-start.1 = (f32[720,128]{1,0:T(8,128)S(1)}, f32[720,128]{1,0:T(8,128)S(1)}, u32[]{:S(2)}, u32[]{:S(2)}) collective-permute-start(f32[720,128]{1,0:T(8,128)S(1)} %get-tuple-element.23.refs_0_), channel_id=1, source_target_pairs={{0,9},{1,8},{2,11},{3,10},{4,13},{5,12},{6,15},{7,14},{8,1},{9,0},... | collective-permute-start | bytes 1105928 | tf_op jit(solution)/shard_map/ppermute | solution.py:295
  8.9 4.7 %collective-permute-start.4 = (f32[80,128]{1,0:T(8,128)S(1)}, f32[80,128]{1,0:T(8,128)S(1)}, u32[]{:S(2)}, u32[]{:S(2)}) collective-permute-start(f32[80,128]{1,0:T(8,128)S(1)} %slice_add_fusion), channel_id=1, source_target_pairs={{0,5},{1,4},{2,7},{3,6},{4,1},{5,0},{6,3},{7,2},{8,13},{9,12},{10,... | collective-permute-start | bytes 122888 | tf_op jit(solution)/shard_map/ppermute | solution.py:295
  11.6 6.5 %collective-permute-start.7 = (f32[128,128]{1,0:T(8,128)S(1)}, f32[128,128]{1,0:T(8,128)S(1)}, u32[]{:S(2)}, u32[]{:S(2)}) collective-permute-start(f32[128,128]{1,0:T(8,128)S(1)} %pad_maximum_fusion), channel_id=1, source_target_pairs={{0,5},{1,4},{2,7},{3,6},{4,1},{5,0},{6,3},{7,2},{8,13},{9,12},{10,... | collective-permute-start | bytes 196616 | tf_op jit(solution)/shard_map/ppermute | solution.py:295
  13.6 4.5 %collective-permute-start.5 = (f32[80,128]{1,0:T(8,128)S(1)}, f32[80,128]{1,0:T(8,128)S(1)}, u32[]{:S(2)}, u32[]{:S(2)}) collective-permute-start(f32[80,128]{1,0:T(8,128)S(1)} %add.26), channel_id=1, source_target_pairs={{0,3},{1,2},{2,1},{3,0},{4,7},{5,6},{6,5},{7,4},{8,11},{9,10},{10,... | collective-permute-start | bytes 122888 | tf_op jit(solution)/shard_map/ppermute | solution.py:295
  16.2 4.3 %collective-permute-start.8 = (f32[720,128]{1,0:T(8,128)S(1)}, f32[720,128]{1,0:T(8,128)S(1)}, u32[]{:S(2)}, u32[]{:S(2)}) collective-permute-start(f32[720,128]{1,0:T(8,128)S(1)} %get-tuple-element.23.refs_0_), channel_id=1, source_target_pairs={{0,1},{1,0},{2,3},{3,2},{4,5},{5,4},{6,7},{7,6},{8,9},{9,8},{10,11... | collective-permute-start | bytes 1105928 | tf_op jit(solution)/shard_map/ppermute | solution.py:295
  18.4 2.1 %collective-permute-start.9 = (f32[720,128]{1,0:T(8,128)S(1)}, f32[720,128]{1,0:T(8,128)S(1)}, u32[]{:S(2)}, u32[]{:S(2)}) collective-permute-start(f32[720,128]{1,0:T(8,128)S(1)} %collective-permute-done.1.refs_1_), channel_id=1, source_target_pairs={{0,1},{1,0},{2,3},{3,2},{4,5},{5,4},{6,7},{7,6},{8,9},{9,8},{10,11... | collective-permute-start | bytes 1105928 | tf_op jit(solution)/shard_map/ppermute | solution.py:295
  18.7 3.5 %collective-permute-start.10 = (f32[80,128]{1,0:T(8,128)S(1)}, f32[80,128]{1,0:T(8,128)S(1)}, u32[]{:S(2)}, u32[]{:S(2)}) collective-permute-start(f32[80,128]{1,0:T(8,128)S(1)} %add.27.refs_6_), channel_id=1, source_target_pairs={{0,17},{1,16},{2,19},{3,18},{4,21},{5,20},{6,23},{7,22},{8,25},{9,... | collective-permute-start | bytes 122888 | tf_op jit(solution)/shard_map/ppermute | solution.py:295
  23.2 3.0 %collective-permute-start.11 = (f32[8,64]{1,0:T(8,128)S(1)}, f32[8,64]{1,0:T(8,128)S(1)}, u32[]{:S(2)}, u32[]{:S(2)}) collective-permute-start(f32[8,64]{1,0:T(8,128)S(1)} %shard_map.85), channel_id=1, source_target_pairs={{0,17},{1,16},{2,19},{3,18},{4,21},{5,20},{6,23},{7,22},{8,25},{9,... | collective-permute-start | bytes 6152 | tf_op jit(solution)/shard_map/ppermute | solution.py:295
  26.2 3.3 %collective-permute-start.12 = (f32[8,64]{1,0:T(8,128)S(1)}, f32[8,64]{1,0:T(8,128)S(1)}, u32[]{:S(2)}, u32[]{:S(2)}) collective-permute-start(f32[8,64]{1,0:T(8,128)S(1)} %add.28), channel_id=1, source_target_pairs={{0,3},{1,2},{2,1},{3,0},{4,7},{5,6},{6,5},{7,4},{8,11},{9,10},{10,... | collective-permute-start | bytes 6152 | tf_op jit(solution)/shard_map/ppermute | solution.py:295
  29.6 4.2 %collective-permute-start.13 = (f32[8,64]{1,0:T(8,128)S(1)}, f32[8,64]{1,0:T(8,128)S(1)}, u32[]{:S(2)}, u32[]{:S(2)}) collective-permute-start(f32[8,64]{1,0:T(8,128)S(1)} %add.29), channel_id=1, source_target_pairs={{0,5},{1,4},{2,7},{3,6},{4,1},{5,0},{6,3},{7,2},{8,13},{9,12},{10,... | collective-permute-start | bytes 6152 | tf_op jit(solution)/shard_map/ppermute | solution.py:295

commit v7 on v6

--- a/solution.py
+++ b/solution.py
@@ -286,8 +286,8 @@
     devices = lax.axis_size("query") * n_corpus
     side, last = n_corpus | 1, 2 * n_corpus
     masks = [1 << k for k in range(devices.bit_length() - 1)]
-    outer = [m for m in reversed(masks) if 1 < m < n_corpus] + [m for m in masks if m >= last]
-    asking = outer[1:] + outer[:1]
+    outer = [m for m in masks if m >= last] + [m for m in reversed(masks) if 1 < m < n_corpus]
+    asking = outer[-1:] + outer[:-1]
     n_out = 1 << len(outer)
     pos = lax.axis_index(AXES).astype(jnp.int32).reshape(1)
 

time: 34.4 us -> 33.6 us (0.977)
  starting transfers between devices: 22.3 us -> 20 us
  waiting for transfers between devices: 7.63 us -> 9.1 us
    ppermute x14, starting transfers between devices: 22.3 us -> 20 us  [swap(): return lax.ppermute(x, AXES, [(i, i ^ mask) for i in range(devices)])]
    ppermute x14, waiting for transfers between devices: 7.63 us -> 9.1 us  [swap(): return lax.ppermute(x, AXES, [(i, i ^ mask) for i in range(devices)])]
  transfers between devices with their start and end apart: 14 -> 14, of which waited for: 8 -> 6; matrix products, arithmetic and copies ran while one was open for 0% -> 0% of each run, Pallas kernels for 4% -> 4%
where the time goes in v7:
time: 33.6 us; the launch traced here: 33.5 us
  starting transfers between devices  20 us (60%)
  waiting for transfers between devices  9.1 us (27%)
  Pallas kernels  3.78 us (11%)
  local copies, waits for them, and re-layouts  0.52 us (2%)
    ppermute x14, starting transfers between devices, swap(): return lax.ppermute(x, AXES, [(i, i ^ mask) for i in range(devices)])  20 us
    ppermute x14, waiting for transfers between devices, swap(): return lax.ppermute(x, AXES, [(i, i ^ mask) for i in range(devices)])  9.1 us
    pallas_call x4, Pallas kernels, call(): pl.pallas_call(kernel, out_shape=[pltpu.VMEM(o.shape, o.dtype) for o in o...  3.78 us
  transfers between devices with their start and end apart: 14, of which 6 were waited for; matrix products, arithmetic and copies ran while one was open for 0% of the time, Pallas kernels for 4%

profile of v7, /device:TPU:0, one launch (start us, length us, event | category | flops | bytes accessed | tf_op | source)
XLA Modules:
  0.0 33.5 jit_solution(17474289192700642216)
XLA Ops:
  0.0 0.0 copy-start
  0.0 1.4 %shard_map.82 = (f32[720,128]{1,0:T(8,128)S(1)}, f32[40,128]{1,0:T(8,128)S(1)}) custom-call(s32[1]{0:T(128)} %bitcast.pos_ref, s32[4]{0:T(128)} %refs_0_.1, f32[720,128]{1,0:T(8,128)} %bitcast.13, s32[4,180]{1,0:T(4,128)} %refs_2_.1, s32[3,32]{1,0:T(4,128)} %bitcast.15, s32[24,32]{1,0:T(8,128)} %bitcast.14, s32[2,32]{1,0:T(2,128)} %bitcast.16, s32[1,32]{1,0:T(1,128)} %bitcast.17), custom_call_target="tpu_custom_call" | custom-call | tf_op jit(solution)/shard_map/pallas_call | solution.py:272
  1.4 0.5 %collective-permute-start.2 = (f32[40,128]{1,0:T(8,128)S(1)}, f32[40,128]{1,0:T(8,128)S(1)}, u32[]{:S(2)}, u32[]{:S(2)}) collective-permute-start(f32[40,128]{1,0:T(8,128)S(1)} %get-tuple-element.24.refs_0_), channel_id=1, source_target_pairs={{0,1},{1,0},{2,3},{3,2},{4,5},{5,4},{6,7},{7,6},{8,9},{9,8},{10,11... | collective-permute-start | bytes 61448 | tf_op jit(solution)/shard_map/ppermute | solution.py:295
  1.9 0.0 copy-done
  1.9 2.7 %collective-permute-start = (f32[32,128]{1,0:T(8,128)S(1)}, f32[32,128]{1,0:T(8,128)S(1)}, u32[]{:S(2)}, u32[]{:S(2)}) collective-permute-start(f32[32,128]{1,0:T(8,128)S(1)} %bitcast.9), channel_id=1, source_target_pairs={{0,3},{1,2},{2,1},{3,0},{4,7},{5,6},{6,5},{7,4},{8,11},{9,10},{10,... | collective-permute-start | bytes 49160 | tf_op jit(solution)/shard_map/ppermute | solution.py:295
  4.6 0.0 collective-permute-done.2.refs_1_
  4.6 0.3 shard_map.83
  5.0 1.2 %collective-permute-start.3 = (f32[96,128]{1,0:T(8,128)S(1)}, f32[96,128]{1,0:T(8,128)S(1)}, u32[]{:S(2)}, u32[]{:S(2)}) collective-permute-start(f32[96,128]{1,0:T(8,128)S(1)} %get-tuple-element.26), channel_id=1, source_target_pairs={{0,9},{1,8},{2,11},{3,10},{4,13},{5,12},{6,15},{7,14},{8,1},{9,0},... | collective-permute-start | bytes 147464 | tf_op jit(solution)/shard_map/ppermute | solution.py:295
  6.2 0.0 collective-permute-done.refs_5_
  6.2 1.6 %collective-permute-start.6 = (f32[64,128]{1,0:T(8,128)S(1)}, f32[64,128]{1,0:T(8,128)S(1)}, u32[]{:S(2)}, u32[]{:S(2)}) collective-permute-start(f32[64,128]{1,0:T(8,128)S(1)} %pad_maximum_fusion.1), channel_id=1, source_target_pairs={{0,17},{1,16},{2,19},{3,18},{4,21},{5,20},{6,23},{7,22},{8,25},{9,... | collective-permute-start | bytes 98312 | tf_op jit(solution)/shard_map/ppermute | solution.py:295
  7.8 1.2 %collective-permute-start.1 = (f32[720,128]{1,0:T(8,128)S(1)}, f32[720,128]{1,0:T(8,128)S(1)}, u32[]{:S(2)}, u32[]{:S(2)}) collective-permute-start(f32[720,128]{1,0:T(8,128)S(1)} %get-tuple-element.23.refs_0_), channel_id=1, source_target_pairs={{0,9},{1,8},{2,11},{3,10},{4,13},{5,12},{6,15},{7,14},{8,1},{9,0},... | collective-permute-start | bytes 1105928 | tf_op jit(solution)/shard_map/ppermute | solution.py:295
  8.9 0.0 collective-permute-done.3.refs_9_
  8.9 1.1 %collective-permute-start.4 = (f32[80,128]{1,0:T(8,128)S(1)}, f32[80,128]{1,0:T(8,128)S(1)}, u32[]{:S(2)}, u32[]{:S(2)}) collective-permute-start(f32[80,128]{1,0:T(8,128)S(1)} %slice_add_fusion), channel_id=1, source_target_pairs={{0,17},{1,16},{2,19},{3,18},{4,21},{5,20},{6,23},{7,22},{8,25},{9,... | collective-permute-start | bytes 122888 | tf_op jit(solution)/shard_map/ppermute | solution.py:295
  10.1 0.0 collective-permute-done.6.refs_6_
  10.1 2.7 %collective-permute-start.7 = (f32[128,128]{1,0:T(8,128)S(1)}, f32[128,128]{1,0:T(8,128)S(1)}, u32[]{:S(2)}, u32[]{:S(2)}) collective-permute-start(f32[128,128]{1,0:T(8,128)S(1)} %pad_maximum_fusion), channel_id=1, source_target_pairs={{0,5},{1,4},{2,7},{3,6},{4,1},{5,0},{6,3},{7,2},{8,13},{9,12},{10,... | collective-permute-start | bytes 196616 | tf_op jit(solution)/shard_map/ppermute | solution.py:295
  12.8 0.0 collective-permute-done.4
  12.8 2.6 %collective-permute-start.5 = (f32[80,128]{1,0:T(8,128)S(1)}, f32[80,128]{1,0:T(8,128)S(1)}, u32[]{:S(2)}, u32[]{:S(2)}) collective-permute-start(f32[80,128]{1,0:T(8,128)S(1)} %add.26), channel_id=1, source_target_pairs={{0,5},{1,4},{2,7},{3,6},{4,1},{5,0},{6,3},{7,2},{8,13},{9,12},{10,... | collective-permute-start | bytes 122888 | tf_op jit(solution)/shard_map/ppermute | solution.py:295
  15.4 0.0 collective-permute-start.8
  15.4 2.0 %collective-permute-done.5 = f32[80,128]{1,0:T(8,128)S(1)} collective-permute-done((f32[80,128]{1,0:T(8,128)S(1)}, f32[80,128]{1,0:T(8,128)S(1)}, u32[]{:S(2)}, u32[]{:S(2)}) %collective-permute-start.5) | collective-permute-done | bytes 40992 | tf_op jit(solution)/shard_map/ppermute | solution.py:295
  17.4 0.0 collective-permute-done.7.refs_7_
  17.4 1.0 %collective-permute-done.1.refs_1_ = f32[720,128]{1,0:T(8,128)S(1)} collective-permute-done((f32[720,128]{1,0:T(8,128)S(1)}, f32[720,128]{1,0:T(8,128)S(1)}, u32[]{:S(2)}, u32[]{:S(2)}) %collective-permute-start.1) | collective-permute-done | bytes 368672 | tf_op jit(solution)/shard_map/ppermute | solution.py:295
  18.4 0.1 collective-permute-start.9
  18.5 1.6 %collective-permute-start.10 = (f32[80,128]{1,0:T(8,128)S(1)}, f32[80,128]{1,0:T(8,128)S(1)}, u32[]{:S(2)}, u32[]{:S(2)}) collective-permute-start(f32[80,128]{1,0:T(8,128)S(1)} %add.27.refs_6_), channel_id=1, source_target_pairs={{0,3},{1,2},{2,1},{3,0},{4,7},{5,6},{6,5},{7,4},{8,11},{9,10},{10,... | collective-permute-start | bytes 122888 | tf_op jit(solution)/shard_map/ppermute | solution.py:295
  20.1 0.0 collective-permute-done.8.refs_2_
  20.1 0.0 collective-permute-done.9.refs_3_
  20.1 1.2 %shard_map.84 = (bf16[720,256]{1,0:T(8,128)(2,1)S(1)}, bf16[720,256]{1,0:T(8,128)(2,1)S(1)}, bf16[720,256]{1,0:T(8,128)(2,1)S(1)}, bf16[720,256]{1,0:T(8,128)(2,...) custom-call(s32[1]{0:T(128)} %bitcast.pos_ref, f32[720,128]{1,0:T(8,128)S(1)} %get-tuple-element.23.refs_0_, ...), custom_call_target="tpu_custom_call" | custom-call | tf_op jit(solution)/shard_map/pallas_call | solution.py:272
  21.2 0.7 %collective-permute-done.10.refs_7_ = f32[80,128]{1,0:T(8,128)S(1)} collective-permute-done((f32[80,128]{1,0:T(8,128)S(1)}, f32[80,128]{1,0:T(8,128)S(1)}, u32[]{:S(2)}, u32[]{:S(2)}) %collective-permute-start.10) | collective-permute-done | bytes 40992 | tf_op jit(solution)/shard_map/ppermute | solution.py:295
  22.0 0.9 %shard_map.85 = f32[8,64]{1,0:T(8,128)S(1)} custom-call(s32[1]{0:T(128)} %bitcast.pos_ref, bf16[720,256]{1,0:T(8,128)(2,1)S(1)} %get-tuple-element.32.refs_0_, bf16[720,256]{1,0:T(8,128)(2,1)S(1)} %get-tuple-element.33.refs_1_, bf16[720,256]{1,0:T(8,128)(2,1)S(1)} %get-tuple-element.34.refs_2_, bf16[720,256]{1,0:T(8,128)(2,1)S(1)} %get-tuple-element.35.refs_3_, ...), custom_call_target="tpu_custom_call" | custom-call | tf_op jit(solution)/shard_map/pallas_call | solution.py:272
  22.9 1.5 %collective-permute-start.11 = (f32[8,64]{1,0:T(8,128)S(1)}, f32[8,64]{1,0:T(8,128)S(1)}, u32[]{:S(2)}, u32[]{:S(2)}) collective-permute-start(f32[8,64]{1,0:T(8,128)S(1)} %shard_map.85), channel_id=1, source_target_pairs={{0,3},{1,2},{2,1},{3,0},{4,7},{5,6},{6,5},{7,4},{8,11},{9,10},{10,... | collective-permute-start | bytes 6152 | tf_op jit(solution)/shard_map/ppermute | solution.py:295
  24.4 1.5 %collective-permute-done.11 = f32[8,64]{1,0:T(8,128)S(1)} collective-permute-done((f32[8,64]{1,0:T(8,128)S(1)}, f32[8,64]{1,0:T(8,128)S(1)}, u32[]{:S(2)}, u32[]{:S(2)}) %collective-permute-start.11) | collective-permute-done | bytes 2080 | tf_op jit(solution)/shard_map/ppermute | solution.py:295
  26.0 2.5 %collective-permute-start.12 = (f32[8,64]{1,0:T(8,128)S(1)}, f32[8,64]{1,0:T(8,128)S(1)}, u32[]{:S(2)}, u32[]{:S(2)}) collective-permute-start(f32[8,64]{1,0:T(8,128)S(1)} %add.28), channel_id=1, source_target_pairs={{0,5},{1,4},{2,7},{3,6},{4,1},{5,0},{6,3},{7,2},{8,13},{9,12},{10,... | collective-permute-start | bytes 6152 | tf_op jit(solution)/shard_map/ppermute | solution.py:295
  28.5 1.4 %collective-permute-done.12 = f32[8,64]{1,0:T(8,128)S(1)} collective-permute-done((f32[8,64]{1,0:T(8,128)S(1)}, f32[8,64]{1,0:T(8,128)S(1)}, u32[]{:S(2)}, u32[]{:S(2)}) %collective-permute-start.12) | collective-permute-done | bytes 2080 | tf_op jit(solution)/shard_map/ppermute | solution.py:295
  29.9 0.6 %collective-permute-start.13 = (f32[8,64]{1,0:T(8,128)S(1)}, f32[8,64]{1,0:T(8,128)S(1)}, u32[]{:S(2)}, u32[]{:S(2)}) collective-permute-start(f32[8,64]{1,0:T(8,128)S(1)} %add.29), channel_id=1, source_target_pairs={{0,17},{1,16},{2,19},{3,18},{4,21},{5,20},{6,23},{7,22},{8,25},{9,... | collective-permute-start | bytes 6152 | tf_op jit(solution)/shard_map/ppermute | solution.py:295
  30.5 2.4 %collective-permute-done.13 = f32[8,64]{1,0:T(8,128)S(1)} collective-permute-done((f32[8,64]{1,0:T(8,128)S(1)}, f32[8,64]{1,0:T(8,128)S(1)}, u32[]{:S(2)}, u32[]{:S(2)}) %collective-permute-start.13) | collective-permute-done | bytes 2080 | tf_op jit(solution)/shard_map/ppermute | solution.py:295
  32.9 0.5 %constant_dynamic-slice_fusion = f32[1,64]{1,0:T(1,128)} fusion(f32[8,64]{1,0:T(8,128)S(1)} %add.30, s32[]{:T(128)S(6)} %select_n.16), kind=kLoop, calls=%fused_computation.3 | loop fusion | bytes 516 | tf_op jit(solution)/shard_map/dynamic_slice | solution.py:345
  (8 shorter events, 0.0 us)
Async XLA Ops:
  0.0 1.9 %copy-start = (f32[1,32,128]{2,1,0:T(8,128)S(1)}, f32[1,32,128]{2,1,0:T(8,128)}, u32[]{:S(2)}) copy-start(f32[1,32,128]{2,1,0:T(8,128)} %param.8) | copy-start | bytes 49156
  1.4 3.2 %collective-permute-start.2 = (f32[40,128]{1,0:T(8,128)S(1)}, f32[40,128]{1,0:T(8,128)S(1)}, u32[]{:S(2)}, u32[]{:S(2)}) collective-permute-start(f32[40,128]{1,0:T(8,128)S(1)} %get-tuple-element.24.refs_0_), channel_id=1, source_target_pairs={{0,1},{1,0},{2,3},{3,2},{4,5},{5,4},{6,7},{7,6},{8,9},{9,8},{10,11... | collective-permute-start | bytes 61448 | tf_op jit(solution)/shard_map/ppermute | solution.py:295
  1.9 4.3 %collective-permute-start = (f32[32,128]{1,0:T(8,128)S(1)}, f32[32,128]{1,0:T(8,128)S(1)}, u32[]{:S(2)}, u32[]{:S(2)}) collective-permute-start(f32[32,128]{1,0:T(8,128)S(1)} %bitcast.9), channel_id=1, source_target_pairs={{0,3},{1,2},{2,1},{3,0},{4,7},{5,6},{6,5},{7,4},{8,11},{9,10},{10,... | collective-permute-start | bytes 49160 | tf_op jit(solution)/shard_map/ppermute | solution.py:295
  5.0 4.0 %collective-permute-start.3 = (f32[96,128]{1,0:T(8,128)S(1)}, f32[96,128]{1,0:T(8,128)S(1)}, u32[]{:S(2)}, u32[]{:S(2)}) collective-permute-start(f32[96,128]{1,0:T(8,128)S(1)} %get-tuple-element.26), channel_id=1, source_target_pairs={{0,9},{1,8},{2,11},{3,10},{4,13},{5,12},{6,15},{7,14},{8,1},{9,0},... | collective-permute-start | bytes 147464 | tf_op jit(solution)/shard_map/ppermute | solution.py:295
  6.2 3.9 %collective-permute-start.6 = (f32[64,128]{1,0:T(8,128)S(1)}, f32[64,128]{1,0:T(8,128)S(1)}, u32[]{:S(2)}, u32[]{:S(2)}) collective-permute-start(f32[64,128]{1,0:T(8,128)S(1)} %pad_maximum_fusion.1), channel_id=1, source_target_pairs={{0,17},{1,16},{2,19},{3,18},{4,21},{5,20},{6,23},{7,22},{8,25},{9,... | collective-permute-start | bytes 98312 | tf_op jit(solution)/shard_map/ppermute | solution.py:295
  7.8 10.6 %collective-permute-start.1 = (f32[720,128]{1,0:T(8,128)S(1)}, f32[720,128]{1,0:T(8,128)S(1)}, u32[]{:S(2)}, u32[]{:S(2)}) collective-permute-start(f32[720,128]{1,0:T(8,128)S(1)} %get-tuple-element.23.refs_0_), channel_id=1, source_target_pairs={{0,9},{1,8},{2,11},{3,10},{4,13},{5,12},{6,15},{7,14},{8,1},{9,0},... | collective-permute-start | bytes 1105928 | tf_op jit(solution)/shard_map/ppermute | solution.py:295
  8.9 3.8 %collective-permute-start.4 = (f32[80,128]{1,0:T(8,128)S(1)}, f32[80,128]{1,0:T(8,128)S(1)}, u32[]{:S(2)}, u32[]{:S(2)}) collective-permute-start(f32[80,128]{1,0:T(8,128)S(1)} %slice_add_fusion), channel_id=1, source_target_pairs={{0,17},{1,16},{2,19},{3,18},{4,21},{5,20},{6,23},{7,22},{8,25},{9,... | collective-permute-start | bytes 122888 | tf_op jit(solution)/shard_map/ppermute | solution.py:295
  10.1 7.3 %collective-permute-start.7 = (f32[128,128]{1,0:T(8,128)S(1)}, f32[128,128]{1,0:T(8,128)S(1)}, u32[]{:S(2)}, u32[]{:S(2)}) collective-permute-start(f32[128,128]{1,0:T(8,128)S(1)} %pad_maximum_fusion), channel_id=1, source_target_pairs={{0,5},{1,4},{2,7},{3,6},{4,1},{5,0},{6,3},{7,2},{8,13},{9,12},{10,... | collective-permute-start | bytes 196616 | tf_op jit(solution)/shard_map/ppermute | solution.py:295
  12.8 4.6 %collective-permute-start.5 = (f32[80,128]{1,0:T(8,128)S(1)}, f32[80,128]{1,0:T(8,128)S(1)}, u32[]{:S(2)}, u32[]{:S(2)}) collective-permute-start(f32[80,128]{1,0:T(8,128)S(1)} %add.26), channel_id=1, source_target_pairs={{0,5},{1,4},{2,7},{3,6},{4,1},{5,0},{6,3},{7,2},{8,13},{9,12},{10,... | collective-permute-start | bytes 122888 | tf_op jit(solution)/shard_map/ppermute | solution.py:295
  15.4 4.7 %collective-permute-start.8 = (f32[720,128]{1,0:T(8,128)S(1)}, f32[720,128]{1,0:T(8,128)S(1)}, u32[]{:S(2)}, u32[]{:S(2)}) collective-permute-start(f32[720,128]{1,0:T(8,128)S(1)} %get-tuple-element.23.refs_0_), channel_id=1, source_target_pairs={{0,1},{1,0},{2,3},{3,2},{4,5},{5,4},{6,7},{7,6},{8,9},{9,8},{10,11... | collective-permute-start | bytes 1105928 | tf_op jit(solution)/shard_map/ppermute | solution.py:295
  18.4 1.7 %collective-permute-start.9 = (f32[720,128]{1,0:T(8,128)S(1)}, f32[720,128]{1,0:T(8,128)S(1)}, u32[]{:S(2)}, u32[]{:S(2)}) collective-permute-start(f32[720,128]{1,0:T(8,128)S(1)} %collective-permute-done.1.refs_1_), channel_id=1, source_target_pairs={{0,1},{1,0},{2,3},{3,2},{4,5},{5,4},{6,7},{7,6},{8,9},{9,8},{10,11... | collective-permute-start | bytes 1105928 | tf_op jit(solution)/shard_map/ppermute | solution.py:295
  18.5 3.5 %collective-permute-start.10 = (f32[80,128]{1,0:T(8,128)S(1)}, f32[80,128]{1,0:T(8,128)S(1)}, u32[]{:S(2)}, u32[]{:S(2)}) collective-permute-start(f32[80,128]{1,0:T(8,128)S(1)} %add.27.refs_6_), channel_id=1, source_target_pairs={{0,3},{1,2},{2,1},{3,0},{4,7},{5,6},{6,5},{7,4},{8,11},{9,10},{10,... | collective-permute-start | bytes 122888 | tf_op jit(solution)/shard_map/ppermute | solution.py:295
  22.9 3.1 %collective-permute-start.11 = (f32[8,64]{1,0:T(8,128)S(1)}, f32[8,64]{1,0:T(8,128)S(1)}, u32[]{:S(2)}, u32[]{:S(2)}) collective-permute-start(f32[8,64]{1,0:T(8,128)S(1)} %shard_map.85), channel_id=1, source_target_pairs={{0,3},{1,2},{2,1},{3,0},{4,7},{5,6},{6,5},{7,4},{8,11},{9,10},{10,... | collective-permute-start | bytes 6152 | tf_op jit(solution)/shard_map/ppermute | solution.py:295
  26.0 3.9 %collective-permute-start.12 = (f32[8,64]{1,0:T(8,128)S(1)}, f32[8,64]{1,0:T(8,128)S(1)}, u32[]{:S(2)}, u32[]{:S(2)}) collective-permute-start(f32[8,64]{1,0:T(8,128)S(1)} %add.28), channel_id=1, source_target_pairs={{0,5},{1,4},{2,7},{3,6},{4,1},{5,0},{6,3},{7,2},{8,13},{9,12},{10,... | collective-permute-start | bytes 6152 | tf_op jit(solution)/shard_map/ppermute | solution.py:295
  29.9 3.0 %collective-permute-start.13 = (f32[8,64]{1,0:T(8,128)S(1)}, f32[8,64]{1,0:T(8,128)S(1)}, u32[]{:S(2)}, u32[]{:S(2)}) collective-permute-start(f32[8,64]{1,0:T(8,128)S(1)} %add.29), channel_id=1, source_target_pairs={{0,17},{1,16},{2,19},{3,18},{4,21},{5,20},{6,23},{7,22},{8,25},{9,... | collective-permute-start | bytes 6152 | tf_op jit(solution)/shard_map/ppermute | solution.py:295

commit v8 on v7

--- a/solution.py
+++ b/solution.py
@@ -216,13 +216,18 @@
         chosen_ref[p * n_out:(p + 1) * n_out, :] = jnp.where(live & (local == float(p)), 1.0, 0.0)
 
 
-def score_kernel(side, outer, held, n_tiles, pos_ref, *refs):
+def score_kernel(side, outer, held, n_tiles, own, pos_ref, *refs):
     wide_refs = refs[:n_tiles]
     values_ref, chosen_ref, mine_ref, theirs_ref, out_ref = refs[n_tiles:]
     pos = pos_ref[0]
-    n_out = 1 << len(outer)
+    n_out = 1 << (len(outer) - 1)
     half = n_out * EXP
-    sums = mine_ref[...] + theirs_ref[...]
+    upper = ((pos & outer[-1]) != 0) == own
+
+    def of_half(low, high):
+        return jnp.where(upper, high, low)
+
+    sums = of_half(mine_ref[:half, :], mine_ref[half:, :]) + of_half(theirs_ref[:half, :], theirs_ref[half:, :])
     scale = lax.rsqrt(jnp.mean(sums * sums, axis=1, keepdims=True) + 1e-05)
     order = (iota((half, 1), 0) % EXP).astype(jnp.float32)
     extra = sums * (scale * (BETA * jnp.log((NCENT + 1.0) / (order + 1.0))))
@@ -242,7 +247,7 @@
     total = largest.shape[1]
     col = iota((n_out, 3 * total), 1) % total
     member = jnp.where(col // EXP == iota((n_out, 3 * total), 0), 1.0 / QL, 0.0).astype(jnp.bfloat16)
-    values = values_ref[...] + nt_dot(member, jnp.concatenate(thirds(largest), axis=1))
+    values = of_half(values_ref[:n_out, :], values_ref[n_out:, :]) + nt_dot(member, jnp.concatenate(thirds(largest), axis=1))
     slots = out_ref.shape[1]
     padded = slots + (-slots % DIM)
     shape = (n_tiles * 8, held * padded)
@@ -250,12 +255,14 @@
     col = iota(shape, 1)
     same = at_steps(pos, [0, side, 1, side ^ 1], col % padded // CAP, entry) & (col % padded < slots)
     pick = jnp.where(same & (entry % 8 == col // padded), 1.0, 0.0).astype(jnp.bfloat16)
-    found = jnp.dot(jnp.concatenate(thirds(values), axis=0), pick, preferred_element_type=jnp.float32)
+    found = jnp.dot(jnp.concatenate([t.astype(jnp.float32) for t in thirds(values)], axis=0).astype(jnp.bfloat16), pick, preferred_element_type=jnp.float32)
     found = found[:n_out] + found[n_out:2 * n_out] + found[2 * n_out:]
     result = jnp.zeros((n_out, slots), jnp.float32)
     for p in range(held):
         value = found[:, p * padded:p * padded + slots]
-        result = jnp.where(chosen_ref[p * n_out:(p + 1) * n_out, :] > 0.5, value, result)
+        at = 2 * p * n_out
+        chosen = of_half(chosen_ref[at:at + n_out, :], chosen_ref[at + n_out:at + 2 * n_out, :])
+        result = jnp.where(chosen > 0.5, value, result)
     out_ref[...] = result
 
 
@@ -336,13 +343,16 @@
         [wide] * len(tiles) + [struct(n_out, 8 * len(tiles)), struct(held * n_out, slots)],
         pos, *tiles, *asks, keep, from_side,
     )
-    table = call(
-        functools.partial(score_kernel, side, outer, held, len(tiles)), [struct(n_out, slots)],
-        pos, *tiles, values, chosen, sums, came,
-    )
-    for step in reversed(steps):
+    theirs, mine = [
+        call(
+            functools.partial(score_kernel, side, outer, held, len(tiles), own), [struct(n_out // 2, slots)],
+            pos, *tiles, values, chosen, sums, came,
+        ) for own in (False, True)
+    ]
+    table = mine + swap(theirs, steps[-1])
+    for step in reversed(steps[:-1]):
         table = table + swap(table, step)
-    return lax.dynamic_slice(table, (gather_bits(pos[0], outer), 0), (1, slots))
+    return lax.dynamic_slice(table, (gather_bits(pos[0], outer[:-1]), 0), (1, slots))
 
 
 def solution(mesh):

time: 33.6 us -> 33.5 us (level)
  waiting for transfers between devices: 9.1 us -> 8.11 us
  Pallas kernels: 3.78 us -> 4.71 us
    ppermute x14, waiting for transfers between devices: 9.1 us -> 8.11 us  [swap(): return lax.ppermute(x, AXES, [(i, i ^ mask) for i in range(devices)])]
    pallas_call x4 -> x5, Pallas kernels: 3.78 us -> 4.71 us  [call(): pl.pallas_call(kernel, out_shape=[pltpu.VMEM(o.shape, o.dtype) for o in o...]
  transfers between devices with their start and end apart: 14 -> 14, of which waited for: 6 -> 6; matrix products, arithmetic and copies ran while one was open for 0% -> 0% of each run, Pallas kernels for 4% -> 7%
where the time goes in v8:
time: 33.5 us; the launch traced here: 33.4 us
  starting transfers between devices  20 us (60%)
  waiting for transfers between devices  8.11 us (24%)
  Pallas kernels  4.71 us (14%)
  local copies, waits for them, and re-layouts  0.52 us (2%)
    ppermute x14, starting transfers between devices, swap(): return lax.ppermute(x, AXES, [(i, i ^ mask) for i in range(devices)])  20 us
    ppermute x14, waiting for transfers between devices, swap(): return lax.ppermute(x, AXES, [(i, i ^ mask) for i in range(devices)])  8.11 us
    pallas_call x5, Pallas kernels, call(): pl.pallas_call(kernel, out_shape=[pltpu.VMEM(o.shape, o.dtype) for o in o...  4.71 us
  transfers between devices with their start and end apart: 14, of which 6 were waited for; matrix products, arithmetic and copies ran while one was open for 0% of the time, Pallas kernels for 7%

profile of v8, /device:TPU:0, one launch (start us, length us, event | category | flops | bytes accessed | tf_op | source)
XLA Modules:
  0.0 33.4 jit_solution(17243127681288333600)
XLA Ops:
  0.0 0.0 copy-start
  0.0 1.4 %shard_map.82 = (f32[720,128]{1,0:T(8,128)S(1)}, f32[40,128]{1,0:T(8,128)S(1)}) custom-call(s32[1]{0:T(128)} %bitcast.pos_ref, s32[4]{0:T(128)} %refs_0_.1, f32[720,128]{1,0:T(8,128)} %bitcast.13, s32[4,180]{1,0:T(4,128)} %refs_2_.1, s32[3,32]{1,0:T(4,128)} %bitcast.15, s32[24,32]{1,0:T(8,128)} %bitcast.14, s32[2,32]{1,0:T(2,128)} %bitcast.16, s32[1,32]{1,0:T(1,128)} %bitcast.17), custom_call_target="tpu_custom_call" | custom-call | tf_op jit(solution)/shard_map/pallas_call | solution.py:279
  1.4 0.5 %collective-permute-start.2 = (f32[40,128]{1,0:T(8,128)S(1)}, f32[40,128]{1,0:T(8,128)S(1)}, u32[]{:S(2)}, u32[]{:S(2)}) collective-permute-start(f32[40,128]{1,0:T(8,128)S(1)} %get-tuple-element.24.refs_0_), channel_id=1, source_target_pairs={{0,1},{1,0},{2,3},{3,2},{4,5},{5,4},{6,7},{7,6},{8,9},{9,8},{10,11... | collective-permute-start | bytes 61448 | tf_op jit(solution)/shard_map/ppermute | solution.py:302
  1.9 0.0 copy-done
  1.9 2.7 %collective-permute-start = (f32[32,128]{1,0:T(8,128)S(1)}, f32[32,128]{1,0:T(8,128)S(1)}, u32[]{:S(2)}, u32[]{:S(2)}) collective-permute-start(f32[32,128]{1,0:T(8,128)S(1)} %bitcast.9), channel_id=1, source_target_pairs={{0,3},{1,2},{2,1},{3,0},{4,7},{5,6},{6,5},{7,4},{8,11},{9,10},{10,... | collective-permute-start | bytes 49160 | tf_op jit(solution)/shard_map/ppermute | solution.py:302
  4.6 0.0 collective-permute-done.2.refs_1_
  4.6 0.3 shard_map.83
  5.0 1.2 %collective-permute-start.3 = (f32[96,128]{1,0:T(8,128)S(1)}, f32[96,128]{1,0:T(8,128)S(1)}, u32[]{:S(2)}, u32[]{:S(2)}) collective-permute-start(f32[96,128]{1,0:T(8,128)S(1)} %get-tuple-element.26), channel_id=1, source_target_pairs={{0,9},{1,8},{2,11},{3,10},{4,13},{5,12},{6,15},{7,14},{8,1},{9,0},... | collective-permute-start | bytes 147464 | tf_op jit(solution)/shard_map/ppermute | solution.py:302
  6.2 0.0 collective-permute-done.refs_5_
  6.2 1.6 %collective-permute-start.6 = (f32[64,128]{1,0:T(8,128)S(1)}, f32[64,128]{1,0:T(8,128)S(1)}, u32[]{:S(2)}, u32[]{:S(2)}) collective-permute-start(f32[64,128]{1,0:T(8,128)S(1)} %pad_maximum_fusion.1), channel_id=1, source_target_pairs={{0,17},{1,16},{2,19},{3,18},{4,21},{5,20},{6,23},{7,22},{8,25},{9,... | collective-permute-start | bytes 98312 | tf_op jit(solution)/shard_map/ppermute | solution.py:302
  7.8 1.2 %collective-permute-start.1 = (f32[720,128]{1,0:T(8,128)S(1)}, f32[720,128]{1,0:T(8,128)S(1)}, u32[]{:S(2)}, u32[]{:S(2)}) collective-permute-start(f32[720,128]{1,0:T(8,128)S(1)} %get-tuple-element.23.refs_0_), channel_id=1, source_target_pairs={{0,9},{1,8},{2,11},{3,10},{4,13},{5,12},{6,15},{7,14},{8,1},{9,0},... | collective-permute-start | bytes 1105928 | tf_op jit(solution)/shard_map/ppermute | solution.py:302
  8.9 0.0 collective-permute-done.3.refs_9_
  8.9 1.1 %collective-permute-start.4 = (f32[80,128]{1,0:T(8,128)S(1)}, f32[80,128]{1,0:T(8,128)S(1)}, u32[]{:S(2)}, u32[]{:S(2)}) collective-permute-start(f32[80,128]{1,0:T(8,128)S(1)} %slice_add_fusion), channel_id=1, source_target_pairs={{0,17},{1,16},{2,19},{3,18},{4,21},{5,20},{6,23},{7,22},{8,25},{9,... | collective-permute-start | bytes 122888 | tf_op jit(solution)/shard_map/ppermute | solution.py:302
  10.1 0.0 collective-permute-done.6.refs_6_
  10.1 2.7 %collective-permute-start.7 = (f32[128,128]{1,0:T(8,128)S(1)}, f32[128,128]{1,0:T(8,128)S(1)}, u32[]{:S(2)}, u32[]{:S(2)}) collective-permute-start(f32[128,128]{1,0:T(8,128)S(1)} %pad_maximum_fusion), channel_id=1, source_target_pairs={{0,5},{1,4},{2,7},{3,6},{4,1},{5,0},{6,3},{7,2},{8,13},{9,12},{10,... | collective-permute-start | bytes 196616 | tf_op jit(solution)/shard_map/ppermute | solution.py:302
  12.8 0.0 collective-permute-done.4
  12.8 2.6 %collective-permute-start.5 = (f32[80,128]{1,0:T(8,128)S(1)}, f32[80,128]{1,0:T(8,128)S(1)}, u32[]{:S(2)}, u32[]{:S(2)}) collective-permute-start(f32[80,128]{1,0:T(8,128)S(1)} %add.26), channel_id=1, source_target_pairs={{0,5},{1,4},{2,7},{3,6},{4,1},{5,0},{6,3},{7,2},{8,13},{9,12},{10,... | collective-permute-start | bytes 122888 | tf_op jit(solution)/shard_map/ppermute | solution.py:302
  15.4 0.0 collective-permute-start.8
  15.4 2.0 %collective-permute-done.5 = f32[80,128]{1,0:T(8,128)S(1)} collective-permute-done((f32[80,128]{1,0:T(8,128)S(1)}, f32[80,128]{1,0:T(8,128)S(1)}, u32[]{:S(2)}, u32[]{:S(2)}) %collective-permute-start.5) | collective-permute-done | bytes 40992 | tf_op jit(solution)/shard_map/ppermute | solution.py:302
  17.4 0.0 collective-permute-done.7.refs_7_
  17.4 1.0 %collective-permute-done.1.refs_1_ = f32[720,128]{1,0:T(8,128)S(1)} collective-permute-done((f32[720,128]{1,0:T(8,128)S(1)}, f32[720,128]{1,0:T(8,128)S(1)}, u32[]{:S(2)}, u32[]{:S(2)}) %collective-permute-start.1) | collective-permute-done | bytes 368672 | tf_op jit(solution)/shard_map/ppermute | solution.py:302
  18.4 0.1 collective-permute-start.9
  18.5 1.6 %collective-permute-start.10 = (f32[80,128]{1,0:T(8,128)S(1)}, f32[80,128]{1,0:T(8,128)S(1)}, u32[]{:S(2)}, u32[]{:S(2)}) collective-permute-start(f32[80,128]{1,0:T(8,128)S(1)} %add.27.refs_6_), channel_id=1, source_target_pairs={{0,3},{1,2},{2,1},{3,0},{4,7},{5,6},{6,5},{7,4},{8,11},{9,10},{10,... | collective-permute-start | bytes 122888 | tf_op jit(solution)/shard_map/ppermute | solution.py:302
  20.1 0.0 collective-permute-done.8.refs_2_
  20.1 0.0 collective-permute-done.9.refs_3_
  20.1 1.1 %shard_map.84 = (bf16[720,256]{1,0:T(8,128)(2,1)S(1)}, bf16[720,256]{1,0:T(8,128)(2,1)S(1)}, bf16[720,256]{1,0:T(8,128)(2,1)S(1)}, bf16[720,256]{1,0:T(8,128)(2,...) custom-call(s32[1]{0:T(128)} %bitcast.pos_ref, f32[720,128]{1,0:T(8,128)S(1)} %get-tuple-element.23.refs_0_, ...), custom_call_target="tpu_custom_call" | custom-call | tf_op jit(solution)/shard_map/pallas_call | solution.py:279
  21.2 0.7 %collective-permute-done.10.refs_7_ = f32[80,128]{1,0:T(8,128)S(1)} collective-permute-done((f32[80,128]{1,0:T(8,128)S(1)}, f32[80,128]{1,0:T(8,128)S(1)}, u32[]{:S(2)}, u32[]{:S(2)}) %collective-permute-start.10) | collective-permute-done | bytes 40992 | tf_op jit(solution)/shard_map/ppermute | solution.py:302
  22.0 0.9 %shard_map.86 = f32[4,64]{1,0:T(4,128)S(1)} custom-call(s32[1]{0:T(128)} %bitcast.pos_ref, bf16[720,256]{1,0:T(8,128)(2,1)S(1)} %get-tuple-element.32.refs_0_, bf16[720,256]{1,0:T(8,128)(2,1)S(1)} %get-tuple-element.33.refs_1_, bf16[720,256]{1,0:T(8,128)(2,1)S(1)} %get-tuple-element.34.refs_2_, bf16[720,256]{1,0:T(8,128)(2,1)S(1)} %get-tuple-element.35.refs_3_, ...), custom_call_target="tpu_custom_call" | custom-call | tf_op jit(solution)/shard_map/pallas_call | solution.py:279
  22.9 1.5 %collective-permute-start.11 = (f32[4,64]{1,0:T(4,128)S(1)}, f32[4,64]{1,0:T(4,128)S(1)}, u32[]{:S(2)}, u32[]{:S(2)}) collective-permute-start(f32[4,64]{1,0:T(4,128)S(1)} %shard_map.86), channel_id=1, source_target_pairs={{0,3},{1,2},{2,1},{3,0},{4,7},{5,6},{6,5},{7,4},{8,11},{9,10},{10,... | collective-permute-start | bytes 3080 | tf_op jit(solution)/shard_map/ppermute | solution.py:302
  24.4 0.9 %shard_map.85 = f32[4,64]{1,0:T(4,128)S(1)} custom-call(s32[1]{0:T(128)} %bitcast.pos_ref, bf16[720,256]{1,0:T(8,128)(2,1)S(1)} %get-tuple-element.32.refs_0_, bf16[720,256]{1,0:T(8,128)(2,1)S(1)} %get-tuple-element.33.refs_1_, bf16[720,256]{1,0:T(8,128)(2,1)S(1)} %get-tuple-element.34.refs_2_, bf16[720,256]{1,0:T(8,128)(2,1)S(1)} %get-tuple-element.35.refs_3_, ...), custom_call_target="tpu_custom_call" | custom-call | tf_op jit(solution)/shard_map/pallas_call | solution.py:279
  25.4 0.6 %collective-permute-done.11 = f32[4,64]{1,0:T(4,128)S(1)} collective-permute-done((f32[4,64]{1,0:T(4,128)S(1)}, f32[4,64]{1,0:T(4,128)S(1)}, u32[]{:S(2)}, u32[]{:S(2)}) %collective-permute-start.11) | collective-permute-done | bytes 1056 | tf_op jit(solution)/shard_map/ppermute | solution.py:302
  25.9 2.5 %collective-permute-start.12 = (f32[4,64]{1,0:T(4,128)S(1)}, f32[4,64]{1,0:T(4,128)S(1)}, u32[]{:S(2)}, u32[]{:S(2)}) collective-permute-start(f32[4,64]{1,0:T(4,128)S(1)} %add.28), channel_id=1, source_target_pairs={{0,5},{1,4},{2,7},{3,6},{4,1},{5,0},{6,3},{7,2},{8,13},{9,12},{10,... | collective-permute-start | bytes 3080 | tf_op jit(solution)/shard_map/ppermute | solution.py:302
  28.5 1.4 %collective-permute-done.12 = f32[4,64]{1,0:T(4,128)S(1)} collective-permute-done((f32[4,64]{1,0:T(4,128)S(1)}, f32[4,64]{1,0:T(4,128)S(1)}, u32[]{:S(2)}, u32[]{:S(2)}) %collective-permute-start.12) | collective-permute-done | bytes 1056 | tf_op jit(solution)/shard_map/ppermute | solution.py:302
  29.8 0.6 %collective-permute-start.13 = (f32[4,64]{1,0:T(4,128)S(1)}, f32[4,64]{1,0:T(4,128)S(1)}, u32[]{:S(2)}, u32[]{:S(2)}) collective-permute-start(f32[4,64]{1,0:T(4,128)S(1)} %add.29), channel_id=1, source_target_pairs={{0,17},{1,16},{2,19},{3,18},{4,21},{5,20},{6,23},{7,22},{8,25},{9,... | collective-permute-start | bytes 3080 | tf_op jit(solution)/shard_map/ppermute | solution.py:302
  30.5 2.4 %collective-permute-done.13 = f32[4,64]{1,0:T(4,128)S(1)} collective-permute-done((f32[4,64]{1,0:T(4,128)S(1)}, f32[4,64]{1,0:T(4,128)S(1)}, u32[]{:S(2)}, u32[]{:S(2)}) %collective-permute-start.13) | collective-permute-done | bytes 1056 | tf_op jit(solution)/shard_map/ppermute | solution.py:302
  32.9 0.5 %constant_dynamic-slice_fusion = f32[1,64]{1,0:T(1,128)} fusion(f32[4,64]{1,0:T(4,128)S(1)} %add.30, s32[]{:T(128)S(6)} %select_n.12), kind=kLoop, calls=%fused_computation.3 | loop fusion | bytes 516 | tf_op jit(solution)/shard_map/dynamic_slice | solution.py:355
  (8 shorter events, 0.0 us)
Async XLA Ops:
  0.0 1.9 %copy-start = (f32[1,32,128]{2,1,0:T(8,128)S(1)}, f32[1,32,128]{2,1,0:T(8,128)}, u32[]{:S(2)}) copy-start(f32[1,32,128]{2,1,0:T(8,128)} %param.8) | copy-start | bytes 49156
  1.4 3.2 %collective-permute-start.2 = (f32[40,128]{1,0:T(8,128)S(1)}, f32[40,128]{1,0:T(8,128)S(1)}, u32[]{:S(2)}, u32[]{:S(2)}) collective-permute-start(f32[40,128]{1,0:T(8,128)S(1)} %get-tuple-element.24.refs_0_), channel_id=1, source_target_pairs={{0,1},{1,0},{2,3},{3,2},{4,5},{5,4},{6,7},{7,6},{8,9},{9,8},{10,11... | collective-permute-start | bytes 61448 | tf_op jit(solution)/shard_map/ppermute | solution.py:302
  1.9 4.3 %collective-permute-start = (f32[32,128]{1,0:T(8,128)S(1)}, f32[32,128]{1,0:T(8,128)S(1)}, u32[]{:S(2)}, u32[]{:S(2)}) collective-permute-start(f32[32,128]{1,0:T(8,128)S(1)} %bitcast.9), channel_id=1, source_target_pairs={{0,3},{1,2},{2,1},{3,0},{4,7},{5,6},{6,5},{7,4},{8,11},{9,10},{10,... | collective-permute-start | bytes 49160 | tf_op jit(solution)/shard_map/ppermute | solution.py:302
  5.0 4.0 %collective-permute-start.3 = (f32[96,128]{1,0:T(8,128)S(1)}, f32[96,128]{1,0:T(8,128)S(1)}, u32[]{:S(2)}, u32[]{:S(2)}) collective-permute-start(f32[96,128]{1,0:T(8,128)S(1)} %get-tuple-element.26), channel_id=1, source_target_pairs={{0,9},{1,8},{2,11},{3,10},{4,13},{5,12},{6,15},{7,14},{8,1},{9,0},... | collective-permute-start | bytes 147464 | tf_op jit(solution)/shard_map/ppermute | solution.py:302
  6.2 3.9 %collective-permute-start.6 = (f32[64,128]{1,0:T(8,128)S(1)}, f32[64,128]{1,0:T(8,128)S(1)}, u32[]{:S(2)}, u32[]{:S(2)}) collective-permute-start(f32[64,128]{1,0:T(8,128)S(1)} %pad_maximum_fusion.1), channel_id=1, source_target_pairs={{0,17},{1,16},{2,19},{3,18},{4,21},{5,20},{6,23},{7,22},{8,25},{9,... | collective-permute-start | bytes 98312 | tf_op jit(solution)/shard_map/ppermute | solution.py:302
  7.8 10.6 %collective-permute-start.1 = (f32[720,128]{1,0:T(8,128)S(1)}, f32[720,128]{1,0:T(8,128)S(1)}, u32[]{:S(2)}, u32[]{:S(2)}) collective-permute-start(f32[720,128]{1,0:T(8,128)S(1)} %get-tuple-element.23.refs_0_), channel_id=1, source_target_pairs={{0,9},{1,8},{2,11},{3,10},{4,13},{5,12},{6,15},{7,14},{8,1},{9,0},... | collective-permute-start | bytes 1105928 | tf_op jit(solution)/shard_map/ppermute | solution.py:302
  8.9 3.8 %collective-permute-start.4 = (f32[80,128]{1,0:T(8,128)S(1)}, f32[80,128]{1,0:T(8,128)S(1)}, u32[]{:S(2)}, u32[]{:S(2)}) collective-permute-start(f32[80,128]{1,0:T(8,128)S(1)} %slice_add_fusion), channel_id=1, source_target_pairs={{0,17},{1,16},{2,19},{3,18},{4,21},{5,20},{6,23},{7,22},{8,25},{9,... | collective-permute-start | bytes 122888 | tf_op jit(solution)/shard_map/ppermute | solution.py:302
  10.1 7.3 %collective-permute-start.7 = (f32[128,128]{1,0:T(8,128)S(1)}, f32[128,128]{1,0:T(8,128)S(1)}, u32[]{:S(2)}, u32[]{:S(2)}) collective-permute-start(f32[128,128]{1,0:T(8,128)S(1)} %pad_maximum_fusion), channel_id=1, source_target_pairs={{0,5},{1,4},{2,7},{3,6},{4,1},{5,0},{6,3},{7,2},{8,13},{9,12},{10,... | collective-permute-start | bytes 196616 | tf_op jit(solution)/shard_map/ppermute | solution.py:302
  12.8 4.6 %collective-permute-start.5 = (f32[80,128]{1,0:T(8,128)S(1)}, f32[80,128]{1,0:T(8,128)S(1)}, u32[]{:S(2)}, u32[]{:S(2)}) collective-permute-start(f32[80,128]{1,0:T(8,128)S(1)} %add.26), channel_id=1, source_target_pairs={{0,5},{1,4},{2,7},{3,6},{4,1},{5,0},{6,3},{7,2},{8,13},{9,12},{10,... | collective-permute-start | bytes 122888 | tf_op jit(solution)/shard_map/ppermute | solution.py:302
  15.4 4.7 %collective-permute-start.8 = (f32[720,128]{1,0:T(8,128)S(1)}, f32[720,128]{1,0:T(8,128)S(1)}, u32[]{:S(2)}, u32[]{:S(2)}) collective-permute-start(f32[720,128]{1,0:T(8,128)S(1)} %get-tuple-element.23.refs_0_), channel_id=1, source_target_pairs={{0,1},{1,0},{2,3},{3,2},{4,5},{5,4},{6,7},{7,6},{8,9},{9,8},{10,11... | collective-permute-start | bytes 1105928 | tf_op jit(solution)/shard_map/ppermute | solution.py:302
  18.4 1.7 %collective-permute-start.9 = (f32[720,128]{1,0:T(8,128)S(1)}, f32[720,128]{1,0:T(8,128)S(1)}, u32[]{:S(2)}, u32[]{:S(2)}) collective-permute-start(f32[720,128]{1,0:T(8,128)S(1)} %collective-permute-done.1.refs_1_), channel_id=1, source_target_pairs={{0,1},{1,0},{2,3},{3,2},{4,5},{5,4},{6,7},{7,6},{8,9},{9,8},{10,11... | collective-permute-start | bytes 1105928 | tf_op jit(solution)/shard_map/ppermute | solution.py:302
  18.5 3.5 %collective-permute-start.10 = (f32[80,128]{1,0:T(8,128)S(1)}, f32[80,128]{1,0:T(8,128)S(1)}, u32[]{:S(2)}, u32[]{:S(2)}) collective-permute-start(f32[80,128]{1,0:T(8,128)S(1)} %add.27.refs_6_), channel_id=1, source_target_pairs={{0,3},{1,2},{2,1},{3,0},{4,7},{5,6},{6,5},{7,4},{8,11},{9,10},{10,... | collective-permute-start | bytes 122888 | tf_op jit(solution)/shard_map/ppermute | solution.py:302
  22.9 3.0 %collective-permute-start.11 = (f32[4,64]{1,0:T(4,128)S(1)}, f32[4,64]{1,0:T(4,128)S(1)}, u32[]{:S(2)}, u32[]{:S(2)}) collective-permute-start(f32[4,64]{1,0:T(4,128)S(1)} %shard_map.86), channel_id=1, source_target_pairs={{0,3},{1,2},{2,1},{3,0},{4,7},{5,6},{6,5},{7,4},{8,11},{9,10},{10,... | collective-permute-start | bytes 3080 | tf_op jit(solution)/shard_map/ppermute | solution.py:302
  25.9 3.9 %collective-permute-start.12 = (f32[4,64]{1,0:T(4,128)S(1)}, f32[4,64]{1,0:T(4,128)S(1)}, u32[]{:S(2)}, u32[]{:S(2)}) collective-permute-start(f32[4,64]{1,0:T(4,128)S(1)} %add.28), channel_id=1, source_target_pairs={{0,5},{1,4},{2,7},{3,6},{4,1},{5,0},{6,3},{7,2},{8,13},{9,12},{10,... | collective-permute-start | bytes 3080 | tf_op jit(solution)/shard_map/ppermute | solution.py:302
  29.8 3.0 %collective-permute-start.13 = (f32[4,64]{1,0:T(4,128)S(1)}, f32[4,64]{1,0:T(4,128)S(1)}, u32[]{:S(2)}, u32[]{:S(2)}) collective-permute-start(f32[4,64]{1,0:T(4,128)S(1)} %add.29), channel_id=1, source_target_pairs={{0,17},{1,16},{2,19},{3,18},{4,21},{5,20},{6,23},{7,22},{8,25},{9,... | collective-permute-start | bytes 3080 | tf_op jit(solution)/shard_map/ppermute | solution.py:302
